TPU v7x, 128 devices: a whole 4x4x4 slice. The times are simulated.
128 devices in a mesh: seq: 32 (over z, x, core), head: 4 (over y).
Axes of the slice: x: 4, y: 4, z: 4, core: 2. Of those that a mesh axis runs over, the one named last changes fastest.
Arguments:
- projections: bfloat16 [16384, 3, 4096], P('seq', None, 'head'), may hold values from -53 to 53
- output_gradient: bfloat16 [16384, 5120], P('seq', 'head'), may hold values from -0.75 to 0.75
- output_projection_weight: bfloat16 [5120, 4096], P(None, 'head'), may hold values from -0.625 to 0.625
- kept_token_indices: int32 [32, 192], P('seq'), may hold values from -1 to 511, as said below
- surviving_token_count: int32 [32], replicated, may hold values from 64 to 192, as said below
Outputs:
- projection_grad: bfloat16 [16384, 3, 4096], P('seq', None, 'head')
- weight_grad: float32 [5120, 4096], P('seq', 'head')
Inputs may be any that keep to these rules, and one draw needn't show every extreme that they name: `kept_token_indices`: row s holds, in its first surviving_token_count[s] entries, distinct indices 0 to 511 in ascending order; its other entries are -1. Every shard that keeps 192 tokens keeps its last token. `surviving_token_count`: some shard keeps exactly 192 tokens and some other keeps exactly 64.
All inputs are finite; a program needn't handle non-finite values.
Results may differ from a plain program's by a relative error of at most 0.0099.
Values may be sent and summed in bfloat16 or wider, within the bound.
A program may use at most 128 MiB of HBM per device.

v0:
```python
import math

import jax
import jax.numpy as jnp
from jax import lax
from jax.sharding import PartitionSpec as P

DH = 128


def contract_rows(left, right):
    return lax.dot_general(
        left, right, (((0,), (0,)), ((), ())), preferred_element_type=jnp.float32
    )


def contract_cols(left, right):
    return lax.dot_general(
        left, right, (((1,), (1,)), ((), ())), preferred_element_type=jnp.float32
    )


def on_device(
    projections,
    output_gradient,
    output_projection_weight,
    kept_token_indices,
    surviving_token_count,
):
    tok_dev = projections.shape[0]
    group_width = projections.shape[2]
    slots_per_shard = kept_token_indices.shape[1]
    head_size = DH
    heads_local = group_width // head_size
    seq_count = lax.axis_size("seq")
    quarters = seq_count // heads_local
    part_rows = slots_per_shard // quarters
    my_quarter = lax.axis_index("seq") % quarters
    selector = (
        kept_token_indices[0][:, None] == jnp.arange(tok_dev, dtype=jnp.int32)[None, :]
    ).astype(jnp.bfloat16)
    packed = jnp.dot(
        selector, projections.reshape(tok_dev, 3 * group_width), preferred_element_type=jnp.float32
    )
    packed = packed.astype(jnp.bfloat16).reshape(slots_per_shard, 3, group_width)
    grad_local = jnp.dot(selector, output_gradient, preferred_element_type=jnp.float32).astype(
        jnp.bfloat16
    )
    grad_rows = lax.all_gather(grad_local, "head", axis=1, tiled=True)
    grad_attn = jnp.dot(
        grad_rows, output_projection_weight, preferred_element_type=jnp.float32
    ).astype(jnp.bfloat16)

    def head_major(matrix):
        return matrix.reshape(slots_per_shard, heads_local, head_size).transpose(1, 0, 2)

    query_side = jnp.concatenate([head_major(packed[:, 0]), head_major(grad_attn)], axis=2)
    query_side = query_side.reshape(seq_count, part_rows, 2 * head_size)
    key_side = jnp.concatenate([head_major(packed[:, 1]), head_major(packed[:, 2])], axis=2)
    key_side = jnp.broadcast_to(
        key_side[:, None], (heads_local, quarters, slots_per_shard, 2 * head_size)
    )
    key_side = key_side.reshape(seq_count, slots_per_shard, 2 * head_size)
    query_in, key_in = (
        lax.all_to_all(query_side, "seq", split_axis=0, concat_axis=0, tiled=True),
        lax.all_to_all(key_side, "seq", split_axis=0, concat_axis=0, tiled=True),
    )
    query_rows = query_in.reshape(seq_count * part_rows, 2 * head_size)
    key_rows = key_in.reshape(seq_count * slots_per_shard, 2 * head_size)
    key_mat = key_rows[:, :head_size]
    value_mat = key_rows[:, head_size:]
    key_position = jnp.arange(seq_count * slots_per_shard, dtype=jnp.int32)
    key_is_alive = (
        key_position % slots_per_shard < surviving_token_count[key_position // slots_per_shard]
    )
    query_pos = (
        jnp.arange(seq_count, dtype=jnp.int32)[:, None] * slots_per_shard + my_quarter * part_rows
    )
    query_pos = (query_pos + jnp.arange(part_rows, dtype=jnp.int32)[None, :]).reshape(-1)
    block_rows = 512
    score_scale = 1.0 / math.sqrt(head_size)

    def attend(running, block_in):
        key_grad, value_grad = running
        block_data, block_pos = block_in
        query_block = block_data[:, :head_size]
        grad_block = block_data[:, head_size:]
        scores = contract_cols(query_block, key_mat) * score_scale
        allowed = key_is_alive[None, :] & (key_position[None, :] <= block_pos[:, None])
        scores = jnp.where(allowed, scores, -1e30)
        row_peak = jnp.max(scores, axis=1, keepdims=True)
        weights = jnp.where(allowed, jnp.exp(scores - row_peak), 0.0)
        probabilities = weights / jnp.sum(weights, axis=1, keepdims=True)
        probs_low = probabilities.astype(jnp.bfloat16)
        attended = jnp.dot(probs_low, value_mat, preferred_element_type=jnp.float32)
        grad_probs = contract_cols(grad_block, value_mat)
        row_dot = jnp.sum(grad_block.astype(jnp.float32) * attended, axis=1, keepdims=True)
        grad_scores = (probabilities * (grad_probs - row_dot)).astype(jnp.bfloat16)
        grad_query = (
            jnp.dot(grad_scores, key_mat, preferred_element_type=jnp.float32) * score_scale
        ).astype(jnp.bfloat16)
        key_grad = key_grad + contract_rows(grad_scores, query_block) * score_scale
        value_grad = value_grad + contract_rows(probs_low, grad_block)
        return (
            (key_grad, value_grad),
            jnp.concatenate([grad_query, attended.astype(jnp.bfloat16)], axis=1),
        )

    empty_grad = jnp.zeros((seq_count * slots_per_shard, head_size), jnp.float32)
    blocks_in = (
        query_rows.reshape(-1, block_rows, 2 * head_size),
        query_pos.reshape(-1, block_rows),
    )
    (key_grad, value_grad), query_out = lax.scan(attend, (empty_grad, empty_grad), blocks_in)
    query_back = query_out.reshape(seq_count, part_rows, 2 * head_size)
    key_back = jnp.concatenate([key_grad, value_grad], axis=1).reshape(
        seq_count, slots_per_shard, 2 * head_size
    )
    query_home = lax.all_to_all(query_back, "seq", split_axis=0, concat_axis=0, tiled=True)
    key_home = lax.all_to_all(key_back, "seq", split_axis=0, concat_axis=0, tiled=True)
    query_home = query_home.reshape(heads_local, slots_per_shard, 2 * head_size).transpose(1, 0, 2)
    key_home = jnp.sum(
        key_home.reshape(heads_local, quarters, slots_per_shard, 2 * head_size), axis=1
    )
    key_home = key_home.astype(jnp.bfloat16).transpose(1, 0, 2)
    grad_query = query_home[:, :, :head_size].reshape(slots_per_shard, group_width)
    attended_low = query_home[:, :, head_size:].reshape(slots_per_shard, group_width)
    grad_key = key_home[:, :, :head_size].reshape(slots_per_shard, group_width)
    grad_value = key_home[:, :, head_size:].reshape(slots_per_shard, group_width)
    grad_packed = jnp.stack([grad_query, grad_key, grad_value], axis=1).reshape(
        slots_per_shard, 3 * group_width
    )
    projection_grad = (
        contract_rows(selector, grad_packed).astype(jnp.bfloat16).reshape(tok_dev, 3, group_width)
    )
    weight_grad = lax.psum_scatter(
        contract_rows(grad_rows, attended_low), "seq", scatter_dimension=0, tiled=True
    )
    return (projection_grad, weight_grad)


def solution(mesh):
    return jax.shard_map(
        on_device,
        mesh=mesh,
        in_specs=(P("seq", None, "head"), P("seq", "head"), P(None, "head"), P("seq", None), P()),
        out_specs=(P("seq", None, "head"), P("seq", "head")),
        check_vma=False,
    )
```

profile of v0, /device:TPU:1, one launch (start us, length us, event | category | flops | bytes accessed | tf_op | source)
XLA Modules:
  0.0 427.5 jit_solution(17707011648399638921)
XLA Ops:
  10.4 4.6 %copy.18 = bf16[512,3,1024]{0,2,1:T(8,128)(2,1)} copy(bf16[512,3,1024]{2,0,1:T(8,128)(2,1)} %param.7) | data formatting | bytes 6291456 | tf_op args[0]
  19.9 5.8 %slice_reduce_fusion.1 = (bf16[192,1024]{1,0:T(8,128)(2,1)S(1)}, bf16[192,1024]{1,0:T(8,128)(2,1)S(1)}, bf16[192,1024]{1,0:T(8,128)(2,1)S(1)}) fusion(bf16[192,3,1024]{2,1,0:T(4,128)(2,1)S(1)} %reshape.106), kind=kLoop, calls=%fused_computation.34 | loop fusion | bytes 2359296 | tf_op jit(solution)/shard_map/slice | solution.py:59
  28.2 9.6 %all-to-all-start.1 = ((bf16[32,192,256]{2,1,0:T(8,128)(2,1)}), bf16[32,192,256]{2,1,0:T(8,128)(2,1)}, u32[]{:S(2)}, u32[]{:S(2)}) async-start(bf16[32,192,256]{2,1,0:T(8,128)(2,1)} %bitcast.117), calls=%async_computation.1 | async-start | bytes 6291456 | tf_op jit(solution)/shard_map/all_to_all | solution.py:66
  42.1 14.0 %compare_reduce_fusion.9 = pred[6144]{0:T(1024)(128)(4,1)S(1)} fusion(), kind=kLoop, calls=%fused_computation.57 | loop fusion | flops 73728 | bytes 6144 | tf_op jit(solution)/shard_map/gather | solution.py:74
  57.5 4.5 %compare_select_fusion.1 = s32[6144,1]{0,1:T(1,128)S(1)} fusion(s32[]{:T(128)} %bitcast.26, s32[]{:T(128)} %bitcast.27, s32[]{:T(128)} %bitcast.28, s32[]{:T(128)} %bitcast.29, s32[]{:T(128)} %bitcast.30, s32[]{:T(128)} %bitcast.32, s32[]{:T(128)} %bitcast.31), kind=kLoop, calls=%fused_computation.73 | loop fusion | flops 141312 | bytes 24604 | tf_op jit(solution)/shard_map/gather | solution.py:74
  62.1 15.6 %fusion.21 = pred[6144]{0:T(1024)(128)(4,1)S(1)} fusion(pred[6144]{0:T(1024)(128)(4,1)S(1)} %compare_reduce_fusion, pred[6144]{0:T(1024)(128)(4,1)S(1)} %compare_reduce_fusion.1, pred[6144]{0:T(1024)(128)(4,1)S(1)} %compare_reduce_fusion.2, pred[6144]{0:T(1024)(128)(4,1)S(1)} %compare_reduce_fusion.3, pred[6144]{0:T(1024)(128)(4,1)S(1)} %compare_reduce_fusion.4, ...), kind=kLoop, calls=%fused_computation.84 | loop fusion | flops 196608 | bytes 184420 | tf_op jit(solution)/shard_map/lt | solution.py:74
  77.7 6.8 %fusion.14 = bf16[24,8,8,128]{3,1,2,0:T(8,128)(2,1)S(1)} fusion(bf16[192,5120]{1,0:T(8,128)(2,1)} %all-gather.2.cloned.1.call-done, bf16[5120,1024]{1,0:T(8,128)(2,1)} %param.9), kind=kOutput, calls=%fused_computation.31 | convolution fusion | flops 2013462528 | bytes 12845056 | tf_op jit(solution)/shard_map/dot_general | solution.py:50
  85.7 7.4 %all-to-all-start = ((bf16[32,48,256]{2,1,0:T(8,128)(2,1)}), bf16[32,48,256]{2,1,0:T(8,128)(2,1)S(1)}, u32[]{:S(2)}, u32[]{:S(2)}) async-start(bf16[32,48,256]{2,1,0:T(8,128)(2,1)} %bitcast.37), calls=%async_computation | async-start | bytes 1572864 | tf_op jit(solution)/shard_map/all_to_all | solution.py:65
  96.4 10.9 %all-to-all-done = bf16[32,48,256]{2,1,0:T(8,128)(2,1)S(1)} async-done(((bf16[32,48,256]{2,1,0:T(8,128)(2,1)}), bf16[32,48,256]{2,1,0:T(8,128)(2,1)S(1)}, u32[]{:S(2)}, u32[]{:S(2)}) %all-to-all-start) | async-done | bytes 786464 | tf_op jit(solution)/shard_map/all_to_all | solution.py:65
  107.3 131.5 %while.15 = (s32[]{:T(128)}, f32[6144,128]{1,0:T(8,128)}, f32[6144,128]{1,0:T(8,128)}, bf16[3,512,256]{2,1,0:T(8,128)(2,1)}, pred[6144]{0:T(1024)(128)(4,1)S(1)}...) while((s32[]{:T(128)}, f32[6144,128]{1,0:T(8,128)}, ...), condition=%wide.region_4.5_spmd.clone, body=%wide.region_0.4_spmd.clone.sunk | while | flops 4899600896 | bytes 242658096 | solution.py:114
  107.5 5.9 %fusion.70 = (f32[512]{0:T(512)S(1)}, f32[512,6144]{1,0:T(8,128)S(1)}) fusion(bf16[6144,128]{1,0:T(8,128)(2,1)} %get-tuple-element.270, bf16[512,256]{0,1:T(8,128)(2,1)S(1)} %bitcast.109, s32[512]{0:T(512)S(1)} %bitcast.132, pred[6144]{0:T(1024)(128)(4,1)S(1)} %get-tuple-element.267), kind=kOutput, calls=%fused_computation.92.clone.1 | convolution fusion | flops 821034496 | bytes 14297088 | tf_op jit(solution)/shard_map/while/body/eval_jaxpr/dot_general | solution.py:18
  126.9 5.2 %multiply_convert_fusion.2 = bf16[512,6144]{1,0:T(8,128)(2,1)} fusion(f32[512,6144]{1,0:T(8,128)S(1)} %fusion.72, bf16[6144,128]{1,0:T(8,128)(2,1)S(1)} %get-tuple-element.271, f32[512]{0:T(512)S(1)} %get-tuple-element.239, bf16[512,256]{0,1:T(8,128)(2,1)S(1)} %bitcast.111), kind=kOutput, calls=%fused_computation.2.clone.1 | convolution fusion | flops 814743552 | bytes 20580352 | tf_op jit(solution)/shard_map/while/body/eval_jaxpr/dot_general | solution.py:18
  132.1 5.0 %fusion.75 = bf16[512,128]{0,1:T(8,128)(2,1)S(1)} fusion(bf16[512,6144]{1,0:T(8,128)(2,1)} %multiply_convert_fusion.2, bf16[6144,128]{1,0:T(8,128)(2,1)S(1)} %copy-done.4), kind=kOutput, calls=%fused_computation.15.clone.1 | convolution fusion | flops 805437440 | bytes 7995392 | tf_op jit(solution)/shard_map/while/body/eval_jaxpr/dot_general | solution.py:100
  138.0 6.4 %fusion.74 = f32[6144,128]{1,0:T(8,128)} fusion(bf16[512,6144]{1,0:T(8,128)(2,1)} %multiply_convert_fusion.2, f32[6144,128]{1,0:T(8,128)} %get-tuple-element.253, pred[]{:T(512)S(6)} %compare.129, bf16[512,256]{0,1:T(8,128)(2,1)S(1)} %bitcast.112), kind=kOutput, calls=%fused_computation.10.clone.1 | convolution fusion | flops 807665664 | bytes 12713985 | tf_op jit(solution)/shard_map/while/body/eval_jaxpr/dot_general | solution.py:12
  149.4 5.9 %fusion.70 = (f32[512]{0:T(512)S(1)}, f32[512,6144]{1,0:T(8,128)S(1)}) fusion(bf16[6144,128]{1,0:T(8,128)(2,1)} %get-tuple-element.270, bf16[512,256]{0,1:T(8,128)(2,1)S(1)} %bitcast.109, s32[512]{0:T(512)S(1)} %bitcast.132, pred[6144]{0:T(1024)(128)(4,1)S(1)} %get-tuple-element.267), kind=kOutput, calls=%fused_computation.92.clone.1 | convolution fusion | flops 821034496 | bytes 14297088 | tf_op jit(solution)/shard_map/while/body/eval_jaxpr/dot_general | solution.py:18
  168.8 5.2 %multiply_convert_fusion.2 = bf16[512,6144]{1,0:T(8,128)(2,1)} fusion(f32[512,6144]{1,0:T(8,128)S(1)} %fusion.72, bf16[6144,128]{1,0:T(8,128)(2,1)S(1)} %get-tuple-element.271, f32[512]{0:T(512)S(1)} %get-tuple-element.239, bf16[512,256]{0,1:T(8,128)(2,1)S(1)} %bitcast.111), kind=kOutput, calls=%fused_computation.2.clone.1 | convolution fusion | flops 814743552 | bytes 20580352 | tf_op jit(solution)/shard_map/while/body/eval_jaxpr/dot_general | solution.py:18
  174.0 5.0 %fusion.75 = bf16[512,128]{0,1:T(8,128)(2,1)S(1)} fusion(bf16[512,6144]{1,0:T(8,128)(2,1)} %multiply_convert_fusion.2, bf16[6144,128]{1,0:T(8,128)(2,1)S(1)} %copy-done.4), kind=kOutput, calls=%fused_computation.15.clone.1 | convolution fusion | flops 805437440 | bytes 7995392 | tf_op jit(solution)/shard_map/while/body/eval_jaxpr/dot_general | solution.py:100
  180.0 7.4 %fusion.74 = f32[6144,128]{1,0:T(8,128)} fusion(bf16[512,6144]{1,0:T(8,128)(2,1)} %multiply_convert_fusion.2, f32[6144,128]{1,0:T(8,128)} %get-tuple-element.253, pred[]{:T(512)S(6)} %compare.129, bf16[512,256]{0,1:T(8,128)(2,1)S(1)} %bitcast.112), kind=kOutput, calls=%fused_computation.10.clone.1 | convolution fusion | flops 807665664 | bytes 12713985 | tf_op jit(solution)/shard_map/while/body/eval_jaxpr/dot_general | solution.py:12
  188.4 5.6 %convolution_add_fusion.2 = f32[6144,128]{1,0:T(8,128)} fusion(f32[6144,128]{1,0:T(8,128)} %get-tuple-element.254, f32[512,6144]{1,0:T(8,128)S(1)} %copy-done.3, pred[]{:T(512)S(6)} %compare.129, bf16[512,256]{0,1:T(8,128)(2,1)S(1)} %bitcast.113), kind=kOutput, calls=%fused_computation.8.clone.1 | convolution fusion | flops 810024960 | bytes 19005440 | tf_op jit(solution)/shard_map/while/body/eval_jaxpr/dot_general | solution.py:12
  194.2 5.9 %fusion.70 = (f32[512]{0:T(512)S(1)}, f32[512,6144]{1,0:T(8,128)S(1)}) fusion(bf16[6144,128]{1,0:T(8,128)(2,1)} %get-tuple-element.270, bf16[512,256]{0,1:T(8,128)(2,1)S(1)} %bitcast.109, s32[512]{0:T(512)S(1)} %bitcast.132, pred[6144]{0:T(1024)(128)(4,1)S(1)} %get-tuple-element.267), kind=kOutput, calls=%fused_computation.92.clone.1 | convolution fusion | flops 821034496 | bytes 14297088 | tf_op jit(solution)/shard_map/while/body/eval_jaxpr/dot_general | solution.py:18
  213.6 5.2 %multiply_convert_fusion.2 = bf16[512,6144]{1,0:T(8,128)(2,1)} fusion(f32[512,6144]{1,0:T(8,128)S(1)} %fusion.72, bf16[6144,128]{1,0:T(8,128)(2,1)S(1)} %get-tuple-element.271, f32[512]{0:T(512)S(1)} %get-tuple-element.239, bf16[512,256]{0,1:T(8,128)(2,1)S(1)} %bitcast.111), kind=kOutput, calls=%fused_computation.2.clone.1 | convolution fusion | flops 814743552 | bytes 20580352 | tf_op jit(solution)/shard_map/while/body/eval_jaxpr/dot_general | solution.py:18
  218.8 5.0 %fusion.75 = bf16[512,128]{0,1:T(8,128)(2,1)S(1)} fusion(bf16[512,6144]{1,0:T(8,128)(2,1)} %multiply_convert_fusion.2, bf16[6144,128]{1,0:T(8,128)(2,1)S(1)} %copy-done.4), kind=kOutput, calls=%fused_computation.15.clone.1 | convolution fusion | flops 805437440 | bytes 7995392 | tf_op jit(solution)/shard_map/while/body/eval_jaxpr/dot_general | solution.py:100
  224.7 7.4 %fusion.74 = f32[6144,128]{1,0:T(8,128)} fusion(bf16[512,6144]{1,0:T(8,128)(2,1)} %multiply_convert_fusion.2, f32[6144,128]{1,0:T(8,128)} %get-tuple-element.253, pred[]{:T(512)S(6)} %compare.129, bf16[512,256]{0,1:T(8,128)(2,1)S(1)} %bitcast.112), kind=kOutput, calls=%fused_computation.10.clone.1 | convolution fusion | flops 807665664 | bytes 12713985 | tf_op jit(solution)/shard_map/while/body/eval_jaxpr/dot_general | solution.py:12
  233.2 5.6 %convolution_add_fusion.2 = f32[6144,128]{1,0:T(8,128)} fusion(f32[6144,128]{1,0:T(8,128)} %get-tuple-element.254, f32[512,6144]{1,0:T(8,128)S(1)} %copy-done.3, pred[]{:T(512)S(6)} %compare.129, bf16[512,256]{0,1:T(8,128)(2,1)S(1)} %bitcast.113), kind=kOutput, calls=%fused_computation.8.clone.1 | convolution fusion | flops 810024960 | bytes 19005440 | tf_op jit(solution)/shard_map/while/body/eval_jaxpr/dot_general | solution.py:12
  238.8 18.6 %all_to_all.20 = bf16[32,48,256]{2,1,0:T(8,128)(2,1)S(1)} all-to-all(bf16[32,48,256]{2,1,0:T(8,128)(2,1)} %bitcast.131), channel_id=1, replica_groups=mesh['seq'=32,'head'=4] {'seq'}, dimensions={0} | all-to-all | bytes 1572864 | tf_op jit(solution)/shard_map/all_to_all | solution.py:119
  257.9 8.6 %fusion.15 = f32[5120,1024]{1,0:T(8,128)} fusion(bf16[192,5120]{1,0:T(8,128)(2,1)S(1)} %copy-done.7, bf16[24,8,8,128]{3,2,1,0:T(8,128)(2,1)S(1)} %bitcast.130), kind=kOutput, calls=%fused_computation.40 | convolution fusion | flops 2013265920 | bytes 23330816 | tf_op jit(solution)/shard_map/dot_general | solution.py:12
  266.5 5.9 %pad_maximum_fusion = f32[6144,256]{1,0:T(8,128)} fusion(f32[6144,128]{1,0:T(8,128)} %get-tuple-element.58, f32[6144,128]{1,0:T(8,128)} %get-tuple-element.57), kind=kLoop, calls=%fused_computation.25 | loop fusion | flops 1572864 | bytes 12582912 | tf_op jit(solution)/shard_map/concatenate | solution.py:116
  272.4 5.1 %all-to-all-start.3 = ((f32[32,192,256]{2,1,0:T(8,128)}), f32[32,192,256]{2,1,0:T(8,128)}, u32[]{:S(2)}, u32[]{:S(2)}) async-start(f32[32,192,256]{2,1,0:T(8,128)} %bitcast.114), calls=%async_computation.3 | async-start | bytes 12582912 | tf_op jit(solution)/shard_map/all_to_all | solution.py:120
  277.7 86.9 %all-to-all-done.3 = f32[32,192,256]{2,1,0:T(8,128)} async-done(((f32[32,192,256]{2,1,0:T(8,128)}), f32[32,192,256]{2,1,0:T(8,128)}, u32[]{:S(2)}, u32[]{:S(2)}) %all-to-all-start.3) | async-done | bytes 6291488 | tf_op jit(solution)/shard_map/all_to_all | solution.py:120
  372.6 4.8 %copy.27 = bf16[512,3072]{0,1:T(8,128)(2,1)} copy(bf16[512,3072]{1,0:T(8,128)(2,1)} %convolution_convert_fusion) | data formatting | bytes 6291456 | tf_op jit(solution)/shard_map/convert_element_type | solution.py:134
  377.3 4.8 %copy.28 = bf16[512,3,1024]{2,0,1:T(8,128)(2,1)} copy(bf16[512,3,1024]{0,2,1:T(8,128)(2,1)} %bitcast.115) | data formatting | bytes 6291456
  382.1 38.2 %reduce-scatter.2.cloned.1.call-done = f32[160,1024]{1,0:T(8,128)} async-done(((f32[5120,1024]{1,0:T(8,128)}), f32[160,1024]{1,0:T(8,128)}) %reduce-scatter.2.cloned.1.call-update) | async-done | bytes 655376 | tf_op jit(solution)/shard_map/reduce_scatter | solution.py:136
  (133 shorter events, 79.5 us)
Async XLA Ops:
  7.2 1.3 copy-start
  7.2 70.5 %all-gather.2.cloned.1.call-start = ((), (), s32[]{:S(2)}) async-start(), calls=%async_computation.5 | async-start | bytes 2457600 | tf_op jit(solution)/shard_map/all_gather | solution.py:49
  10.4 4.7 %copy-start.9 = (s32[1,192]{1,0:T(1,128)S(1)}, s32[1,192]{1,0:T(1,128)}, u32[]{:S(2)}) copy-start(s32[1,192]{1,0:T(1,128)} %param.10) | copy-start | bytes 2308
  28.2 27.9 %copy-start.8 = (s32[32]{0:T(128)S(1)}, s32[32]{0:T(128)}, u32[]{:S(2)}) copy-start(s32[32]{0:T(128)} %param.11) | copy-start | bytes 388
  28.2 57.5 %all-to-all-start.1 = ((bf16[32,192,256]{2,1,0:T(8,128)(2,1)}), bf16[32,192,256]{2,1,0:T(8,128)(2,1)}, u32[]{:S(2)}, u32[]{:S(2)}) async-start(bf16[32,192,256]{2,1,0:T(8,128)(2,1)} %bitcast.117), calls=%async_computation.1 | async-start | bytes 6291456 | tf_op jit(solution)/shard_map/all_to_all | solution.py:66
  85.7 21.6 %all-to-all-start = ((bf16[32,48,256]{2,1,0:T(8,128)(2,1)}), bf16[32,48,256]{2,1,0:T(8,128)(2,1)S(1)}, u32[]{:S(2)}, u32[]{:S(2)}) async-start(bf16[32,48,256]{2,1,0:T(8,128)(2,1)} %bitcast.37), calls=%async_computation | async-start | bytes 1572864 | tf_op jit(solution)/shard_map/all_to_all | solution.py:65
  93.1 327.2 %reduce-scatter.2.cloned.1.call-start = ((), (), s32[]{:S(2)}) async-start(), calls=%async_computation.6 | async-start | bytes 21626880 | tf_op jit(solution)/shard_map/reduce_scatter | solution.py:136
  107.3 6.1 %copy-start.5 = (bf16[3,512,256]{2,1,0:T(8,128)(2,1)}, bf16[3,512,256]{2,1,0:T(8,128)(2,1)S(1)}, u32[]{:S(2)}) copy-start(bf16[3,512,256]{2,1,0:T(8,128)(2,1)S(1)} %get-tuple-element.269) | copy-start | bytes 2359300 | tf_op jit(solution)/shard_map/while
  122.3 4.6 %copy-start.2 = (f32[512,6144]{1,0:T(8,128)}, f32[512,6144]{1,0:T(8,128)S(1)}, u32[]{:S(2)}) copy-start(f32[512,6144]{1,0:T(8,128)S(1)} %fusion.72) | copy-start | bytes 37748740 | tf_op jit(solution)/shard_map/while
  126.9 5.2 %copy-start.4 = (bf16[6144,128]{1,0:T(8,128)(2,1)S(1)}, bf16[6144,128]{1,0:T(8,128)(2,1)}, u32[]{:S(2)}) copy-start(bf16[6144,128]{1,0:T(8,128)(2,1)} %get-tuple-element.270) | copy-start | bytes 4718596 | tf_op jit(solution)/shard_map/while
  138.0 7.5 %copy-start.3 = (f32[512,6144]{1,0:T(8,128)S(1)}, f32[512,6144]{1,0:T(8,128)}, u32[]{:S(2)}) copy-start(f32[512,6144]{1,0:T(8,128)} %copy-done.2) | copy-start | bytes 37748740 | tf_op jit(solution)/shard_map/while
  145.6 3.7 copy-start.6
  149.2 6.1 %copy-start.5 = (bf16[3,512,256]{2,1,0:T(8,128)(2,1)}, bf16[3,512,256]{2,1,0:T(8,128)(2,1)S(1)}, u32[]{:S(2)}) copy-start(bf16[3,512,256]{2,1,0:T(8,128)(2,1)S(1)} %get-tuple-element.269) | copy-start | bytes 2359300 | tf_op jit(solution)/shard_map/while
  164.2 4.6 %copy-start.2 = (f32[512,6144]{1,0:T(8,128)}, f32[512,6144]{1,0:T(8,128)S(1)}, u32[]{:S(2)}) copy-start(f32[512,6144]{1,0:T(8,128)S(1)} %fusion.72) | copy-start | bytes 37748740 | tf_op jit(solution)/shard_map/while
  168.8 5.2 %copy-start.4 = (bf16[6144,128]{1,0:T(8,128)(2,1)S(1)}, bf16[6144,128]{1,0:T(8,128)(2,1)}, u32[]{:S(2)}) copy-start(bf16[6144,128]{1,0:T(8,128)(2,1)} %get-tuple-element.270) | copy-start | bytes 4718596 | tf_op jit(solution)/shard_map/while
  179.9 8.4 %copy-start.3 = (f32[512,6144]{1,0:T(8,128)S(1)}, f32[512,6144]{1,0:T(8,128)}, u32[]{:S(2)}) copy-start(f32[512,6144]{1,0:T(8,128)} %copy-done.2) | copy-start | bytes 37748740 | tf_op jit(solution)/shard_map/while
  188.4 5.6 %copy-start.6 = (bf16[3,512,256]{2,1,0:T(8,128)(2,1)S(1)}, bf16[3,512,256]{2,1,0:T(8,128)(2,1)}, u32[]{:S(2)}) copy-start(bf16[3,512,256]{2,1,0:T(8,128)(2,1)} %copy-done.5) | copy-start | bytes 2359300 | tf_op jit(solution)/shard_map/while
  194.0 6.1 %copy-start.5 = (bf16[3,512,256]{2,1,0:T(8,128)(2,1)}, bf16[3,512,256]{2,1,0:T(8,128)(2,1)S(1)}, u32[]{:S(2)}) copy-start(bf16[3,512,256]{2,1,0:T(8,128)(2,1)S(1)} %get-tuple-element.269) | copy-start | bytes 2359300 | tf_op jit(solution)/shard_map/while
  209.0 4.6 %copy-start.2 = (f32[512,6144]{1,0:T(8,128)}, f32[512,6144]{1,0:T(8,128)S(1)}, u32[]{:S(2)}) copy-start(f32[512,6144]{1,0:T(8,128)S(1)} %fusion.72) | copy-start | bytes 37748740 | tf_op jit(solution)/shard_map/while
  213.6 5.2 %copy-start.4 = (bf16[6144,128]{1,0:T(8,128)(2,1)S(1)}, bf16[6144,128]{1,0:T(8,128)(2,1)}, u32[]{:S(2)}) copy-start(bf16[6144,128]{1,0:T(8,128)(2,1)} %get-tuple-element.270) | copy-start | bytes 4718596 | tf_op jit(solution)/shard_map/while
  224.7 8.4 %copy-start.3 = (f32[512,6144]{1,0:T(8,128)S(1)}, f32[512,6144]{1,0:T(8,128)}, u32[]{:S(2)}) copy-start(f32[512,6144]{1,0:T(8,128)} %copy-done.2) | copy-start | bytes 37748740 | tf_op jit(solution)/shard_map/while
  233.2 5.6 %copy-start.6 = (bf16[3,512,256]{2,1,0:T(8,128)(2,1)S(1)}, bf16[3,512,256]{2,1,0:T(8,128)(2,1)}, u32[]{:S(2)}) copy-start(bf16[3,512,256]{2,1,0:T(8,128)(2,1)} %copy-done.5) | copy-start | bytes 2359300 | tf_op jit(solution)/shard_map/while
  238.8 19.1 %copy-start.7 = (bf16[192,5120]{1,0:T(8,128)(2,1)S(1)}, bf16[192,5120]{1,0:T(8,128)(2,1)}, u32[]{:S(2)}) copy-start(bf16[192,5120]{1,0:T(8,128)(2,1)} %all-gather.2.cloned.1.call-done) | copy-start | bytes 5898244
  272.4 92.2 %all-to-all-start.3 = ((f32[32,192,256]{2,1,0:T(8,128)}), f32[32,192,256]{2,1,0:T(8,128)}, u32[]{:S(2)}, u32[]{:S(2)}) async-start(f32[32,192,256]{2,1,0:T(8,128)} %bitcast.114), calls=%async_computation.3 | async-start | bytes 12582912 | tf_op jit(solution)/shard_map/all_to_all | solution.py:120
  369.1 0.7 copy-start.10
  377.3 43.0 %copy-start.1 = (bf16[512,1280]{1,0:T(8,128)(2,1)S(1)}, bf16[512,1280]{1,0:T(8,128)(2,1)}, u32[]{:S(2)}) copy-start(bf16[512,1280]{1,0:T(8,128)(2,1)} %param.8) | copy-start | bytes 3932164
Sparse Core Ops, SparseCore 0:
  10.5 32.9 all-gather.1
  266.6 153.6 reduce-scatter.1
where the time goes:
time: 436 us; the launch traced here: 428 us
  waiting for transfers between devices  136 us (31%)
  matrix products  115 us (26%)
  other arithmetic  74.8 us (17%)
  local copies, waits for them, and re-layouts  46.2 us (11%)
  starting transfers between devices  22.2 us (5%)
  blocking collectives  18.6 us (4%)
  between operations  14.7 us (3%)
    all_to_all x1, waiting for transfers between devices, on_device(): lax.all_to_all(key_back, 'seq', split_axis=0, concat_axis=0, tiled=True)  86.9 us
    dot_general x8, matrix products, contract_rows(): lax.dot_general(left, right, (((0,), (0,)), ((), ())), preferred_element_...  47.5 us
    reduce_scatter x1, waiting for transfers between devices, on_device(): lax.psum_scatter(contract_rows(grad_rows, attended_low), 'seq', scatter_d...  38.2 us
    dot_general x6, matrix products, contract_cols(): lax.dot_general(left, right, (((1,), (1,)), ((), ())), preferred_element_...  33.5 us
    gather x26, other arithmetic, on_device(): surviving_token_count[key_position // slots_per_shard]  22.5 us
    all_to_all x1, blocking collectives, on_device(): lax.all_to_all(query_back, 'seq', split_axis=0, concat_axis=0, tiled=True)  18.6 us
    lt x1, other arithmetic, on_device(): key_position % slots_per_shard  15.6 us
    dot_general x3, matrix products, attend(): jnp.dot(grad_scores, key_mat, preferred_element_type=jnp.float32)  15.1 us
  transfers between devices with their start and end apart: 5, of which 3 were waited for; matrix products, arithmetic and copies ran while one was open for 22% of the time, Pallas kernels for 0%

commit v1 on v0

v1 whole, which is shorter than its diff:
```python
import math

import jax
import jax.numpy as jnp
from jax import lax
from jax.experimental import pallas as pl
from jax.experimental.pallas import tpu as pltpu
from jax.sharding import PartitionSpec as P

DH = 128
BQ = 256
BK = 512
GROUP = 16
NEG = -1e30


def contract_rows(left, right):
    return lax.dot_general(
        left, right, (((0,), (0,)), ((), ())), preferred_element_type=jnp.float32
    )


def contract_cols(left, right):
    return lax.dot_general(
        left, right, (((1,), (1,)), ((), ())), preferred_element_type=jnp.float32
    )


def wide(column, width):
    return jnp.concatenate([column] * (width // DH), axis=1)


def attend_kernel(
    count_ref,
    quarter_ref,
    q_ref,
    k_ref,
    bias_ref,
    q_out,
    k_out,
    qc,
    gc,
    kc,
    vc,
    dkc,
    dvc,
    oc,
    s_scr,
    qpos,
    peak,
    total,
    acc,
    group_pos,
):
    shards, part_rows, _ = q_ref.shape
    slots = k_ref.shape[1]
    quarter = quarter_ref[0]
    groups = part_rows // GROUP
    score_scale = 1.0 / math.sqrt(DH)
    log2e = score_scale * math.log2(math.e)

    def pack(s, carry):
        at_k, at_q = carry
        live = (count_ref[s] + GROUP - 1) // GROUP
        first = lax.rem(quarter + s, 4)
        at_k = pl.multiple_of(at_k, GROUP)
        at_q = pl.multiple_of(at_q, GROUP)
        kc[pl.ds(at_k, slots), :] = k_ref[s, :, :DH]
        vc[pl.ds(at_k, slots), :] = k_ref[s, :, DH:]
        qc[pl.ds(at_q, part_rows), :] = q_ref[s, :, :DH]
        gc[pl.ds(at_q, part_rows), :] = q_ref[s, :, DH:]
        rows = lax.broadcasted_iota(jnp.int32, (GROUP, DH), 0)
        for i in range(groups):
            base = at_k + (first + 4 * i) * GROUP
            qpos[pl.ds(at_q + i * GROUP, GROUP), :] = base + rows
            group_pos[at_q // GROUP + i] = base
        return at_k + live * GROUP, at_q + (live - first + 3) // 4 * GROUP

    end_k, end_q = lax.fori_loop(0, shards, pack, (jnp.int32(0), jnp.int32(0)))
    end_k = pl.multiple_of(end_k, GROUP)
    end_q = pl.multiple_of(end_q, GROUP)
    kc[pl.ds(end_k, BK), :] = jnp.zeros((BK, DH), jnp.bfloat16)
    vc[pl.ds(end_k, BK), :] = jnp.zeros((BK, DH), jnp.bfloat16)
    qc[pl.ds(end_q, BQ), :] = jnp.zeros((BQ, DH), jnp.bfloat16)
    gc[pl.ds(end_q, BQ), :] = jnp.zeros((BQ, DH), jnp.bfloat16)
    qpos[pl.ds(end_q, BQ), :] = jnp.zeros((BQ, DH), jnp.int32)
    blocks = (end_q + BQ - 1) // BQ
    oc[pl.ds(pl.multiple_of(blocks * BQ, BQ), part_rows), :] = jnp.zeros(
        (part_rows, 2 * DH), jnp.bfloat16
    )

    def clear(i, carry):
        rows = pl.ds(pl.multiple_of(i * slots, slots), slots)
        dkc[rows, :] = jnp.zeros((slots, DH), jnp.float32)
        dvc[rows, :] = jnp.zeros((slots, DH), jnp.float32)
        return carry

    lax.fori_loop(0, shards, clear, 0)

    def block(b, carry):
        rows = pl.ds(pl.multiple_of(b * BQ, BQ), BQ)
        last_group = jnp.minimum((b + 1) * (BQ // GROUP), end_q // GROUP) - 1
        chunks = (group_pos[last_group] + GROUP + BK - 1) // BK
        clear_chunks = (group_pos[b * (BQ // GROUP)] + 1) // BK

        def score(c, masked):
            at = pl.multiple_of(c * BK, BK)
            keys = pl.ds(at, BK)
            s = contract_cols(qc[rows, :], kc[keys, :]) + bias_ref[:, keys]
            if masked:
                column = at + lax.broadcasted_iota(jnp.int32, (BQ, BK), 1)
                s = jnp.where(column <= wide(qpos[rows, :], BK), s, NEG)
            s_scr[:, keys] = s
            top = peak[...]
            for i in range(BK // DH):
                top = jnp.maximum(top, s[:, i * DH : (i + 1) * DH])
            peak[...] = top

        peak[...] = jnp.full((BQ, DH), NEG, jnp.float32)

        def score_clear(c, carry):
            score(c, False)
            return carry

        def score_masked(c, carry):
            score(c, True)
            return carry

        lax.fori_loop(0, clear_chunks, score_clear, 0)
        lax.fori_loop(clear_chunks, chunks, score_masked, 0)
        peak[...] = jnp.broadcast_to(jnp.max(peak[...], axis=1, keepdims=True), (BQ, DH))
        total[...] = jnp.zeros((BQ, DH), jnp.float32)
        acc[...] = jnp.zeros((BQ, DH), jnp.float32)

        def weigh(c, carry):
            keys = pl.ds(pl.multiple_of(c * BK, BK), BK)
            p = jnp.exp2((s_scr[:, keys] - wide(peak[...], BK)) * log2e)
            s_scr[:, keys] = p
            add = total[...]
            for i in range(BK // DH):
                add = add + p[:, i * DH : (i + 1) * DH]
            total[...] = add
            acc[...] += jnp.dot(
                p.astype(jnp.bfloat16), vc[keys, :], preferred_element_type=jnp.float32
            )
            return carry

        lax.fori_loop(0, chunks, weigh, 0)
        inverse = 1.0 / jnp.broadcast_to(
            jnp.sum(total[...], axis=1, keepdims=True), (BQ, DH)
        )
        total[...] = inverse
        attended = acc[...] * inverse
        oc[rows, DH:] = attended.astype(jnp.bfloat16)
        peak[...] = jnp.broadcast_to(
            jnp.sum(gc[rows, :].astype(jnp.float32) * attended, axis=1, keepdims=True), (BQ, DH)
        )
        acc[...] = jnp.zeros((BQ, DH), jnp.float32)

        def back(c, carry):
            keys = pl.ds(pl.multiple_of(c * BK, BK), BK)
            p = s_scr[:, keys] * wide(total[...], BK)
            grad_probs = contract_cols(gc[rows, :], vc[keys, :])
            ds = (p * (grad_probs - wide(peak[...], BK))).astype(jnp.bfloat16)
            acc[...] += jnp.dot(ds, kc[keys, :], preferred_element_type=jnp.float32)
            dkc[keys, :] += contract_rows(ds, qc[rows, :])
            dvc[keys, :] += contract_rows(p.astype(jnp.bfloat16), gc[rows, :])
            return carry

        lax.fori_loop(0, chunks, back, 0)
        oc[rows, :DH] = (acc[...] * score_scale).astype(jnp.bfloat16)
        return carry

    lax.fori_loop(0, blocks, block, 0)

    def unpack(s, carry):
        at_k, at_q = carry
        live = (count_ref[s] + GROUP - 1) // GROUP
        first = lax.rem(quarter + s, 4)
        at_k = pl.multiple_of(at_k, GROUP)
        at_q = pl.multiple_of(at_q, GROUP)
        q_out[s] = oc[pl.ds(at_q, part_rows), :]
        k_out[s, :, :DH] = (dkc[pl.ds(at_k, slots), :] * score_scale).astype(jnp.bfloat16)
        k_out[s, :, DH:] = dvc[pl.ds(at_k, slots), :].astype(jnp.bfloat16)
        return at_k + live * GROUP, at_q + (live - first + 3) // 4 * GROUP

    lax.fori_loop(0, shards, unpack, (jnp.int32(0), jnp.int32(0)))


def attend(counts, quarter, query_in, key_in):
    shards, part_rows, _ = query_in.shape
    slots = key_in.shape[1]
    keys = shards * slots
    queries = shards * part_rows
    rounded = (counts + GROUP - 1) // GROUP * GROUP
    start = jnp.cumsum(rounded) - rounded
    place = jnp.arange(keys, dtype=jnp.int32)[None, :]
    live = jnp.any(
        (place >= start[:, None]) & (place < (start + counts)[:, None]), axis=0, keepdims=True
    )
    bias = jnp.where(live, 0.0, NEG).astype(jnp.float32)
    vmem = pl.BlockSpec(memory_space=pltpu.VMEM)
    smem = pl.BlockSpec(memory_space=pltpu.SMEM)
    return pl.pallas_call(
        attend_kernel,
        out_shape=(
            jax.ShapeDtypeStruct(query_in.shape, jnp.bfloat16),
            jax.ShapeDtypeStruct(key_in.shape, jnp.bfloat16),
        ),
        in_specs=[smem, smem, vmem, vmem, vmem],
        out_specs=(vmem, vmem),
        scratch_shapes=[
            pltpu.VMEM((queries + BQ, DH), jnp.bfloat16),
            pltpu.VMEM((queries + BQ, DH), jnp.bfloat16),
            pltpu.VMEM((keys + BK, DH), jnp.bfloat16),
            pltpu.VMEM((keys + BK, DH), jnp.bfloat16),
            pltpu.VMEM((keys, DH), jnp.float32),
            pltpu.VMEM((keys, DH), jnp.float32),
            pltpu.VMEM((queries + BQ, 2 * DH), jnp.bfloat16),
            pltpu.VMEM((BQ, keys), jnp.float32),
            pltpu.VMEM((queries + BQ, DH), jnp.int32),
            pltpu.VMEM((BQ, DH), jnp.float32),
            pltpu.VMEM((BQ, DH), jnp.float32),
            pltpu.VMEM((BQ, DH), jnp.float32),
            pltpu.SMEM((queries // GROUP + 8,), jnp.int32),
        ],
        compiler_params=pltpu.CompilerParams(vmem_limit_bytes=48 * 1024 * 1024),
        cost_estimate=pl.CostEstimate(
            flops=6 * queries * keys * DH, bytes_accessed=16 * 1024 * 1024, transcendentals=0
        ),
        name="attend",
    )(counts, quarter, query_in, key_in, bias)


def on_device(
    projections,
    output_gradient,
    output_projection_weight,
    kept_token_indices,
    surviving_token_count,
):
    tok_dev = projections.shape[0]
    group_width = projections.shape[2]
    slots = kept_token_indices.shape[1]
    heads_local = group_width // DH
    seq_count = lax.axis_size("seq")
    quarters = seq_count // heads_local
    part_rows = slots // quarters
    me = lax.axis_index("seq")
    my_quarter = (me % quarters).astype(jnp.int32)[None]

    kept = kept_token_indices[0]
    dealt = kept.reshape(part_rows // GROUP, quarters, GROUP).transpose(1, 0, 2)
    dealt = lax.dynamic_slice_in_dim(
        jnp.concatenate([dealt, dealt], axis=0), me % quarters, quarters, axis=0
    ).reshape(slots)
    token = jnp.arange(tok_dev, dtype=jnp.int32)[None, :]
    selector = (kept[:, None] == token).astype(jnp.bfloat16)
    dealt_selector = (dealt[:, None] == token).astype(jnp.bfloat16)

    def pick(which, values):
        return jnp.dot(which, values, preferred_element_type=jnp.float32).astype(jnp.bfloat16)

    grad_local = pick(dealt_selector, output_gradient)
    grad_rows = lax.all_gather(grad_local, "head", axis=1, tiled=True)
    query = pick(dealt_selector, projections[:, 0])
    key = pick(selector, projections[:, 1])
    value = pick(selector, projections[:, 2])

    def head_major(matrix):
        return matrix.reshape(slots, heads_local, DH).transpose(1, 0, 2)

    key_side = jnp.concatenate([head_major(key), head_major(value)], axis=2)
    key_side = jnp.broadcast_to(key_side[:, None], (heads_local, quarters, slots, 2 * DH))
    key_side = key_side.reshape(seq_count, slots, 2 * DH)
    key_in = lax.all_to_all(key_side, "seq", split_axis=0, concat_axis=0, tiled=True)
    grad_attn = jnp.dot(
        grad_rows, output_projection_weight, preferred_element_type=jnp.float32
    ).astype(jnp.bfloat16)
    query_side = jnp.concatenate([head_major(query), head_major(grad_attn)], axis=2)
    query_side = query_side.reshape(seq_count, part_rows, 2 * DH)
    query_in = lax.all_to_all(query_side, "seq", split_axis=0, concat_axis=0, tiled=True)

    query_back, key_back = attend(surviving_token_count, my_quarter, query_in, key_in)

    query_home = lax.all_to_all(query_back, "seq", split_axis=0, concat_axis=0, tiled=True)
    query_home = query_home.reshape(heads_local, slots, 2 * DH)
    attended_low = query_home[:, :, DH:].transpose(1, 0, 2).reshape(slots, group_width)
    weight_grad = lax.psum_scatter(
        contract_rows(grad_rows, attended_low).astype(jnp.bfloat16),
        "seq",
        scatter_dimension=0,
        tiled=True,
    ).astype(jnp.float32)
    key_home = lax.all_to_all(key_back, "seq", split_axis=0, concat_axis=0, tiled=True)
    key_home = jnp.sum(
        key_home.reshape(heads_local, quarters, slots, 2 * DH).astype(jnp.float32), axis=1
    ).astype(jnp.bfloat16)

    def rows_major(part):
        return part.transpose(1, 0, 2).reshape(slots, group_width)

    projection_grad = jnp.stack(
        [
            contract_rows(dealt_selector, rows_major(query_home[:, :, :DH])).astype(jnp.bfloat16),
            contract_rows(selector, rows_major(key_home[:, :, :DH])).astype(jnp.bfloat16),
            contract_rows(selector, rows_major(key_home[:, :, DH:])).astype(jnp.bfloat16),
        ],
        axis=1,
    )
    return (projection_grad, weight_grad)


def solution(mesh):
    return jax.shard_map(
        on_device,
        mesh=mesh,
        in_specs=(P("seq", None, "head"), P("seq", "head"), P(None, "head"), P("seq", None), P()),
        out_specs=(P("seq", None, "head"), P("seq", "head")),
        check_vma=False,
    )
```

time: 436 us -> 251 us (0.58); the launches traced: 428 us -> 250 us
  matrix products: 115 us -> 20.2 us
  other arithmetic: 74.8 us -> 9.21 us
  local copies, waits for them, and re-layouts: 46.2 us -> 5.75 us
  Pallas kernels: 0 us -> 28.9 us
  waiting for transfers between devices: 136 us -> 127 us
  blocking collectives: 18.6 us -> 24.5 us
    dot_general x14 -> x4, matrix products: 60.4 us -> 6.2 us  [pick(): jnp.dot(which, values, preferred_element_type=jnp.float32)]
    all_to_all x1, waiting for transfers between devices: 86.9 us -> 38.4 us  [on_device(): lax.all_to_all(key_back, 'seq', split_axis=0, concat_axis=0, tiled=True)]
    dot_general x8 -> x4, matrix products: 47.5 us -> 7.25 us  [contract_rows(): lax.dot_general(left, right, (((0,), (0,)), ((), ())), preferred_element_...]
    pallas_call x0 -> x1, Pallas kernels: none -> 28.9 us  [attend(): pl.pallas_call(attend_kernel, out_shape=(jax.ShapeDtypeStruct(query_in.sh...]
    gather x26 -> x0, other arithmetic: 22.5 us -> none  [on_device(): surviving_token_count[key_position // slots_per_shard]]
    all_gather x1, waiting for transfers between devices: 0.02 us -> 16.2 us  [on_device(): grad_rows = lax.all_gather(grad_local, 'head', axis=1, tiled=True)]
    lt x1 -> x0, other arithmetic: 15.6 us -> none  [on_device(): key_position % slots_per_shard]
    reduce_sum x4 -> x1, other arithmetic: 17.2 us -> 2.32 us  [on_device(): jnp.sum(key_home.reshape(heads_local, quarters, slots, 2 * DH).astype(jnp...]
  transfers between devices with their start and end apart: 5 -> 5, of which waited for: 3 -> 5; matrix products, arithmetic and copies ran while one was open for 22% -> 9% of each run, Pallas kernels for 0% -> 0%
where the time goes in v1:
time: 251 us; the launch traced here: 250 us
  waiting for transfers between devices  127 us (51%)
  Pallas kernels  28.9 us (12%)
  blocking collectives  24.5 us (10%)
  starting transfers between devices  21 us (8%)
  matrix products  20.2 us (8%)
  between operations  14.3 us (6%)
  other arithmetic  9.21 us (4%)
  local copies, waits for them, and re-layouts  5.75 us (2%)
    reduce_scatter x1, waiting for transfers between devices, on_device(): lax.psum_scatter(contract_rows(grad_rows, attended_low).astype(jnp.bfloat...  44.9 us
    all_to_all x1, waiting for transfers between devices, on_device(): lax.all_to_all(key_back, 'seq', split_axis=0, concat_axis=0, tiled=True)  38.4 us
    pallas_call x1, Pallas kernels, attend(): pl.pallas_call(attend_kernel, out_shape=(jax.ShapeDtypeStruct(query_in.sh...  28.9 us
    all_to_all x1, blocking collectives, on_device(): lax.all_to_all(query_back, 'seq', split_axis=0, concat_axis=0, tiled=True)  24.5 us
    all_gather x1, waiting for transfers between devices, on_device(): grad_rows = lax.all_gather(grad_local, 'head', axis=1, tiled=True)  16.2 us
    all_to_all x1, waiting for transfers between devices, on_device(): lax.all_to_all(query_side, 'seq', split_axis=0, concat_axis=0, tiled=True)  13.7 us
    all_to_all x1, waiting for transfers between devices, on_device(): lax.all_to_all(key_side, 'seq', split_axis=0, concat_axis=0, tiled=True)  13.4 us
    all_to_all x1, starting transfers between devices, on_device(): lax.all_to_all(key_side, 'seq', split_axis=0, concat_axis=0, tiled=True)  9.48 us
  transfers between devices with their start and end apart: 5, of which 5 were waited for; matrix products, arithmetic and copies ran while one was open for 9% of the time, Pallas kernels for 0%

profile of v1, /device:TPU:1, one launch (start us, length us, event | category | flops | bytes accessed | tf_op | source)
XLA Modules:
  0.0 250.4 jit_solution(10186516117178999090)
XLA Ops:
  7.3 0.5 broadcast.48
  7.8 1.3 reduce.5
  9.3 1.2 convolution_convert_fusion.1
  10.6 1.7 fusion.5
  12.3 1.6 fusion.4
  14.2 0.2 copy.30
  14.3 2.0 broadcast_in_dim.11
  16.3 9.5 %all-to-all-start.1 = ((bf16[32,192,256]{2,1,0:T(8,128)(2,1)}), bf16[32,192,256]{2,1,0:T(8,128)(2,1)}, u32[]{:S(2)}, u32[]{:S(2)}) async-start(bf16[32,192,256]{2,1,0:T(8,128)(2,1)} %bitcast.81), calls=%async_computation.1 | async-start | bytes 6291456 | tf_op jit(solution)/shard_map/all_to_all | solution.py:276
  25.8 1.6 fusion.3
  27.6 16.2 %all-gather.2.cloned.1.call-done = bf16[192,5120]{1,0:T(8,128)(2,1)} async-done(((bf16[192,1280]{1,0:T(8,128)(2,1)}), bf16[192,5120]{1,0:T(8,128)(2,1)}) %all-gather.2.cloned.1.call-update) | async-done | bytes 1966096 | tf_op jit(solution)/shard_map/all_gather | solution.py:265
  43.7 6.8 %fusion.6 = bf16[24,8,8,128]{3,2,1,0:T(8,128)(2,1)S(1)} fusion(bf16[192,5120]{1,0:T(8,128)(2,1)} %all-gather.2.cloned.1.call-done, bf16[5120,1024]{1,0:T(8,128)(2,1)} %param.7), kind=kOutput, calls=%fused_computation.17 | convolution fusion | flops 2013462528 | bytes 12845056 | tf_op jit(solution)/shard_map/dot_general | solution.py:277
  50.6 1.0 pad_maximum_fusion.1
  51.6 13.4 %all-to-all-done.1.k_ref = bf16[32,192,256]{2,1,0:T(8,128)(2,1)} async-done(((bf16[32,192,256]{2,1,0:T(8,128)(2,1)}), bf16[32,192,256]{2,1,0:T(8,128)(2,1)}, u32[]{:S(2)}, u32[]{:S(2)}) %all-to-all-start.1) | async-done | bytes 3145760 | tf_op jit(solution)/shard_map/all_to_all | solution.py:276
  65.0 6.4 %all-to-all-start = ((bf16[32,48,256]{2,1,0:T(8,128)(2,1)}), bf16[32,48,256]{2,1,0:T(8,128)(2,1)S(1)}, u32[]{:S(2)}, u32[]{:S(2)}) async-start(bf16[32,48,256]{2,1,0:T(8,128)(2,1)} %bitcast.5), calls=%async_computation | async-start | bytes 1572864 | tf_op jit(solution)/shard_map/all_to_all | solution.py:282
  71.8 0.3 fusion.14
  72.1 13.7 %all-to-all-done.q_ref = bf16[32,48,256]{2,1,0:T(8,128)(2,1)S(1)} async-done(((bf16[32,48,256]{2,1,0:T(8,128)(2,1)}), bf16[32,48,256]{2,1,0:T(8,128)(2,1)S(1)}, u32[]{:S(2)}, u32[]{:S(2)}) %all-to-all-start) | async-done | bytes 786464 | tf_op jit(solution)/shard_map/all_to_all | solution.py:282
  85.8 28.9 %attend.1 = (bf16[32,48,256]{2,1,0:T(8,128)(2,1)S(1)}, bf16[32,192,256]{2,1,0:T(8,128)(2,1)S(1)}) custom-call(s32[32]{0:T(128)S(1)} %copy-done.2, s32[1]{0:T(128)} %bitcast.1.quarter_ref, bf16[32,48,256]{2,1,0:T(8,128)(2,1)S(1)} %all-to-all-done.q_ref, bf16[32,192,256]{2,1,0:T(8,128)(2,1)} %all-to-all-done.1.k_ref, f32[1,6144]{1,0:T(1,128)S(1)} %bitcast.80), custom_call_target="tpu_custom_call" | custom-call | flops 7247757312 | bytes 16777216 | tf_op jit(solution)/shard_map/attend/pallas_call | solution.py:204
  114.7 1.7 copy-done.1
  116.4 24.5 %all_to_all.20 = bf16[32,48,256]{2,1,0:T(8,128)(2,1)S(1)} all-to-all(bf16[32,48,256]{2,1,0:T(8,128)(2,1)S(1)} %get-tuple-element.4), channel_id=1, replica_groups=mesh['seq'=32,'head'=4] {'seq'}, dimensions={0} | all-to-all | bytes 1572864 | tf_op jit(solution)/shard_map/all_to_all | solution.py:286
  141.0 0.3 copy.37
  141.3 5.6 %convolution_convert_fusion = bf16[5120,1024]{1,0:T(8,128)(2,1)} fusion(bf16[192,5120]{1,0:T(8,128)(2,1)S(1)} %copy-done.3, bf16[24,8,8,128]{3,2,1,0:T(8,128)(2,1)S(1)} %bitcast.88), kind=kOutput, calls=%fused_computation | convolution fusion | flops 2018508800 | bytes 12845056 | tf_op jit(solution)/shard_map/dot_general | solution.py:18
  146.9 5.0 %all-to-all-start.3 = ((bf16[32,192,256]{2,1,0:T(8,128)(2,1)}), bf16[32,192,256]{2,1,0:T(8,128)(2,1)}, u32[]{:S(2)}, u32[]{:S(2)}) async-start(bf16[32,192,256]{2,1,0:T(8,128)(2,1)} %copy-done.1), calls=%async_computation.3 | async-start | bytes 6291456 | tf_op jit(solution)/shard_map/all_to_all | solution.py:295
  151.9 0.3 copy.36
  152.2 0.6 fusion
  152.7 38.4 %all-to-all-done.3 = bf16[32,192,256]{2,1,0:T(8,128)(2,1)} async-done(((bf16[32,192,256]{2,1,0:T(8,128)(2,1)}), bf16[32,192,256]{2,1,0:T(8,128)(2,1)}, u32[]{:S(2)}, u32[]{:S(2)}) %all-to-all-start.3) | async-done | bytes 3145760 | tf_op jit(solution)/shard_map/all_to_all | solution.py:295
  191.1 2.3 bitcast_reduce_fusion
  193.4 0.2 slice_bitcast_fusion.1
  193.6 0.6 fusion.1
  194.2 0.6 fusion.2
  194.8 2.1 pad_maximum_fusion
  196.8 44.9 %reduce-scatter.2.cloned.1.call-done = bf16[160,1024]{1,0:T(8,128)(2,1)} async-done(((bf16[5120,1024]{1,0:T(8,128)(2,1)}), bf16[160,1024]{1,0:T(8,128)(2,1)}) %reduce-scatter.2.cloned.1.call-update) | async-done | bytes 327696 | tf_op jit(solution)/shard_map/reduce_scatter | solution.py:289
  241.7 1.9 convert_element_type.43
  (29 shorter events, 1.1 us)
Async XLA Ops:
  7.2 2.2 copy-start
  7.2 5.1 %copy-start.4 = (s32[1,192]{1,0:T(1,128)S(1)}, s32[1,192]{1,0:T(1,128)}, u32[]{:S(2)}) copy-start(s32[1,192]{1,0:T(1,128)} %param.8) | copy-start | bytes 2308
  7.2 36.5 %all-gather.2.cloned.1.call-start = ((), (), s32[]{:S(2)}) async-start(), calls=%async_computation.5 | async-start | bytes 2457600 | tf_op jit(solution)/shard_map/all_gather | solution.py:265
  16.3 48.7 %all-to-all-start.1 = ((bf16[32,192,256]{2,1,0:T(8,128)(2,1)}), bf16[32,192,256]{2,1,0:T(8,128)(2,1)}, u32[]{:S(2)}, u32[]{:S(2)}) async-start(bf16[32,192,256]{2,1,0:T(8,128)(2,1)} %bitcast.81), calls=%async_computation.1 | async-start | bytes 6291456 | tf_op jit(solution)/shard_map/all_to_all | solution.py:276
  50.5 21.0 %copy-start.2 = (s32[32]{0:T(128)S(1)}, s32[32]{0:T(128)}, u32[]{:S(2)}) copy-start(s32[32]{0:T(128)} %count_ref.1) | copy-start | bytes 388
  65.0 20.7 %all-to-all-start = ((bf16[32,48,256]{2,1,0:T(8,128)(2,1)}), bf16[32,48,256]{2,1,0:T(8,128)(2,1)S(1)}, u32[]{:S(2)}, u32[]{:S(2)}) async-start(bf16[32,48,256]{2,1,0:T(8,128)(2,1)} %bitcast.5), calls=%async_computation | async-start | bytes 1572864 | tf_op jit(solution)/shard_map/all_to_all | solution.py:282
  71.5 170.3 %reduce-scatter.2.cloned.1.call-start = ((), (), s32[]{:S(2)}) async-start(), calls=%async_computation.6 | async-start | bytes 10813440 | tf_op jit(solution)/shard_map/reduce_scatter | solution.py:289
  114.7 1.7 copy-start.1
  116.4 24.9 %copy-start.3 = (bf16[192,5120]{1,0:T(8,128)(2,1)S(1)}, bf16[192,5120]{1,0:T(8,128)(2,1)}, u32[]{:S(2)}) copy-start(bf16[192,5120]{1,0:T(8,128)(2,1)} %all-gather.2.cloned.1.call-done) | copy-start | bytes 5898244
  146.9 44.2 %all-to-all-start.3 = ((bf16[32,192,256]{2,1,0:T(8,128)(2,1)}), bf16[32,192,256]{2,1,0:T(8,128)(2,1)}, u32[]{:S(2)}, u32[]{:S(2)}) async-start(bf16[32,192,256]{2,1,0:T(8,128)(2,1)} %copy-done.1), calls=%async_computation.3 | async-start | bytes 6291456 | tf_op jit(solution)/shard_map/all_to_all | solution.py:295
Sparse Core Ops, SparseCore 0:
  10.7 32.9 all-gather.1
  147.0 94.6 reduce-scatter.1

commit v2 on v1

--- a/solution.py
+++ b/solution.py
@@ -36,7 +36,8 @@
     q_ref,
     k_ref,
     bias_ref,
-    q_out,
+    dq_out,
+    o_out,
     k_out,
     qc,
     gc,
@@ -179,7 +180,8 @@
         first = lax.rem(quarter + s, 4)
         at_k = pl.multiple_of(at_k, GROUP)
         at_q = pl.multiple_of(at_q, GROUP)
-        q_out[s] = oc[pl.ds(at_q, part_rows), :]
+        dq_out[s] = oc[pl.ds(at_q, part_rows), :DH]
+        o_out[s] = oc[pl.ds(at_q, part_rows), DH:]
         k_out[s, :, :DH] = (dkc[pl.ds(at_k, slots), :] * score_scale).astype(jnp.bfloat16)
         k_out[s, :, DH:] = dvc[pl.ds(at_k, slots), :].astype(jnp.bfloat16)
         return at_k + live * GROUP, at_q + (live - first + 3) // 4 * GROUP
@@ -204,11 +206,12 @@
     return pl.pallas_call(
         attend_kernel,
         out_shape=(
-            jax.ShapeDtypeStruct(query_in.shape, jnp.bfloat16),
+            jax.ShapeDtypeStruct((shards, part_rows, DH), jnp.bfloat16),
+            jax.ShapeDtypeStruct((shards, part_rows, DH), jnp.bfloat16),
             jax.ShapeDtypeStruct(key_in.shape, jnp.bfloat16),
         ),
         in_specs=[smem, smem, vmem, vmem, vmem],
-        out_specs=(vmem, vmem),
+        out_specs=(vmem, vmem, vmem),
         scratch_shapes=[
             pltpu.VMEM((queries + BQ, DH), jnp.bfloat16),
             pltpu.VMEM((queries + BQ, DH), jnp.bfloat16),
@@ -232,6 +235,210 @@
     )(counts, quarter, query_in, key_in, bias)
 
 
+def block_bytes_wait(ref, sem):
+    pltpu.make_async_copy(ref, ref, sem).wait()
+
+
+def greet(peers, peer_of):
+    barrier = pltpu.get_barrier_semaphore()
+
+    def signal(k, carry):
+        pl.semaphore_signal(
+            barrier, inc=1, device_id={"seq": peer_of(k)}, device_id_type=pl.DeviceIdType.MESH
+        )
+        return carry
+
+    lax.fori_loop(1, peers + 1, signal, 0)
+    pl.semaphore_wait(barrier, peers)
+
+
+def send(src, dst, send_sem, recv_sem, target):
+    copy = pltpu.make_async_remote_copy(
+        src_ref=src,
+        dst_ref=dst,
+        send_sem=send_sem,
+        recv_sem=recv_sem,
+        device_id={"seq": target},
+        device_id_type=pl.DeviceIdType.MESH,
+    )
+    copy.start()
+    return copy
+
+
+def home_kernel(
+    o_ref,
+    dq_ref,
+    k_ref,
+    g0_ref,
+    g1_ref,
+    g2_ref,
+    g3_ref,
+    dq_home,
+    gk_home,
+    gv_home,
+    wg_out,
+    oz,
+    kx,
+    ks,
+    kin,
+    part,
+    px,
+    rs,
+    rin,
+    send_sem,
+    recv_sem,
+):
+    shards, part_rows, _ = o_ref.shape
+    slots = k_ref.shape[1]
+    me = lax.axis_index("seq")
+    core = me % 2
+    sibling = me + 1 - 2 * core
+    chip = me // 2
+    chips = shards // 2
+    head = me // 4
+    quarter = me % 4
+    plane_x = chip % 4
+    out_rows = wg_out.shape[0]
+    my_rows = pl.ds(pl.multiple_of(quarter * part_rows, GROUP), part_rows)
+    my_cols = pl.ds(pl.multiple_of(head * DH, DH), DH)
+
+    greet(shards - 1, lambda k: lax.rem(me + k, shards))
+
+    def send_o(k, carry):
+        t = lax.rem(me + k, shards)
+        send(o_ref.at[t], oz.at[0, my_rows, my_cols], send_sem.at[0], recv_sem.at[0], t)
+        return carry
+
+    lax.fori_loop(1, shards, send_o, 0)
+    swap = send(k_ref.at[:, 1 - core], kx, send_sem.at[1], recv_sem.at[1], sibling)
+    oz[0, my_rows, my_cols] = o_ref[me]
+    dq_home[my_rows, my_cols] = dq_ref[me]
+    block_bytes_wait(o_ref.at[pl.ds(0, shards - 1)], recv_sem.at[0])
+
+    along_z = [
+        send(oz.at[0], oz.at[k], send_sem.at[1 + k], recv_sem.at[1 + k], lax.rem(me + 8 * k, shards))
+        for k in (1, 2, 3)
+    ]
+    swap.wait()
+
+    def send_k(k, carry):
+        t = lax.rem(chip + k, chips)
+        ks[t] = (k_ref[t, core].astype(jnp.float32) + kx[t].astype(jnp.float32)).astype(
+            jnp.bfloat16
+        )
+        send(ks.at[t], kin.at[chip], send_sem.at[5], recv_sem.at[5], 2 * t + core)
+        return carry
+
+    lax.fori_loop(1, chips, send_k, 0)
+    kin[chip] = (k_ref[chip, core].astype(jnp.float32) + kx[chip].astype(jnp.float32)).astype(
+        jnp.bfloat16
+    )
+    for copy in along_z:
+        copy.wait()
+
+    width = 256
+
+    def multiply(j, carry):
+        cols = pl.ds(pl.multiple_of(j * width, width), width)
+        total = contract_rows(g0_ref[:, cols], oz[0])
+        total += contract_rows(g1_ref[:, cols], oz[1])
+        total += contract_rows(g2_ref[:, cols], oz[2])
+        total += contract_rows(g3_ref[:, cols], oz[3])
+        part[cols, :] = total.astype(jnp.bfloat16)
+        return carry
+
+    lax.fori_loop(0, part.shape[0] // width, multiply, 0)
+
+    def piece(x, c):
+        return pl.ds(pl.multiple_of((2 * x + c) * out_rows, 32), out_rows)
+
+    swaps = [
+        send(part.at[piece(x, 1 - core)], px.at[x], send_sem.at[6 + x], recv_sem.at[6 + x], sibling)
+        for x in range(4)
+    ]
+
+    def send_dq(k, carry):
+        t = lax.rem(me + k, shards)
+        send(dq_ref.at[t], dq_home.at[my_rows, my_cols], send_sem.at[10], recv_sem.at[10], t)
+        return carry
+
+    for copy in swaps:
+        copy.wait()
+
+    def pair_sum(x):
+        return part[piece(x, core), :].astype(jnp.float32) + px[x].astype(jnp.float32)
+
+    along_x = []
+    for k in (1, 2, 3):
+        x = lax.rem(plane_x + k, 4)
+        rs[k - 1] = pair_sum(x).astype(jnp.bfloat16)
+        along_x.append(
+            send(
+                rs.at[k - 1],
+                rin.at[k - 1],
+                send_sem.at[10 + k],
+                recv_sem.at[10 + k],
+                me + 2 * (x - plane_x),
+            )
+        )
+    lax.fori_loop(1, shards, send_dq, 0)
+    wg_out[...] = pair_sum(plane_x)
+
+    block_bytes_wait(kin.at[pl.ds(0, chips - 1)], recv_sem.at[5])
+    for h in range(chips // 2):
+        pair = kin[2 * h].astype(jnp.float32) + kin[2 * h + 1].astype(jnp.float32)
+        pair = pair.astype(jnp.bfloat16)
+        gk_home[:, h * DH : (h + 1) * DH] = pair[:, :DH]
+        gv_home[:, h * DH : (h + 1) * DH] = pair[:, DH:]
+    for copy in along_x:
+        copy.wait()
+    wg_out[...] += (
+        rin[0].astype(jnp.float32) + rin[1].astype(jnp.float32) + rin[2].astype(jnp.float32)
+    )
+    block_bytes_wait(dq_ref.at[pl.ds(0, shards - 1)], recv_sem.at[10])
+    block_bytes_wait(o_ref.at[pl.ds(0, shards - 1)], send_sem.at[0])
+    block_bytes_wait(ks.at[pl.ds(0, chips - 1)], send_sem.at[5])
+    block_bytes_wait(dq_ref.at[pl.ds(0, shards - 1)], send_sem.at[10])
+
+
+def bring_home(o_back, dq_back, key_back, grad_parts, out_rows):
+    shards, part_rows, _ = o_back.shape
+    slots = key_back.shape[1]
+    chips = shards // 2
+    width = shards // 4 * DH
+    rows = grad_parts[0].shape[1]
+    key_back = key_back.reshape(chips, 2, slots, 2 * DH)
+    vmem = pl.BlockSpec(memory_space=pltpu.VMEM)
+    bf16 = jnp.bfloat16
+    return pl.pallas_call(
+        home_kernel,
+        out_shape=(
+            jax.ShapeDtypeStruct((slots, width), bf16),
+            jax.ShapeDtypeStruct((slots, width), bf16),
+            jax.ShapeDtypeStruct((slots, width), bf16),
+            jax.ShapeDtypeStruct((out_rows, width), jnp.float32),
+        ),
+        in_specs=[vmem] * 7,
+        out_specs=(vmem,) * 4,
+        scratch_shapes=[
+            pltpu.VMEM((4, slots, width), bf16),
+            pltpu.VMEM((chips, slots, 2 * DH), bf16),
+            pltpu.VMEM((chips, slots, 2 * DH), bf16),
+            pltpu.VMEM((chips, slots, 2 * DH), bf16),
+            pltpu.VMEM((rows, width), bf16),
+            pltpu.VMEM((4, out_rows, width), bf16),
+            pltpu.VMEM((3, out_rows, width), bf16),
+            pltpu.VMEM((3, out_rows, width), bf16),
+            pltpu.SemaphoreType.DMA((14,)),
+            pltpu.SemaphoreType.DMA((14,)),
+        ],
+        compiler_params=pltpu.CompilerParams(
+            collective_id=1, has_side_effects=True, vmem_limit_bytes=48 * 1024 * 1024
+        ),
+        name="home",
+    )(o_back, dq_back, key_back, *grad_parts)
+
+
 def on_device(
     projections,
     output_gradient,
@@ -281,30 +488,30 @@
     query_side = query_side.reshape(seq_count, part_rows, 2 * DH)
     query_in = lax.all_to_all(query_side, "seq", split_axis=0, concat_axis=0, tiled=True)
 
-    query_back, key_back = attend(surviving_token_count, my_quarter, query_in, key_in)
-
-    query_home = lax.all_to_all(query_back, "seq", split_axis=0, concat_axis=0, tiled=True)
-    query_home = query_home.reshape(heads_local, slots, 2 * DH)
-    attended_low = query_home[:, :, DH:].transpose(1, 0, 2).reshape(slots, group_width)
-    weight_grad = lax.psum_scatter(
-        contract_rows(grad_rows, attended_low).astype(jnp.bfloat16),
-        "seq",
-        scatter_dimension=0,
-        tiled=True,
-    ).astype(jnp.float32)
-    key_home = lax.all_to_all(key_back, "seq", split_axis=0, concat_axis=0, tiled=True)
-    key_home = jnp.sum(
-        key_home.reshape(heads_local, quarters, slots, 2 * DH).astype(jnp.float32), axis=1
-    ).astype(jnp.bfloat16)
-
-    def rows_major(part):
-        return part.transpose(1, 0, 2).reshape(slots, group_width)
-
+    blocks = grad_rows.reshape(slots, 4, -1)
+    my_z = me // 8
+
+    def along_z(k):
+        block = lax.dynamic_index_in_dim(blocks, (my_z + k) % 4, axis=1, keepdims=False)
+        if k == 0:
+            return block
+        return lax.ppermute(
+            block, "seq", [(i, (i + 8 * k) % seq_count) for i in range(seq_count)]
+        )
+
+    grad_parts = [along_z(k) for k in range(4)]
+    dq_back, o_back, key_back = attend(
+        surviving_token_count, my_quarter, query_in, key_in
+    )
+    out_rows = output_projection_weight.shape[0] // seq_count
+    grad_query, grad_key, grad_value, weight_grad = bring_home(
+        o_back, dq_back, key_back, grad_parts, out_rows
+    )
     projection_grad = jnp.stack(
         [
-            contract_rows(dealt_selector, rows_major(query_home[:, :, :DH])).astype(jnp.bfloat16),
-            contract_rows(selector, rows_major(key_home[:, :, :DH])).astype(jnp.bfloat16),
-            contract_rows(selector, rows_major(key_home[:, :, DH:])).astype(jnp.bfloat16),
+            contract_rows(dealt_selector, grad_query).astype(jnp.bfloat16),
+            contract_rows(selector, grad_key).astype(jnp.bfloat16),
+            contract_rows(selector, grad_value).astype(jnp.bfloat16),
         ],
         axis=1,
     )

time: 251 us -> 220 us (0.88)
  waiting for transfers between devices: 127 us -> 29.2 us
  Pallas kernels: 28.9 us -> 114 us
  blocking collectives: 24.5 us -> 0 us
  local copies, waits for them, and re-layouts: 5.75 us -> 20.6 us
  matrix products: 20.2 us -> 14.7 us
  other arithmetic: 9.21 us -> 4.95 us
    pallas_call x1 -> x2, Pallas kernels: 28.9 us -> 114 us  [the longest x1 76.4 us: bring_home(): pl.pallas_call(home_kernel, out_shape=(jax.ShapeDtypeStruct((slots, width...]
    reduce_scatter x1 -> x0, waiting for transfers between devices: 44.9 us -> none  [on_device(): lax.psum_scatter(contract_rows(grad_rows, attended_low).astype(jnp.bfloat...]
    all_to_all x1 -> x0, waiting for transfers between devices: 38.4 us -> none  [on_device(): lax.all_to_all(key_back, 'seq', split_axis=0, concat_axis=0, tiled=True)]
    all_to_all x1 -> x0, blocking collectives: 24.5 us -> none  [on_device(): lax.all_to_all(query_back, 'seq', split_axis=0, concat_axis=0, tiled=True)]
    all_to_all x1, waiting for transfers between devices: 13.7 us -> 0.01 us  [on_device(): lax.all_to_all(query_side, 'seq', split_axis=0, concat_axis=0, tiled=True)]
    dynamic_slice x0 -> x1, local copies, waits for them, and re-layouts: none -> 7.64 us  [along_z(): lax.dynamic_index_in_dim(blocks, (my_z + k) % 4, axis=1, keepdims=False)]
    dot_general x4 -> x3, matrix products: 7.25 us -> 1.68 us  [contract_rows(): lax.dot_general(left, right, (((0,), (0,)), ((), ())), preferred_element_...]
    ppermute x0 -> x3, starting transfers between devices: none -> 5.13 us  [along_z(): lax.ppermute(block, 'seq', [(i, (i + 8 * k) % seq_count) for i in range(s...]
  transfers between devices with their start and end apart: 5 -> 6, of which waited for: 5 -> 2; matrix products, arithmetic and copies ran while one was open for 9% -> 14% of each run, Pallas kernels for 0% -> 17%
where the time goes in v2:
time: 220 us; the launch traced here: 219 us
  Pallas kernels  114 us (52%)
  waiting for transfers between devices  29.2 us (13%)
  starting transfers between devices  21.2 us (10%)
  local copies, waits for them, and re-layouts  20.6 us (9%)
  matrix products  14.7 us (7%)
  between operations  14.4 us (7%)
  other arithmetic  4.95 us (2%)
    pallas_call x1, Pallas kernels, bring_home(): pl.pallas_call(home_kernel, out_shape=(jax.ShapeDtypeStruct((slots, width...  76.4 us
    pallas_call x1, Pallas kernels, attend(): pl.pallas_call(attend_kernel, out_shape=(jax.ShapeDtypeStruct((shards, pa...  38 us
    all_gather x1, waiting for transfers between devices, on_device(): grad_rows = lax.all_gather(grad_local, 'head', axis=1, tiled=True)  15.6 us
    all_to_all x1, waiting for transfers between devices, on_device(): lax.all_to_all(key_side, 'seq', split_axis=0, concat_axis=0, tiled=True)  13.6 us
    all_to_all x1, starting transfers between devices, on_device(): lax.all_to_all(key_side, 'seq', split_axis=0, concat_axis=0, tiled=True)  9.62 us
    dynamic_slice x1, local copies, waits for them, and re-layouts, along_z(): lax.dynamic_index_in_dim(blocks, (my_z + k) % 4, axis=1, keepdims=False)  7.64 us
    dot_general x1, matrix products, on_device(): jnp.dot(grad_rows, output_projection_weight, preferred_element_type=jnp.f...  6.78 us
    all_to_all x1, starting transfers between devices, on_device(): lax.all_to_all(query_side, 'seq', split_axis=0, concat_axis=0, tiled=True)  6.41 us
  transfers between devices with their start and end apart: 6, of which 2 were waited for; matrix products, arithmetic and copies ran while one was open for 14% of the time, Pallas kernels for 17%

profile of v2, /device:TPU:1, one launch (start us, length us, event | category | flops | bytes accessed | tf_op | source)
XLA Modules:
  0.0 219.4 jit_solution(9869366962058124429)
XLA Ops:
  7.3 0.5 broadcast.53
  7.8 1.3 reduce.4
  9.3 1.2 convolution_convert_fusion
  10.6 1.7 fusion.5
  12.3 1.6 fusion.4
  14.2 0.2 copy.27
  14.3 2.0 broadcast_in_dim.11
  16.3 9.6 %all-to-all-start.1 = ((bf16[32,192,256]{2,1,0:T(8,128)(2,1)}), bf16[32,192,256]{2,1,0:T(8,128)(2,1)}, u32[]{:S(2)}, u32[]{:S(2)}) async-start(bf16[32,192,256]{2,1,0:T(8,128)(2,1)} %bitcast.73), calls=%async_computation.1 | async-start | bytes 6291456 | tf_op jit(solution)/shard_map/all_to_all | solution.py:483
  26.2 0.1 reduce.1
  26.3 1.6 fusion.3
  28.1 15.6 %all-gather.2.cloned.1.call-done = bf16[192,5120]{1,0:T(8,128)(2,1)} async-done(((bf16[192,1280]{1,0:T(8,128)(2,1)}), bf16[192,5120]{1,0:T(8,128)(2,1)}) %all-gather.2.cloned.1.call-update) | async-done | bytes 1966096 | tf_op jit(solution)/shard_map/all_gather | solution.py:472
  43.7 6.8 %fusion.6 = bf16[24,8,8,128]{3,2,1,0:T(8,128)(2,1)S(1)} fusion(bf16[192,5120]{1,0:T(8,128)(2,1)} %all-gather.2.cloned.1.call-done, bf16[5120,1024]{1,0:T(8,128)(2,1)} %param.7), kind=kOutput, calls=%fused_computation.15 | convolution fusion | flops 2013462528 | bytes 12845056 | tf_op jit(solution)/shard_map/dot_general | solution.py:484
  50.6 1.0 pad_maximum_fusion.1
  51.6 13.6 %all-to-all-done.1.k_ref = bf16[32,192,256]{2,1,0:T(8,128)(2,1)} async-done(((bf16[32,192,256]{2,1,0:T(8,128)(2,1)}), bf16[32,192,256]{2,1,0:T(8,128)(2,1)}, u32[]{:S(2)}, u32[]{:S(2)}) %all-to-all-start.1) | async-done | bytes 3145760 | tf_op jit(solution)/shard_map/all_to_all | solution.py:483
  65.2 6.4 %all-to-all-start = ((bf16[32,48,256]{2,1,0:T(8,128)(2,1)}), bf16[32,48,256]{2,1,0:T(8,128)(2,1)S(1)}, u32[]{:S(2)}, u32[]{:S(2)}) async-start(bf16[32,48,256]{2,1,0:T(8,128)(2,1)} %bitcast.5), calls=%async_computation | async-start | bytes 1572864 | tf_op jit(solution)/shard_map/all_to_all | solution.py:489
  71.6 0.3 fusion.14
  71.9 4.7 %reshape.79 = bf16[192,4,1280]{2,1,0:T(4,128)(2,1)} reshape(bf16[192,5120]{1,0:T(8,128)(2,1)} %all-gather.2.cloned.1.call-done) | data formatting | bytes 3932160 | tf_op jit(solution)/shard_map/reshape | solution.py:491
  76.6 7.6 %constant_dynamic-slice_fusion = (bf16[192,1,1280]{2,1,0:T(2,128)(2,1)S(1)}, bf16[192,1,1280]{2,1,0:T(2,128)(2,1)S(1)}, bf16[192,1,1280]{2,1,0:T(2,128)(2,1)S(1)}, bf16[192,1,1280]{2,1,0:T(2,128)(2,1)S(1)}) fusion(bf16[192,4,1280]{2,1,0:T(4,128)(2,1)} %reshape.79, s32[]{:T(128)S(6)} %select_n.69, s32[]{:T(128)S(6)} %select_n.67, s32[]{:T(128)S(6)} %select_n.65, ...), kind=kLoop, calls=%fused_computation.49 | loop fusion | bytes 3932176 | tf_op jit(solution)/shard_map/jit(dynamic_index_in_dim)/dynamic_slice | solution.py:495
  84.2 0.8 copy.48
  85.0 0.9 copy.49
  85.9 0.8 copy.50
  86.8 1.5 collective-permute-start
  88.3 2.5 %collective-permute-start.1 = (bf16[192,1280]{1,0:T(8,128)(2,1)}, bf16[192,1280]{1,0:T(8,128)(2,1)}, u32[]{:S(2)}, u32[]{:S(2)}) collective-permute-start(bf16[192,1280]{1,0:T(8,128)(2,1)} %bitcast.62), channel_id=1, source_target_pairs={{0,64},{4,68},{8,72},{12,76},{16,80},{20,84},{24,88},{28,92},{32,9... | collective-permute-start | bytes 1474568 | tf_op jit(solution)/shard_map/ppermute | solution.py:498
  90.8 1.1 collective-permute-start.2
  91.9 38.0 %attend.1 = (bf16[32,48,128]{2,1,0:T(8,128)(2,1)S(1)}, bf16[32,48,128]{2,1,0:T(8,128)(2,1)S(1)}, bf16[32,192,256]{2,1,0:T(8,128)(2,1)S(1)}) custom-call(s32[32]{0:T(128)S(1)} %copy-done.2, s32[1]{0:T(128)} %bitcast.1.quarter_ref, bf16[32,48,256]{2,1,0:T(8,128)(2,1)S(1)} %all-to-all-done.q_ref, bf16[32,192,256]{2,1,0:T(8,128)(2,1)} %all-to-all-done.1.k_ref, ...), custom_call_target="tpu_custom_call" | custom-call | flops 7247757312 | bytes 16777216 | tf_op jit(solution)/shard_map/attend/pallas_call | solution.py:206
  130.0 1.7 copy-done.1
  131.6 76.4 %home.1 = (bf16[192,1024]{1,0:T(8,128)(2,1)S(1)}, bf16[192,1024]{1,0:T(8,128)(2,1)S(1)}, bf16[192,1024]{1,0:T(8,128)(2,1)S(1)}, f32[160,1024]{1,0:T(8,128)S(1)}) custom-call(bf16[32,48,128]{2,1,0:T(8,128)(2,1)S(1)} %get-tuple-element.9.o_ref, bf16[32,48,128]{2,1,0:T(8,128)(2,1)S(1)} %get-tuple-element.10.dq_ref, bf16[16,2,192,256]{3,2,1,0:T(8,128)(2,1)} %bitcast.70, ...), custom_call_target="tpu_custom_call" | custom-call | tf_op jit(solution)/shard_map/home/pallas_call | solution.py:413
  208.0 0.6 fusion
  208.6 0.6 fusion.1
  209.2 0.6 fusion.2
  209.7 2.0 pad_maximum_fusion
  211.7 0.8 copy.56
  (28 shorter events, 0.9 us)
Async XLA Ops:
  7.2 2.2 copy-start
  7.2 5.1 %copy-start.3 = (s32[1,192]{1,0:T(1,128)S(1)}, s32[1,192]{1,0:T(1,128)}, u32[]{:S(2)}) copy-start(s32[1,192]{1,0:T(1,128)} %param.8) | copy-start | bytes 2308
  7.2 36.5 %all-gather.2.cloned.1.call-start = ((), (), s32[]{:S(2)}) async-start(), calls=%async_computation.2 | async-start | bytes 2457600 | tf_op jit(solution)/shard_map/all_gather | solution.py:472
  16.3 9.7 %copy-start.2 = (s32[32]{0:T(128)S(1)}, s32[32]{0:T(128)}, u32[]{:S(2)}) copy-start(s32[32]{0:T(128)} %count_ref.1) | copy-start | bytes 388
  16.3 48.8 %all-to-all-start.1 = ((bf16[32,192,256]{2,1,0:T(8,128)(2,1)}), bf16[32,192,256]{2,1,0:T(8,128)(2,1)}, u32[]{:S(2)}, u32[]{:S(2)}) async-start(bf16[32,192,256]{2,1,0:T(8,128)(2,1)} %bitcast.73), calls=%async_computation.1 | async-start | bytes 6291456 | tf_op jit(solution)/shard_map/all_to_all | solution.py:483
  65.2 26.8 %all-to-all-start = ((bf16[32,48,256]{2,1,0:T(8,128)(2,1)}), bf16[32,48,256]{2,1,0:T(8,128)(2,1)S(1)}, u32[]{:S(2)}, u32[]{:S(2)}) async-start(bf16[32,48,256]{2,1,0:T(8,128)(2,1)} %bitcast.5), calls=%async_computation | async-start | bytes 1572864 | tf_op jit(solution)/shard_map/all_to_all | solution.py:489
  86.8 44.8 %collective-permute-start = (bf16[192,1280]{1,0:T(8,128)(2,1)}, bf16[192,1280]{1,0:T(8,128)(2,1)S(1)}, u32[]{:S(2)}, u32[]{:S(2)}) collective-permute-start(bf16[192,1280]{1,0:T(8,128)(2,1)} %bitcast.63), channel_id=1, source_target_pairs={{0,32},{4,36},{8,40},{12,44},{16,48},{20,52},{24,56},{28,60},{32,6... | collective-permute-start | bytes 1474568 | tf_op jit(solution)/shard_map/ppermute | solution.py:498
  88.3 43.3 %collective-permute-start.1 = (bf16[192,1280]{1,0:T(8,128)(2,1)}, bf16[192,1280]{1,0:T(8,128)(2,1)}, u32[]{:S(2)}, u32[]{:S(2)}) collective-permute-start(bf16[192,1280]{1,0:T(8,128)(2,1)} %bitcast.62), channel_id=1, source_target_pairs={{0,64},{4,68},{8,72},{12,76},{16,80},{20,84},{24,88},{28,92},{32,9... | collective-permute-start | bytes 1474568 | tf_op jit(solution)/shard_map/ppermute | solution.py:498
  90.8 40.8 %collective-permute-start.2 = (bf16[192,1280]{1,0:T(8,128)(2,1)}, bf16[192,1280]{1,0:T(8,128)(2,1)}, u32[]{:S(2)}, u32[]{:S(2)}) collective-permute-start(bf16[192,1280]{1,0:T(8,128)(2,1)} %bitcast.61), channel_id=1, source_target_pairs={{0,96},{4,100},{8,104},{12,108},{16,112},{20,116},{24,120},{28,124... | collective-permute-start | bytes 1474568 | tf_op jit(solution)/shard_map/ppermute | solution.py:498
  130.0 1.7 copy-start.1
Sparse Core Ops, SparseCore 0:
  10.7 32.9 all-gather.1

commit v3 on v2

--- a/solution.py
+++ b/solution.py
@@ -34,7 +34,9 @@
     count_ref,
     quarter_ref,
     q_ref,
+    g_ref,
     k_ref,
+    v_ref,
     bias_ref,
     dq_out,
     o_out,
@@ -66,10 +68,10 @@
         first = lax.rem(quarter + s, 4)
         at_k = pl.multiple_of(at_k, GROUP)
         at_q = pl.multiple_of(at_q, GROUP)
-        kc[pl.ds(at_k, slots), :] = k_ref[s, :, :DH]
-        vc[pl.ds(at_k, slots), :] = k_ref[s, :, DH:]
-        qc[pl.ds(at_q, part_rows), :] = q_ref[s, :, :DH]
-        gc[pl.ds(at_q, part_rows), :] = q_ref[s, :, DH:]
+        kc[pl.ds(at_k, slots), :] = k_ref[s]
+        vc[pl.ds(at_k, slots), :] = v_ref[s]
+        qc[pl.ds(at_q, part_rows), :] = q_ref[s]
+        gc[pl.ds(at_q, part_rows), :] = g_ref[s]
         rows = lax.broadcasted_iota(jnp.int32, (GROUP, DH), 0)
         for i in range(groups):
             base = at_k + (first + 4 * i) * GROUP
@@ -189,7 +191,7 @@
     lax.fori_loop(0, shards, unpack, (jnp.int32(0), jnp.int32(0)))
 
 
-def attend(counts, quarter, query_in, key_in):
+def attend(counts, quarter, query_in, grad_in, key_in, value_in):
     shards, part_rows, _ = query_in.shape
     slots = key_in.shape[1]
     keys = shards * slots
@@ -208,9 +210,9 @@
         out_shape=(
             jax.ShapeDtypeStruct((shards, part_rows, DH), jnp.bfloat16),
             jax.ShapeDtypeStruct((shards, part_rows, DH), jnp.bfloat16),
-            jax.ShapeDtypeStruct(key_in.shape, jnp.bfloat16),
+            jax.ShapeDtypeStruct((shards, slots, 2 * DH), jnp.bfloat16),
         ),
-        in_specs=[smem, smem, vmem, vmem, vmem],
+        in_specs=[smem, smem, vmem, vmem, vmem, vmem, vmem],
         out_specs=(vmem, vmem, vmem),
         scratch_shapes=[
             pltpu.VMEM((queries + BQ, DH), jnp.bfloat16),
@@ -232,14 +234,14 @@
             flops=6 * queries * keys * DH, bytes_accessed=16 * 1024 * 1024, transcendentals=0
         ),
         name="attend",
-    )(counts, quarter, query_in, key_in, bias)
+    )(counts, quarter, query_in, grad_in, key_in, value_in, bias)
 
 
 def block_bytes_wait(ref, sem):
     pltpu.make_async_copy(ref, ref, sem).wait()
 
 
-def greet(peers, peer_of):
+def greet(peers, peer_of, ring=0):
     barrier = pltpu.get_barrier_semaphore()
 
     def signal(k, carry):
@@ -249,20 +251,222 @@
         return carry
 
     lax.fori_loop(1, peers + 1, signal, 0)
+    if ring:
+        row = lax.axis_index("head")
+        for k in range(1, ring):
+            pl.semaphore_signal(
+                barrier,
+                inc=1,
+                device_id={"head": lax.rem(row + k, ring)},
+                device_id_type=pl.DeviceIdType.MESH,
+            )
+        peers = peers + ring - 1
     pl.semaphore_wait(barrier, peers)
 
 
-def send(src, dst, send_sem, recv_sem, target):
+def send(src, dst, send_sem, recv_sem, target, axis="seq"):
     copy = pltpu.make_async_remote_copy(
         src_ref=src,
         dst_ref=dst,
         send_sem=send_sem,
         recv_sem=recv_sem,
-        device_id={"seq": target},
+        device_id={axis: target},
         device_id_type=pl.DeviceIdType.MESH,
     )
     copy.start()
     return copy
+
+
+def spread_kernel(
+    grad_ref,
+    q_ref,
+    k_ref,
+    v_ref,
+    w_hbm,
+    gblk,
+    q_in,
+    g_in,
+    k_in,
+    v_in,
+    w_ref,
+    acc,
+    g_local,
+    w_sem,
+    y_send,
+    y_recv,
+    kv_send,
+    kv_recv,
+    pass_send,
+    pass_recv,
+    q_send,
+    q_recv,
+):
+    shards, part_rows, _ = q_in.shape
+    slots, cols = grad_ref.shape
+    half = cols // 2
+    me = lax.axis_index("seq")
+    row = lax.axis_index("head")
+    core = me % 2
+    sibling = me + 1 - 2 * core
+    chip = me // 2
+    chips = shards // 2
+    my_z = me // 8
+    my_head = me // 4
+    my_rows = pl.ds(pl.multiple_of((me % 4) * part_rows, GROUP), part_rows)
+
+    load_w = pltpu.make_async_copy(w_hbm, w_ref, w_sem)
+    load_w.start()
+    greet(shards - 1, lambda k: lax.rem(me + k, shards), 4)
+
+    def head_cols(head):
+        return pl.ds(pl.multiple_of(head * DH, DH), DH)
+
+    def slot_of(y):
+        return lax.rem(y - my_z + 4, 4)
+
+    right, left, across = lax.rem(row + 1, 4), lax.rem(row + 3, 4), lax.rem(row + 2, 4)
+    to_right = send(grad_ref, gblk.at[slot_of(row)], y_send.at[0], y_recv.at[0], right, "head")
+    to_left = send(grad_ref, gblk.at[slot_of(row)], y_send.at[1], y_recv.at[1], left, "head")
+
+    def send_kv(k, carry):
+        t = lax.rem(chip + k, chips)
+        source = head_cols(t // 2)
+        target = 2 * t + core
+        send(k_ref.at[:, source], k_in.at[me], kv_send.at[0], kv_recv.at[k], target)
+        send(v_ref.at[:, source], v_in.at[me], kv_send.at[1], kv_recv.at[chips + k], target)
+        return carry
+
+    lax.fori_loop(1, chips, send_kv, 0)
+    own = head_cols(my_head)
+    send(k_ref.at[:, own], k_in.at[me], pass_send.at[0], pass_recv.at[0], sibling)
+    send(v_ref.at[:, own], v_in.at[me], pass_send.at[1], pass_recv.at[1], sibling)
+    k_in[me] = k_ref[:, own]
+    v_in[me] = v_ref[:, own]
+
+    def send_q(k, carry):
+        t = lax.rem(me + k, shards)
+        rows = pl.ds(pl.multiple_of((t % 4) * part_rows, GROUP), part_rows)
+        send(q_ref.at[rows, head_cols(t // 4)], q_in.at[me], q_send.at[0], q_recv.at[0], t)
+        return carry
+
+    lax.fori_loop(1, shards, send_q, 0)
+    q_in[me] = q_ref[my_rows, own]
+
+    width = 256
+    tiles = acc.shape[1] // width
+    gblk[slot_of(row)] = grad_ref[...]
+    load_w.wait()
+
+    def multiply(y, first):
+        def tile(j, carry):
+            at = pl.ds(pl.multiple_of(j * width, width), width)
+            rows = pl.ds(pl.multiple_of(y * cols, width), cols)
+            part = jnp.dot(gblk[slot_of(y)], w_ref[rows, at], preferred_element_type=jnp.float32)
+            acc[:, at] = part if first else acc[:, at] + part
+            return carry
+
+        lax.fori_loop(0, tiles, tile, 0)
+
+    multiply(row, True)
+    to_right.wait_recv()
+    from_left = gblk.at[slot_of(left), :, pl.ds(0, half)]
+    on_right = send(from_left, from_left, y_send.at[2], y_recv.at[2], right, "head")
+    to_left.wait_recv()
+    from_right = gblk.at[slot_of(right), :, pl.ds(half, half)]
+    on_left = send(from_right, from_right, y_send.at[3], y_recv.at[3], left, "head")
+    multiply(left, False)
+    multiply(right, False)
+
+    def pass_on(k, carry):
+        s = 2 * lax.rem(chip - k + chips, chips) + core
+        block_bytes_wait(k_in.at[s], kv_recv.at[k])
+        send(k_in.at[s], k_in.at[s], pass_send.at[0], pass_recv.at[0], sibling)
+        block_bytes_wait(v_in.at[s], kv_recv.at[chips + k])
+        send(v_in.at[s], v_in.at[s], pass_send.at[1], pass_recv.at[1], sibling)
+        return carry
+
+    lax.fori_loop(1, chips, pass_on, 0)
+    on_right.wait_recv()
+    on_left.wait_recv()
+
+    def finish(step, carry):
+        j = lax.rem(my_head // 2 + step, tiles)
+        at = pl.ds(pl.multiple_of(j * width, width), width)
+        rows = pl.ds(pl.multiple_of(across * cols, width), cols)
+        part = jnp.dot(gblk[slot_of(across)], w_ref[rows, at], preferred_element_type=jnp.float32)
+        g_local[:, at] = (acc[:, at] + part).astype(jnp.bfloat16)
+        for i in range(8):
+            t = j * 8 + i
+            part_at = (i % 4) * part_rows
+
+            @pl.when(t != me)
+            def _():
+                send(
+                    g_local.at[pl.ds(part_at, part_rows), head_cols(t // 4)],
+                    g_in.at[me],
+                    q_send.at[1],
+                    q_recv.at[1],
+                    t,
+                )
+
+        return carry
+
+    lax.fori_loop(0, tiles, finish, 0)
+    g_in[me] = g_local[my_rows, own]
+
+    others = pl.ds(0, shards - 1)
+    block_bytes_wait(q_in.at[others], q_recv.at[0])
+    block_bytes_wait(q_in.at[others], q_send.at[0])
+    passed = pl.ds(0, chips)
+    block_bytes_wait(k_in.at[passed], pass_recv.at[0])
+    block_bytes_wait(v_in.at[passed], pass_recv.at[1])
+    block_bytes_wait(k_in.at[passed], pass_send.at[0])
+    block_bytes_wait(v_in.at[passed], pass_send.at[1])
+    sent = pl.ds(0, chips - 1)
+    block_bytes_wait(k_in.at[sent], kv_send.at[0])
+    block_bytes_wait(v_in.at[sent], kv_send.at[1])
+    for copy in (to_right, to_left, on_right, on_left):
+        copy.wait_send()
+    block_bytes_wait(g_in.at[others], q_recv.at[1])
+    block_bytes_wait(g_in.at[others], q_send.at[1])
+
+
+def spread(grad_local, query, key, value, weight, shards):
+    slots, cols = grad_local.shape
+    depth, width = weight.shape
+    part_rows = slots // 4
+    bf16 = jnp.bfloat16
+    vmem = pl.BlockSpec(memory_space=pltpu.VMEM)
+    return pl.pallas_call(
+        spread_kernel,
+        out_shape=(
+            jax.ShapeDtypeStruct((4, slots, cols), bf16),
+            jax.ShapeDtypeStruct((shards, part_rows, DH), bf16),
+            jax.ShapeDtypeStruct((shards, part_rows, DH), bf16),
+            jax.ShapeDtypeStruct((shards, slots, DH), bf16),
+            jax.ShapeDtypeStruct((shards, slots, DH), bf16),
+        ),
+        in_specs=[vmem] * 4 + [pl.BlockSpec(memory_space=pl.ANY)],
+        out_specs=(vmem,) * 5,
+        scratch_shapes=[
+            pltpu.VMEM((depth, width), bf16),
+            pltpu.VMEM((slots, width), jnp.float32),
+            pltpu.VMEM((slots, width), bf16),
+            pltpu.SemaphoreType.DMA,
+            pltpu.SemaphoreType.DMA((4,)),
+            pltpu.SemaphoreType.DMA((4,)),
+            pltpu.SemaphoreType.DMA((2,)),
+            pltpu.SemaphoreType.DMA((shards,)),
+            pltpu.SemaphoreType.DMA((2,)),
+            pltpu.SemaphoreType.DMA((2,)),
+            pltpu.SemaphoreType.DMA((2,)),
+            pltpu.SemaphoreType.DMA((2,)),
+        ],
+        compiler_params=pltpu.CompilerParams(
+            collective_id=2, has_side_effects=True, vmem_limit_bytes=48 * 1024 * 1024
+        ),
+        name="spread",
+    )(grad_local, query, key, value, weight)
 
 
 def home_kernel(
@@ -469,39 +673,24 @@
         return jnp.dot(which, values, preferred_element_type=jnp.float32).astype(jnp.bfloat16)
 
     grad_local = pick(dealt_selector, output_gradient)
-    grad_rows = lax.all_gather(grad_local, "head", axis=1, tiled=True)
     query = pick(dealt_selector, projections[:, 0])
     key = pick(selector, projections[:, 1])
     value = pick(selector, projections[:, 2])
 
-    def head_major(matrix):
-        return matrix.reshape(slots, heads_local, DH).transpose(1, 0, 2)
-
-    key_side = jnp.concatenate([head_major(key), head_major(value)], axis=2)
-    key_side = jnp.broadcast_to(key_side[:, None], (heads_local, quarters, slots, 2 * DH))
-    key_side = key_side.reshape(seq_count, slots, 2 * DH)
-    key_in = lax.all_to_all(key_side, "seq", split_axis=0, concat_axis=0, tiled=True)
-    grad_attn = jnp.dot(
-        grad_rows, output_projection_weight, preferred_element_type=jnp.float32
-    ).astype(jnp.bfloat16)
-    query_side = jnp.concatenate([head_major(query), head_major(grad_attn)], axis=2)
-    query_side = query_side.reshape(seq_count, part_rows, 2 * DH)
-    query_in = lax.all_to_all(query_side, "seq", split_axis=0, concat_axis=0, tiled=True)
-
-    blocks = grad_rows.reshape(slots, 4, -1)
-    my_z = me // 8
+    blocks, query_in, grad_in, key_in, value_in = spread(
+        grad_local, query, key, value, output_projection_weight, seq_count
+    )
 
     def along_z(k):
-        block = lax.dynamic_index_in_dim(blocks, (my_z + k) % 4, axis=1, keepdims=False)
         if k == 0:
-            return block
+            return blocks[0]
         return lax.ppermute(
-            block, "seq", [(i, (i + 8 * k) % seq_count) for i in range(seq_count)]
+            blocks[k], "seq", [(i, (i + 8 * k) % seq_count) for i in range(seq_count)]
         )
 
     grad_parts = [along_z(k) for k in range(4)]
     dq_back, o_back, key_back = attend(
-        surviving_token_count, my_quarter, query_in, key_in
+        surviving_token_count, my_quarter, query_in, grad_in, key_in, value_in
     )
     out_rows = output_projection_weight.shape[0] // seq_count
     grad_query, grad_key, grad_value, weight_grad = bring_home(

time: 220 us -> 180 us (0.82)
  Pallas kernels: 114 us -> 155 us
  waiting for transfers between devices: 29.2 us -> 0.01 us
  starting transfers between devices: 21.2 us -> 2.45 us
  between operations: 14.4 us -> 0.82 us
  local copies, waits for them, and re-layouts: 20.6 us -> 10.5 us
  matrix products: 14.7 us -> 7.2 us
    pallas_call x0 -> x1, Pallas kernels: none -> 41.3 us  [spread(): pl.pallas_call(spread_kernel, out_shape=(jax.ShapeDtypeStruct((4, slots,...]
    all_to_all x2 -> x0, starting transfers between devices: 16 us -> none  [the longest x1 9.62 us: on_device(): lax.all_to_all(key_side, 'seq', split_axis=0, concat_axis=0, tiled=True)]
    all_gather x1 -> x0, waiting for transfers between devices: 15.6 us -> none  [on_device(): grad_rows = lax.all_gather(grad_local, 'head', axis=1, tiled=True)]
    all_to_all x2 -> x0, waiting for transfers between devices: 13.6 us -> none  [the longest x1 13.6 us: on_device(): lax.all_to_all(key_side, 'seq', split_axis=0, concat_axis=0, tiled=True)]
    dynamic_slice x1 -> x0, local copies, waits for them, and re-layouts: 7.64 us -> none  [along_z(): lax.dynamic_index_in_dim(blocks, (my_z + k) % 4, axis=1, keepdims=False)]
    dot_general x1 -> x0, matrix products: 6.78 us -> none  [on_device(): jnp.dot(grad_rows, output_projection_weight, preferred_element_type=jnp.f...]
    reshape x3 -> x0, local copies, waits for them, and re-layouts: 4.81 us -> none  [the longest x1 4.67 us: on_device(): blocks = grad_rows.reshape(slots, 4, -1)]
    squeeze x0 -> x1, local copies, waits for them, and re-layouts: none -> 4.01 us  [along_z(): blocks[k]]
  transfers between devices with their start and end apart: 6 -> 3, of which waited for: 2 -> 0; matrix products, arithmetic and copies ran while one was open for 14% -> 0% of each run, Pallas kernels for 17% -> 21%
where the time goes in v3:
time: 180 us; the launch traced here: 179 us
  Pallas kernels  155 us (86%)
  local copies, waits for them, and re-layouts  10.5 us (6%)
  matrix products  7.2 us (4%)
  other arithmetic  3.18 us (2%)
  starting transfers between devices  2.45 us (1%)
    pallas_call x1, Pallas kernels, bring_home(): pl.pallas_call(home_kernel, out_shape=(jax.ShapeDtypeStruct((slots, width...  76.1 us
    pallas_call x1, Pallas kernels, spread(): pl.pallas_call(spread_kernel, out_shape=(jax.ShapeDtypeStruct((4, slots,...  41.3 us
    pallas_call x1, Pallas kernels, attend(): pl.pallas_call(attend_kernel, out_shape=(jax.ShapeDtypeStruct((shards, pa...  37.7 us
    unnamed x24, local copies, waits for them, and re-layouts  6.19 us
    dot_general x4, matrix products, pick(): jnp.dot(which, values, preferred_element_type=jnp.float32)  5.52 us
    squeeze x1, local copies, waits for them, and re-layouts, along_z(): blocks[k]  4.01 us
  transfers between devices with their start and end apart: 3, of which 0 were waited for; matrix products, arithmetic and copies ran while one was open for 0% of the time, Pallas kernels for 21%

profile of v3, /device:TPU:1, one launch (start us, length us, event | category | flops | bytes accessed | tf_op | source)
XLA Modules:
  0.0 179.3 jit_solution(11763045008234033119)
XLA Ops:
  0.6 0.0 copy-start
  0.6 0.0 copy-start.10
  0.7 1.8 convolution_convert_fusion.4.v_ref
  2.4 1.7 convolution_convert_fusion.5.k_ref
  4.1 0.5 broadcast.47
  4.6 0.7 reduce.4
  5.3 0.1 reshape_squeeze.3
  5.4 0.1 eq.33
  5.5 1.6 convolution_convert_fusion.6.q_ref
  7.2 0.5 convolution_convert_fusion.grad_ref
  7.6 41.3 %spread.1 = (bf16[4,192,1280]{2,1,0:T(8,128)(2,1)}, bf16[32,48,128]{2,1,0:T(8,128)(2,1)S(1)}, bf16[32,48,128]{2,1,0:T(8,128)(2,1)S(1)}, bf16[32,192,128]{2,1,0:T(8,128)(2,1)S(1)}, bf16[32,192,128]{2,1,0:T(8,128)(2,1)S(1)}) custom-call(bf16[192,1280]{1,0:T(8,128)(2,1)S(1)} %convolution_convert_fusion.grad_ref, ...), custom_call_target="tpu_custom_call" | custom-call | tf_op jit(solution)/shard_map/spread/pallas_call | solution.py:440
  49.0 0.0 copy-start.2
  49.0 0.0 copy-start.1
  49.0 4.0 %slice_bitcast_fusion = (bf16[192,1280]{1,0:T(8,128)(2,1)}, bf16[192,1280]{1,0:T(8,128)(2,1)}, bf16[192,1280]{1,0:T(8,128)(2,1)}, bf16[192,1280]{1,0:T(8,128)(2,1)S(1)}) fusion(bf16[4,192,1280]{2,1,0:T(8,128)(2,1)} %get-tuple-element.21), kind=kLoop, calls=%fused_computation.21 | loop fusion | bytes 3932160 | tf_op jit(solution)/shard_map/squeeze | solution.py:688
  53.0 1.8 %collective-permute-start.2 = (bf16[192,1280]{1,0:T(8,128)(2,1)}, bf16[192,1280]{1,0:T(8,128)(2,1)S(1)}, u32[]{:S(2)}, u32[]{:S(2)}) collective-permute-start(bf16[192,1280]{1,0:T(8,128)(2,1)} %get-tuple-element.28), channel_id=1, source_target_pairs={{0,96},{4,100},{8,104},{12,108},{16,112},{20,116},{24,120},{28,124... | collective-permute-start | bytes 1474568 | tf_op jit(solution)/shard_map/ppermute | solution.py:687
  54.9 0.1 collective-permute-start.1
  55.0 0.5 collective-permute-start
  55.5 0.1 copy.11
  55.6 0.1 reduce-window.9
  55.7 0.1 reduce.1
  55.8 0.3 fusion.10
  56.1 1.4 copy-done.3
  57.5 1.4 copy-done.5
  58.9 1.0 copy-done.7
  59.9 1.0 copy-done.9
  60.9 37.7 %attend.1 = (bf16[32,48,128]{2,1,0:T(8,128)(2,1)S(1)}, bf16[32,48,128]{2,1,0:T(8,128)(2,1)S(1)}, bf16[32,192,256]{2,1,0:T(8,128)(2,1)}) custom-call(s32[32]{0:T(128)S(1)} %copy-done.1, s32[1]{0:T(128)} %bitcast.1.quarter_ref, bf16[32,48,128]{2,1,0:T(8,128)(2,1)S(1)} %copy-done.7, bf16[32,48,128]{2,1,0:T(8,128)(2,1)S(1)} %copy-done.9, ...), custom_call_target="tpu_custom_call" | custom-call | flops 7247757312 | bytes 16777216 | tf_op jit(solution)/shard_map/attend/pallas_call | solution.py:208
  98.6 76.1 %home.1 = (bf16[192,1024]{1,0:T(8,128)(2,1)S(1)}, bf16[192,1024]{1,0:T(8,128)(2,1)S(1)}, bf16[192,1024]{1,0:T(8,128)(2,1)S(1)}, f32[160,1024]{1,0:T(8,128)S(1)}) custom-call(bf16[32,48,128]{2,1,0:T(8,128)(2,1)S(1)} %get-tuple-element.18.o_ref, bf16[32,48,128]{2,1,0:T(8,128)(2,1)S(1)} %get-tuple-element.19.dq_ref, bf16[16,2,192,256]{3,2,1,0:T(8,128)(2,1)} %bitcast.37, ...), custom_call_target="tpu_custom_call" | custom-call | tf_op jit(solution)/shard_map/home/pallas_call | solution.py:617
  174.7 0.6 fusion
  175.3 0.6 fusion.1
  175.9 0.6 fusion.2
  176.4 2.0 %pad_maximum_fusion = bf16[512,3,1024]{2,0,1:T(8,128)(2,1)} fusion(bf16[512,1,1024]{2,0,1:T(8,128)(2,1)S(1)} %fusion.2, bf16[512,1,1024]{2,0,1:T(8,128)(2,1)S(1)} %fusion.1, bf16[512,1,1024]{2,0,1:T(8,128)(2,1)S(1)} %fusion), kind=kLoop, calls=%fused_computation | loop fusion | flops 3145728 | bytes 6291456 | tf_op jit(solution)/shard_map/stack | solution.py:699
  178.4 0.8 copy.15
  (22 shorter events, 0.1 us)
Async XLA Ops:
  0.6 6.5 %copy-start = (bf16[512,1280]{1,0:T(8,128)(2,1)S(1)}, bf16[512,1280]{1,0:T(8,128)(2,1)}, u32[]{:S(2)}) copy-start(bf16[512,1280]{1,0:T(8,128)(2,1)} %param.6) | copy-start | bytes 3932164
  0.6 4.0 %copy-start.10 = (s32[1,192]{1,0:T(1,128)S(1)}, s32[1,192]{1,0:T(1,128)}, u32[]{:S(2)}) copy-start(s32[1,192]{1,0:T(1,128)} %param.8) | copy-start | bytes 2308
  49.0 6.0 %copy-start.2 = (bf16[32,192,128]{2,1,0:T(8,128)(2,1)}, bf16[32,192,128]{2,1,0:T(8,128)(2,1)S(1)}, u32[]{:S(2)}) copy-start(bf16[32,192,128]{2,1,0:T(8,128)(2,1)S(1)} %get-tuple-element.16.k_ref) | copy-start | bytes 4718596
  49.0 6.0 %copy-start.4 = (bf16[32,192,128]{2,1,0:T(8,128)(2,1)}, bf16[32,192,128]{2,1,0:T(8,128)(2,1)S(1)}, u32[]{:S(2)}) copy-start(bf16[32,192,128]{2,1,0:T(8,128)(2,1)S(1)} %get-tuple-element.17.v_ref) | copy-start | bytes 4718596
  49.0 6.5 %copy-start.6 = (bf16[32,48,128]{2,1,0:T(8,128)(2,1)}, bf16[32,48,128]{2,1,0:T(8,128)(2,1)S(1)}, u32[]{:S(2)}) copy-start(bf16[32,48,128]{2,1,0:T(8,128)(2,1)S(1)} %get-tuple-element.14.q_ref) | copy-start | bytes 1179652
  49.0 6.5 %copy-start.8 = (bf16[32,48,128]{2,1,0:T(8,128)(2,1)}, bf16[32,48,128]{2,1,0:T(8,128)(2,1)S(1)}, u32[]{:S(2)}) copy-start(bf16[32,48,128]{2,1,0:T(8,128)(2,1)S(1)} %get-tuple-element.15.g_ref) | copy-start | bytes 1179652
  49.0 6.5 %copy-start.1 = (s32[32]{0:T(128)S(1)}, s32[32]{0:T(128)}, u32[]{:S(2)}) copy-start(s32[32]{0:T(128)} %count_ref.1) | copy-start | bytes 388
  53.0 45.6 %collective-permute-start.2 = (bf16[192,1280]{1,0:T(8,128)(2,1)}, bf16[192,1280]{1,0:T(8,128)(2,1)S(1)}, u32[]{:S(2)}, u32[]{:S(2)}) collective-permute-start(bf16[192,1280]{1,0:T(8,128)(2,1)} %get-tuple-element.28), channel_id=1, source_target_pairs={{0,96},{4,100},{8,104},{12,108},{16,112},{20,116},{24,120},{28,124... | collective-permute-start | bytes 1474568 | tf_op jit(solution)/shard_map/ppermute | solution.py:687
  54.9 43.7 %collective-permute-start.1 = (bf16[192,1280]{1,0:T(8,128)(2,1)}, bf16[192,1280]{1,0:T(8,128)(2,1)S(1)}, u32[]{:S(2)}, u32[]{:S(2)}) collective-permute-start(bf16[192,1280]{1,0:T(8,128)(2,1)} %get-tuple-element.29), channel_id=1, source_target_pairs={{0,64},{4,68},{8,72},{12,76},{16,80},{20,84},{24,88},{28,92},{32,9... | collective-permute-start | bytes 1474568 | tf_op jit(solution)/shard_map/ppermute | solution.py:687
  55.0 43.6 %collective-permute-start = (bf16[192,1280]{1,0:T(8,128)(2,1)}, bf16[192,1280]{1,0:T(8,128)(2,1)S(1)}, u32[]{:S(2)}, u32[]{:S(2)}) collective-permute-start(bf16[192,1280]{1,0:T(8,128)(2,1)} %get-tuple-element.30), channel_id=1, source_target_pairs={{0,32},{4,36},{8,40},{12,44},{16,48},{20,52},{24,56},{28,60},{32,6... | collective-permute-start | bytes 1474568 | tf_op jit(solution)/shard_map/ppermute | solution.py:687
  56.1 1.4 copy-start.3
  57.5 1.4 copy-start.5
  58.9 1.0 copy-start.7
  59.9 1.0 copy-start.9

commit v4 on v3

--- a/solution.py
+++ b/solution.py
@@ -9,7 +9,7 @@
 
 DH = 128
 BQ = 256
-BK = 512
+BK = 1536
 GROUP = 16
 NEG = -1e30
 
@@ -20,40 +20,36 @@
     )
 
 
-def contract_cols(left, right):
-    return lax.dot_general(
-        left, right, (((1,), (1,)), ((), ())), preferred_element_type=jnp.float32
-    )
-
-
-def wide(column, width):
-    return jnp.concatenate([column] * (width // DH), axis=1)
-
-
 def attend_kernel(
     count_ref,
     quarter_ref,
+    q_hbm,
+    g_hbm,
+    k_hbm,
+    v_hbm,
+    dq_out,
+    o_out,
+    k_out,
     q_ref,
     g_ref,
     k_ref,
     v_ref,
-    bias_ref,
-    dq_out,
-    o_out,
-    k_out,
     qc,
     gc,
     kc,
     vc,
+    k_turned,
+    v_turned,
+    q_turned,
     dkc,
     dvc,
     oc,
     s_scr,
+    p_scr,
     qpos,
-    peak,
-    total,
     acc,
     group_pos,
+    load_sem,
 ):
     shards, part_rows, _ = q_ref.shape
     slots = k_ref.shape[1]
@@ -61,6 +57,33 @@
     groups = part_rows // GROUP
     score_scale = 1.0 / math.sqrt(DH)
     log2e = score_scale * math.log2(math.e)
+    bf16 = jnp.bfloat16
+    loads = [
+        pltpu.make_async_copy(src, dst, load_sem.at[i])
+        for i, (src, dst) in enumerate(
+            ((q_hbm, q_ref), (g_hbm, g_ref), (k_hbm, k_ref), (v_hbm, v_ref))
+        )
+    ]
+    for load in loads:
+        load.start()
+
+    def clear(i, carry):
+        rows = pl.ds(pl.multiple_of(i * slots, slots), slots)
+        dkc[rows, :] = jnp.zeros((slots, DH), jnp.float32)
+        dvc[rows, :] = jnp.zeros((slots, DH), jnp.float32)
+        return carry
+
+    lax.fori_loop(0, shards, clear, 0)
+    q_turned[DH:, :] = jnp.where(
+        lax.broadcasted_iota(jnp.int32, (DH, BQ), 0) == 0, 1.0, 0.0
+    ).astype(bf16)
+    for load in loads:
+        load.wait()
+
+    def dead_marks(rows, live):
+        row = lax.broadcasted_iota(jnp.int32, (rows, DH), 0)
+        lane = lax.broadcasted_iota(jnp.int32, (rows, DH), 1)
+        return jnp.where((row >= live) & (lane == 0), NEG, 0.0).astype(bf16)
 
     def pack(s, carry):
         at_k, at_q = carry
@@ -68,7 +91,8 @@
         first = lax.rem(quarter + s, 4)
         at_k = pl.multiple_of(at_k, GROUP)
         at_q = pl.multiple_of(at_q, GROUP)
-        kc[pl.ds(at_k, slots), :] = k_ref[s]
+        kc[pl.ds(at_k, slots), :DH] = k_ref[s]
+        kc[pl.ds(at_k, slots), DH:] = dead_marks(slots, count_ref[s])
         vc[pl.ds(at_k, slots), :] = v_ref[s]
         qc[pl.ds(at_q, part_rows), :] = q_ref[s]
         gc[pl.ds(at_q, part_rows), :] = g_ref[s]
@@ -82,96 +106,77 @@
     end_k, end_q = lax.fori_loop(0, shards, pack, (jnp.int32(0), jnp.int32(0)))
     end_k = pl.multiple_of(end_k, GROUP)
     end_q = pl.multiple_of(end_q, GROUP)
-    kc[pl.ds(end_k, BK), :] = jnp.zeros((BK, DH), jnp.bfloat16)
-    vc[pl.ds(end_k, BK), :] = jnp.zeros((BK, DH), jnp.bfloat16)
-    qc[pl.ds(end_q, BQ), :] = jnp.zeros((BQ, DH), jnp.bfloat16)
-    gc[pl.ds(end_q, BQ), :] = jnp.zeros((BQ, DH), jnp.bfloat16)
+    kc[pl.ds(end_k, BK), :DH] = jnp.zeros((BK, DH), bf16)
+    kc[pl.ds(end_k, BK), DH:] = dead_marks(BK, 0)
+    vc[pl.ds(end_k, BK), :] = jnp.zeros((BK, DH), bf16)
+    qc[pl.ds(end_q, BQ), :] = jnp.zeros((BQ, DH), bf16)
+    gc[pl.ds(end_q, BQ), :] = jnp.zeros((BQ, DH), bf16)
     qpos[pl.ds(end_q, BQ), :] = jnp.zeros((BQ, DH), jnp.int32)
     blocks = (end_q + BQ - 1) // BQ
     oc[pl.ds(pl.multiple_of(blocks * BQ, BQ), part_rows), :] = jnp.zeros(
-        (part_rows, 2 * DH), jnp.bfloat16
-    )
-
-    def clear(i, carry):
-        rows = pl.ds(pl.multiple_of(i * slots, slots), slots)
-        dkc[rows, :] = jnp.zeros((slots, DH), jnp.float32)
-        dvc[rows, :] = jnp.zeros((slots, DH), jnp.float32)
-        return carry
-
-    lax.fori_loop(0, shards, clear, 0)
+        (part_rows, 2 * DH), bf16
+    )
+
+    def turn(c, carry):
+        keys = pl.ds(pl.multiple_of(c * BK, BK), BK)
+        k_turned[:, keys] = kc[keys, :DH].T
+        v_turned[:, keys] = vc[keys, :].T
+        return carry
+
+    lax.fori_loop(0, (end_k + BK - 1) // BK, turn, 0)
 
     def block(b, carry):
         rows = pl.ds(pl.multiple_of(b * BQ, BQ), BQ)
         last_group = jnp.minimum((b + 1) * (BQ // GROUP), end_q // GROUP) - 1
         chunks = (group_pos[last_group] + GROUP + BK - 1) // BK
         clear_chunks = (group_pos[b * (BQ // GROUP)] + 1) // BK
-
-        def score(c, masked):
+        q_turned[:DH, :] = qc[rows, :].T
+        last_key = qpos[rows, :].T[0:1, :]
+
+        def score(c, top, masked):
             at = pl.multiple_of(c * BK, BK)
             keys = pl.ds(at, BK)
-            s = contract_cols(qc[rows, :], kc[keys, :]) + bias_ref[:, keys]
+            s = jnp.dot(kc[keys, :], q_turned[...], preferred_element_type=jnp.float32)
             if masked:
-                column = at + lax.broadcasted_iota(jnp.int32, (BQ, BK), 1)
-                s = jnp.where(column <= wide(qpos[rows, :], BK), s, NEG)
-            s_scr[:, keys] = s
-            top = peak[...]
-            for i in range(BK // DH):
-                top = jnp.maximum(top, s[:, i * DH : (i + 1) * DH])
-            peak[...] = top
-
-        peak[...] = jnp.full((BQ, DH), NEG, jnp.float32)
-
-        def score_clear(c, carry):
-            score(c, False)
-            return carry
-
-        def score_masked(c, carry):
-            score(c, True)
-            return carry
-
-        lax.fori_loop(0, clear_chunks, score_clear, 0)
-        lax.fori_loop(clear_chunks, chunks, score_masked, 0)
-        peak[...] = jnp.broadcast_to(jnp.max(peak[...], axis=1, keepdims=True), (BQ, DH))
-        total[...] = jnp.zeros((BQ, DH), jnp.float32)
-        acc[...] = jnp.zeros((BQ, DH), jnp.float32)
-
-        def weigh(c, carry):
+                key = at + lax.broadcasted_iota(jnp.int32, (BK, BQ), 0)
+                s = jnp.where(key <= last_key, s, NEG)
+            s_scr[keys, :] = s
+            return jnp.maximum(top, jnp.max(s, axis=0, keepdims=True))
+
+        top = jnp.full((1, BQ), NEG, jnp.float32)
+        top = lax.fori_loop(0, clear_chunks, lambda c, t: score(c, t, False), top)
+        top = lax.fori_loop(clear_chunks, chunks, lambda c, t: score(c, t, True), top)
+        acc[...] = jnp.zeros((DH, BQ), jnp.float32)
+
+        def weigh(c, total):
             keys = pl.ds(pl.multiple_of(c * BK, BK), BK)
-            p = jnp.exp2((s_scr[:, keys] - wide(peak[...], BK)) * log2e)
-            s_scr[:, keys] = p
-            add = total[...]
-            for i in range(BK // DH):
-                add = add + p[:, i * DH : (i + 1) * DH]
-            total[...] = add
-            acc[...] += jnp.dot(
-                p.astype(jnp.bfloat16), vc[keys, :], preferred_element_type=jnp.float32
-            )
-            return carry
-
-        lax.fori_loop(0, chunks, weigh, 0)
-        inverse = 1.0 / jnp.broadcast_to(
-            jnp.sum(total[...], axis=1, keepdims=True), (BQ, DH)
-        )
-        total[...] = inverse
+            p = jnp.exp2((s_scr[keys, :] - top) * log2e)
+            p_low = p.astype(bf16)
+            p_scr[keys, :] = p_low
+            acc[...] += jnp.dot(v_turned[:, keys], p_low, preferred_element_type=jnp.float32)
+            return total + jnp.sum(p, axis=0, keepdims=True)
+
+        total = lax.fori_loop(0, chunks, weigh, jnp.zeros((1, BQ), jnp.float32))
+        inverse = 1.0 / total
         attended = acc[...] * inverse
-        oc[rows, DH:] = attended.astype(jnp.bfloat16)
-        peak[...] = jnp.broadcast_to(
-            jnp.sum(gc[rows, :].astype(jnp.float32) * attended, axis=1, keepdims=True), (BQ, DH)
-        )
-        acc[...] = jnp.zeros((BQ, DH), jnp.float32)
+        oc[rows, DH:] = attended.T.astype(bf16)
+        g_turned = (gc[rows, :].astype(jnp.float32).T * inverse).astype(bf16)
+        row_dot = jnp.sum(g_turned.astype(jnp.float32) * attended, axis=0, keepdims=True)
+        g_part = g_turned.T
+        acc[...] = jnp.zeros((DH, BQ), jnp.float32)
 
         def back(c, carry):
             keys = pl.ds(pl.multiple_of(c * BK, BK), BK)
-            p = s_scr[:, keys] * wide(total[...], BK)
-            grad_probs = contract_cols(gc[rows, :], vc[keys, :])
-            ds = (p * (grad_probs - wide(peak[...], BK))).astype(jnp.bfloat16)
-            acc[...] += jnp.dot(ds, kc[keys, :], preferred_element_type=jnp.float32)
-            dkc[keys, :] += contract_rows(ds, qc[rows, :])
-            dvc[keys, :] += contract_rows(p.astype(jnp.bfloat16), gc[rows, :])
+            p_low = p_scr[keys, :]
+            grad_probs = jnp.dot(vc[keys, :], g_turned, preferred_element_type=jnp.float32)
+            ds = (p_low.astype(jnp.float32) * (grad_probs - row_dot)).astype(bf16)
+            acc[...] += jnp.dot(k_turned[:, keys], ds, preferred_element_type=jnp.float32)
+            dkc[keys, :] += jnp.dot(ds, qc[rows, :], preferred_element_type=jnp.float32)
+            dvc[keys, :] += jnp.dot(p_low, g_part, preferred_element_type=jnp.float32)
             return carry
 
         lax.fori_loop(0, chunks, back, 0)
-        oc[rows, :DH] = (acc[...] * score_scale).astype(jnp.bfloat16)
+        oc[rows, :DH] = (acc[...] * score_scale).T.astype(bf16)
         return carry
 
     lax.fori_loop(0, blocks, block, 0)
@@ -184,8 +189,8 @@
         at_q = pl.multiple_of(at_q, GROUP)
         dq_out[s] = oc[pl.ds(at_q, part_rows), :DH]
         o_out[s] = oc[pl.ds(at_q, part_rows), DH:]
-        k_out[s, :, :DH] = (dkc[pl.ds(at_k, slots), :] * score_scale).astype(jnp.bfloat16)
-        k_out[s, :, DH:] = dvc[pl.ds(at_k, slots), :].astype(jnp.bfloat16)
+        k_out[s, :, :DH] = (dkc[pl.ds(at_k, slots), :] * score_scale).astype(bf16)
+        k_out[s, :, DH:] = dvc[pl.ds(at_k, slots), :].astype(bf16)
         return at_k + live * GROUP, at_q + (live - first + 3) // 4 * GROUP
 
     lax.fori_loop(0, shards, unpack, (jnp.int32(0), jnp.int32(0)))
@@ -196,45 +201,47 @@
     slots = key_in.shape[1]
     keys = shards * slots
     queries = shards * part_rows
-    rounded = (counts + GROUP - 1) // GROUP * GROUP
-    start = jnp.cumsum(rounded) - rounded
-    place = jnp.arange(keys, dtype=jnp.int32)[None, :]
-    live = jnp.any(
-        (place >= start[:, None]) & (place < (start + counts)[:, None]), axis=0, keepdims=True
-    )
-    bias = jnp.where(live, 0.0, NEG).astype(jnp.float32)
+    bf16 = jnp.bfloat16
     vmem = pl.BlockSpec(memory_space=pltpu.VMEM)
     smem = pl.BlockSpec(memory_space=pltpu.SMEM)
+    hbm = pl.BlockSpec(memory_space=pl.ANY)
     return pl.pallas_call(
         attend_kernel,
         out_shape=(
-            jax.ShapeDtypeStruct((shards, part_rows, DH), jnp.bfloat16),
-            jax.ShapeDtypeStruct((shards, part_rows, DH), jnp.bfloat16),
-            jax.ShapeDtypeStruct((shards, slots, 2 * DH), jnp.bfloat16),
+            jax.ShapeDtypeStruct((shards, part_rows, DH), bf16),
+            jax.ShapeDtypeStruct((shards, part_rows, DH), bf16),
+            jax.ShapeDtypeStruct((shards, slots, 2 * DH), bf16),
         ),
-        in_specs=[smem, smem, vmem, vmem, vmem, vmem, vmem],
+        in_specs=[smem, smem, hbm, hbm, hbm, hbm],
         out_specs=(vmem, vmem, vmem),
         scratch_shapes=[
-            pltpu.VMEM((queries + BQ, DH), jnp.bfloat16),
-            pltpu.VMEM((queries + BQ, DH), jnp.bfloat16),
-            pltpu.VMEM((keys + BK, DH), jnp.bfloat16),
-            pltpu.VMEM((keys + BK, DH), jnp.bfloat16),
+            pltpu.VMEM((shards, part_rows, DH), bf16),
+            pltpu.VMEM((shards, part_rows, DH), bf16),
+            pltpu.VMEM((shards, slots, DH), bf16),
+            pltpu.VMEM((shards, slots, DH), bf16),
+            pltpu.VMEM((queries + BQ, DH), bf16),
+            pltpu.VMEM((queries + BQ, DH), bf16),
+            pltpu.VMEM((keys + BK, 2 * DH), bf16),
+            pltpu.VMEM((keys + BK, DH), bf16),
+            pltpu.VMEM((DH, keys), bf16),
+            pltpu.VMEM((DH, keys), bf16),
+            pltpu.VMEM((2 * DH, BQ), bf16),
             pltpu.VMEM((keys, DH), jnp.float32),
             pltpu.VMEM((keys, DH), jnp.float32),
-            pltpu.VMEM((queries + BQ, 2 * DH), jnp.bfloat16),
-            pltpu.VMEM((BQ, keys), jnp.float32),
+            pltpu.VMEM((queries + BQ, 2 * DH), bf16),
+            pltpu.VMEM((keys, BQ), jnp.float32),
+            pltpu.VMEM((keys, BQ), bf16),
             pltpu.VMEM((queries + BQ, DH), jnp.int32),
-            pltpu.VMEM((BQ, DH), jnp.float32),
-            pltpu.VMEM((BQ, DH), jnp.float32),
-            pltpu.VMEM((BQ, DH), jnp.float32),
+            pltpu.VMEM((DH, BQ), jnp.float32),
             pltpu.SMEM((queries // GROUP + 8,), jnp.int32),
+            pltpu.SemaphoreType.DMA((4,)),
         ],
-        compiler_params=pltpu.CompilerParams(vmem_limit_bytes=48 * 1024 * 1024),
+        compiler_params=pltpu.CompilerParams(vmem_limit_bytes=52 * 1024 * 1024),
         cost_estimate=pl.CostEstimate(
             flops=6 * queries * keys * DH, bytes_accessed=16 * 1024 * 1024, transcendentals=0
         ),
         name="attend",
-    )(counts, quarter, query_in, grad_in, key_in, value_in, bias)
+    )(counts, quarter, query_in, grad_in, key_in, value_in)
 
 
 def block_bytes_wait(ref, sem):
@@ -283,7 +290,10 @@
     k_ref,
     v_ref,
     w_hbm,
-    gblk,
+    g0_out,
+    g1_out,
+    g2_out,
+    g3_out,
     q_in,
     g_in,
     k_in,
@@ -291,7 +301,9 @@
     w_ref,
     acc,
     g_local,
+    gblk,
     w_sem,
+    copy_sem,
     y_send,
     y_recv,
     kv_send,
@@ -413,6 +425,14 @@
 
     lax.fori_loop(0, tiles, finish, 0)
     g_in[me] = g_local[my_rows, own]
+    copies = [
+        pltpu.make_async_copy(gblk.at[k], out, copy_sem.at[k])
+        for k, out in enumerate((g0_out, g1_out, g2_out, g3_out))
+    ]
+    for copy in copies:
+        copy.start()
+    for copy in copies:
+        copy.wait()
 
     others = pl.ds(0, shards - 1)
     block_bytes_wait(q_in.at[others], q_recv.at[0])
@@ -440,19 +460,24 @@
     return pl.pallas_call(
         spread_kernel,
         out_shape=(
-            jax.ShapeDtypeStruct((4, slots, cols), bf16),
+            jax.ShapeDtypeStruct((slots, cols), bf16),
+            jax.ShapeDtypeStruct((slots, cols), bf16),
+            jax.ShapeDtypeStruct((slots, cols), bf16),
+            jax.ShapeDtypeStruct((slots, cols), bf16),
             jax.ShapeDtypeStruct((shards, part_rows, DH), bf16),
             jax.ShapeDtypeStruct((shards, part_rows, DH), bf16),
             jax.ShapeDtypeStruct((shards, slots, DH), bf16),
             jax.ShapeDtypeStruct((shards, slots, DH), bf16),
         ),
         in_specs=[vmem] * 4 + [pl.BlockSpec(memory_space=pl.ANY)],
-        out_specs=(vmem,) * 5,
+        out_specs=(pl.BlockSpec(memory_space=pl.ANY),) * 4 + (vmem,) * 4,
         scratch_shapes=[
             pltpu.VMEM((depth, width), bf16),
             pltpu.VMEM((slots, width), jnp.float32),
             pltpu.VMEM((slots, width), bf16),
+            pltpu.VMEM((4, slots, cols), bf16),
             pltpu.SemaphoreType.DMA,
+            pltpu.SemaphoreType.DMA((4,)),
             pltpu.SemaphoreType.DMA((4,)),
             pltpu.SemaphoreType.DMA((4,)),
             pltpu.SemaphoreType.DMA((2,)),
@@ -677,7 +702,7 @@
     key = pick(selector, projections[:, 1])
     value = pick(selector, projections[:, 2])
 
-    blocks, query_in, grad_in, key_in, value_in = spread(
+    *blocks, query_in, grad_in, key_in, value_in = spread(
         grad_local, query, key, value, output_projection_weight, seq_count
     )
 

time: 180 us -> 165 us (0.917)
  local copies, waits for them, and re-layouts: 10.5 us -> 2.7 us
  Pallas kernels: 155 us -> 148 us
    pallas_call x1, Pallas kernels: 37.7 us -> 32.3 us  [attend(): pl.pallas_call(attend_kernel, out_shape=(jax.ShapeDtypeStruct((shards, pa...]
    squeeze x1 -> x0, local copies, waits for them, and re-layouts: 4.01 us -> none  [along_z(): blocks[k]]
    unnamed x24 -> x10, local copies, waits for them, and re-layouts: 6.19 us -> 2.52 us
    pallas_call x1, Pallas kernels: 76.1 us -> 74.1 us  [bring_home(): pl.pallas_call(home_kernel, out_shape=(jax.ShapeDtypeStruct((slots, width...]
  transfers between devices with their start and end apart: 3 -> 3, of which waited for: 0 -> 0; matrix products, arithmetic and copies ran while one was open for 0% -> 0% of each run, Pallas kernels for 21% -> 20%
where the time goes in v4:
time: 165 us
  Pallas kernels  148 us (90%)
  matrix products  7.2 us (4%)
  starting transfers between devices  3.66 us (2%)
  local copies, waits for them, and re-layouts  2.7 us (2%)
  other arithmetic  2.69 us (2%)
    pallas_call x1, Pallas kernels, bring_home(): pl.pallas_call(home_kernel, out_shape=(jax.ShapeDtypeStruct((slots, width...  74.1 us
    pallas_call x1, Pallas kernels, spread(): pl.pallas_call(spread_kernel, out_shape=(jax.ShapeDtypeStruct((slots, col...  41.2 us
    pallas_call x1, Pallas kernels, attend(): pl.pallas_call(attend_kernel, out_shape=(jax.ShapeDtypeStruct((shards, pa...  32.3 us
    dot_general x4, matrix products, pick(): jnp.dot(which, values, preferred_element_type=jnp.float32)  5.52 us
    ppermute x3, starting transfers between devices, along_z(): lax.ppermute(blocks[k], 'seq', [(i, (i + 8 * k) % seq_count) for i in ran...  3.66 us
  transfers between devices with their start and end apart: 3, of which 0 were waited for; matrix products, arithmetic and copies ran while one was open for 0% of the time, Pallas kernels for 20%

profile of v4, /device:TPU:1, one launch (start us, length us, event | category | flops | bytes accessed | tf_op | source)
XLA Modules:
  0.0 164.7 jit_solution(4336406119925795088)
XLA Ops:
  0.6 0.0 copy-start
  0.6 0.0 copy-start.3
  0.7 1.8 %convolution_convert_fusion.4.v_ref = bf16[192,1024]{1,0:T(8,128)(2,1)S(1)} fusion(bf16[512,3,1024]{2,0,1:T(8,128)(2,1)} %param.5, s32[192]{0:T(256)} %bitcast.27), kind=kOutput, calls=%fused_computation.8 | convolution fusion | flops 201621504 | bytes 1442816 | tf_op jit(solution)/shard_map/dot_general | solution.py:698
  2.4 1.7 %convolution_convert_fusion.5.k_ref = bf16[192,1024]{1,0:T(8,128)(2,1)S(1)} fusion(bf16[512,3,1024]{2,0,1:T(8,128)(2,1)} %param.5, s32[192]{0:T(256)} %bitcast.28), kind=kOutput, calls=%fused_computation.9 | convolution fusion | flops 201621504 | bytes 1442816 | tf_op jit(solution)/shard_map/dot_general | solution.py:698
  4.1 0.5 broadcast.4
  4.6 0.0 copy-done.3
  4.6 0.7 reduce.3
  5.3 0.1 reshape_squeeze.3
  5.4 0.1 eq.33
  5.5 1.6 convolution_convert_fusion.6.q_ref
  7.1 0.0 copy-done
  7.2 0.5 convolution_convert_fusion.grad_ref
  7.6 0.0 copy-start.2
  7.6 41.2 %spread.1 = (bf16[192,1280]{1,0:T(8,128)(2,1)S(1)}, bf16[192,1280]{1,0:T(8,128)(2,1)S(1)}, bf16[192,1280]{1,0:T(8,128)(2,1)S(1)}, bf16[192,1280]{1,0:T(8,128)(2,...) custom-call(bf16[192,1280]{1,0:T(8,128)(2,1)S(1)} %convolution_conve, ...), custom_call_target="tpu_custom_call" | custom-call | tf_op jit(solution)/shard_map/spread/pallas_call | solution.py:460
  48.8 0.0 copy-start.1
  48.9 1.1 copy-done.1
  50.0 0.2 collective-permute-start
  50.2 2.8 %collective-permute-start.1 = (bf16[192,1280]{1,0:T(8,128)(2,1)S(1)}, bf16[192,1280]{1,0:T(8,128)(2,1)S(1)}, u32[]{:S(2)}, u32[]{:S(2)}) collective-permute-start(bf16[192,1280]{1,0:T(8,128)(2,1)S(1)} %get-tuple-element.26), channel_id=1, source_target_pairs={{0,64},{4,68},{8,72},{12,76},{16,80},{20,84},{24,88},{28,92},{32,9... | collective-permute-start | bytes 1474568 | tf_op jit(solution)/shard_map/ppermute | solution.py:712
  53.0 0.6 collective-permute-start.2
  53.7 0.0 copy-done.2
  53.7 32.3 %attend.1 = (bf16[32,48,128]{2,1,0:T(8,128)(2,1)S(1)}, bf16[32,48,128]{2,1,0:T(8,128)(2,1)S(1)}, bf16[32,192,256]{2,1,0:T(8,128)(2,1)}) custom-call(s32[32]{0:T(128)S(1)} %copy-done.2, s32[1]{0:T(128)} %bitcast.1.quarter_ref, bf16[32,48,128]{2,1,0:T(8,128)(2,1)S(1)} %get-tuple-element.17.q_hbm, bf16[32,48,128]{2,1,0:T(8,128)(2,1)S(1)} %get-tuple-element.18.g_hbm, ...), custom_call_target="tpu_custom_call" | custom-call | flops 7247757312 | bytes 16777216 | tf_op jit(solution)/shard_map/attend/pallas_call | solution.py:208
  86.0 0.0 collective-permute-done.g1_ref
  86.0 0.0 collective-permute-done.1.g2_ref
  86.0 0.0 collective-permute-done.2.g3_ref
  86.0 74.1 %home.1 = (bf16[192,1024]{1,0:T(8,128)(2,1)S(1)}, bf16[192,1024]{1,0:T(8,128)(2,1)S(1)}, bf16[192,1024]{1,0:T(8,128)(2,1)S(1)}, f32[160,1024]{1,0:T(8,128)S(1)}) custom-call(bf16[32,48,128]{2,1,0:T(8,128)(2,1)S(1)} %get-tuple-element.21.o_ref, bf16[32,48,128]{2,1,0:T(8,128)(2,1)S(1)} %get-tuple-element.22.dq_ref, bf16[16,2,192,256]{3,2,1,0:T(8,128)(2,1)} %bitcast.25, ...), custom_call_target="tpu_custom_call" | custom-call | tf_op jit(solution)/shard_map/home/pallas_call | solution.py:642
  160.2 0.6 fusion
  160.7 0.6 fusion.1
  161.3 0.6 fusion.2
  161.9 2.0 %pad_maximum_fusion = bf16[512,3,1024]{2,0,1:T(8,128)(2,1)} fusion(bf16[512,1,1024]{2,0,1:T(8,128)(2,1)S(1)} %fusion.2, bf16[512,1,1024]{2,0,1:T(8,128)(2,1)S(1)} %fusion.1, bf16[512,1,1024]{2,0,1:T(8,128)(2,1)S(1)} %fusion), kind=kLoop, calls=%fused_computation | loop fusion | flops 3145728 | bytes 6291456 | tf_op jit(solution)/shard_map/stack | solution.py:724
  163.9 0.8 copy.11
  (2 shorter events, 0.0 us)
Async XLA Ops:
  0.6 6.5 %copy-start = (bf16[512,1280]{1,0:T(8,128)(2,1)S(1)}, bf16[512,1280]{1,0:T(8,128)(2,1)}, u32[]{:S(2)}) copy-start(bf16[512,1280]{1,0:T(8,128)(2,1)} %param.6) | copy-start | bytes 3932164
  0.6 4.0 %copy-start.3 = (s32[1,192]{1,0:T(1,128)S(1)}, s32[1,192]{1,0:T(1,128)}, u32[]{:S(2)}) copy-start(s32[1,192]{1,0:T(1,128)} %param.8) | copy-start | bytes 2308
  7.6 46.0 %copy-start.2 = (s32[32]{0:T(128)S(1)}, s32[32]{0:T(128)}, u32[]{:S(2)}) copy-start(s32[32]{0:T(128)} %count_ref.1) | copy-start | bytes 388
  48.8 1.2 copy-start.1
  50.0 36.0 %collective-permute-start = (bf16[192,1280]{1,0:T(8,128)(2,1)S(1)}, bf16[192,1280]{1,0:T(8,128)(2,1)S(1)}, u32[]{:S(2)}, u32[]{:S(2)}) collective-permute-start(bf16[192,1280]{1,0:T(8,128)(2,1)S(1)} %get-tuple-element.25), channel_id=1, source_target_pairs={{0,32},{4,36},{8,40},{12,44},{16,48},{20,52},{24,56},{28,60},{32,6... | collective-permute-start | bytes 1474568 | tf_op jit(solution)/shard_map/ppermute | solution.py:712
  50.2 35.8 %collective-permute-start.1 = (bf16[192,1280]{1,0:T(8,128)(2,1)S(1)}, bf16[192,1280]{1,0:T(8,128)(2,1)S(1)}, u32[]{:S(2)}, u32[]{:S(2)}) collective-permute-start(bf16[192,1280]{1,0:T(8,128)(2,1)S(1)} %get-tuple-element.26), channel_id=1, source_target_pairs={{0,64},{4,68},{8,72},{12,76},{16,80},{20,84},{24,88},{28,92},{32,9... | collective-permute-start | bytes 1474568 | tf_op jit(solution)/shard_map/ppermute | solution.py:712
  53.0 33.0 %collective-permute-start.2 = (bf16[192,1280]{1,0:T(8,128)(2,1)S(1)}, bf16[192,1280]{1,0:T(8,128)(2,1)S(1)}, u32[]{:S(2)}, u32[]{:S(2)}) collective-permute-start(bf16[192,1280]{1,0:T(8,128)(2,1)S(1)} %get-tuple-element.27), channel_id=1, source_target_pairs={{0,96},{4,100},{8,104},{12,108},{16,112},{20,116},{24,120},{28,124... | collective-permute-start | bytes 1474568 | tf_op jit(solution)/shard_map/ppermute | solution.py:712

commit v5 on v4

--- a/solution.py
+++ b/solution.py
@@ -12,6 +12,9 @@
 BK = 1536
 GROUP = 16
 NEG = -1e30
+CHUNKS = 4
+K_STEP = 4
+DQ_STEP = 4
 
 
 def contract_rows(left, right):
@@ -506,30 +509,41 @@
     gk_home,
     gv_home,
     wg_out,
+    g_turned,
     oz,
     kx,
     ks,
-    kin,
+    k_row,
+    k_pair,
+    k_col,
     part,
     px,
-    rs,
-    rin,
+    half_send,
+    half_recv,
+    full_send,
+    full_recv,
     send_sem,
     recv_sem,
+    k_send,
+    k_recv,
+    z_send,
+    z_recv,
+    p_send,
+    p_recv,
+    x_send,
+    x_recv,
 ):
     shards, part_rows, _ = o_ref.shape
-    slots = k_ref.shape[1]
+    slots = k_ref.shape[3]
     me = lax.axis_index("seq")
     core = me % 2
     sibling = me + 1 - 2 * core
-    chip = me // 2
-    chips = shards // 2
-    head = me // 4
-    quarter = me % 4
-    plane_x = chip % 4
-    out_rows = wg_out.shape[0]
-    my_rows = pl.ds(pl.multiple_of(quarter * part_rows, GROUP), part_rows)
-    my_cols = pl.ds(pl.multiple_of(head * DH, DH), DH)
+    plane_x = me // 2 % 4
+    my_z = me // 8
+    out_rows, width = wg_out.shape
+    my_rows = pl.ds(pl.multiple_of((me % 4) * part_rows, GROUP), part_rows)
+    my_cols = pl.ds(pl.multiple_of((me // 4) * DH, DH), DH)
+    f32, bf16 = jnp.float32, jnp.bfloat16
 
     greet(shards - 1, lambda k: lax.rem(me + k, shards))
 
@@ -539,104 +553,213 @@
         return carry
 
     lax.fori_loop(1, shards, send_o, 0)
-    swap = send(k_ref.at[:, 1 - core], kx, send_sem.at[1], recv_sem.at[1], sibling)
+    swap = send(k_ref.at[:, :, 1 - core], kx, send_sem.at[1], recv_sem.at[1], sibling)
     oz[0, my_rows, my_cols] = o_ref[me]
     dq_home[my_rows, my_cols] = dq_ref[me]
+
+    tile = 256
+
+    def turn(j, carry):
+        cols = pl.ds(pl.multiple_of(j * tile, tile), tile)
+        for k, g_ref in enumerate((g0_ref, g1_ref, g2_ref, g3_ref)):
+            g_turned[k, cols, :] = g_ref[:, cols].T
+        return carry
+
+    lax.fori_loop(0, part.shape[0] // tile, turn, 0)
     block_bytes_wait(o_ref.at[pl.ds(0, shards - 1)], recv_sem.at[0])
 
-    along_z = [
-        send(oz.at[0], oz.at[k], send_sem.at[1 + k], recv_sem.at[1 + k], lax.rem(me + 8 * k, shards))
-        for k in (1, 2, 3)
-    ]
-    swap.wait()
-
-    def send_k(k, carry):
-        t = lax.rem(chip + k, chips)
-        ks[t] = (k_ref[t, core].astype(jnp.float32) + kx[t].astype(jnp.float32)).astype(
-            jnp.bfloat16
-        )
-        send(ks.at[t], kin.at[chip], send_sem.at[5], recv_sem.at[5], 2 * t + core)
-        return carry
-
-    lax.fori_loop(1, chips, send_k, 0)
-    kin[chip] = (k_ref[chip, core].astype(jnp.float32) + kx[chip].astype(jnp.float32)).astype(
-        jnp.bfloat16
-    )
-    for copy in along_z:
-        copy.wait()
-
-    width = 256
-
-    def multiply(j, carry):
-        cols = pl.ds(pl.multiple_of(j * width, width), width)
-        total = contract_rows(g0_ref[:, cols], oz[0])
-        total += contract_rows(g1_ref[:, cols], oz[1])
-        total += contract_rows(g2_ref[:, cols], oz[2])
-        total += contract_rows(g3_ref[:, cols], oz[3])
-        part[cols, :] = total.astype(jnp.bfloat16)
-        return carry
-
-    lax.fori_loop(0, part.shape[0] // width, multiply, 0)
+    chunk = width // CHUNKS
+    z_up, z_down = lax.rem(me + 8, shards), lax.rem(me + 24, shards)
+    x_up = me + 2 * (lax.rem(plane_x + 1, 4) - plane_x)
+    x_down = me + 2 * (lax.rem(plane_x + 3, 4) - plane_x)
+    upper, lower = pl.ds(0, slots // 2), pl.ds(slots // 2, slots // 2)
+    top, bottom = pl.ds(0, out_rows // 2), pl.ds(out_rows // 2, out_rows // 2)
+
+    def cols_of(c):
+        return pl.ds(c * chunk, chunk)
+
+    def start_z(c):
+        own = oz.at[0, :, cols_of(c)]
+        send(own, oz.at[1, :, cols_of(c)], z_send.at[0], z_recv.at[0, c], z_up)
+        send(own, oz.at[3, :, cols_of(c)], z_send.at[1], z_recv.at[1, c], z_down)
+
+    def forward_z(c):
+        cols = cols_of(c)
+        block_bytes_wait(oz.at[1, :, cols], z_recv.at[0, c])
+        send(
+            oz.at[1, upper, cols], oz.at[2, upper, cols], z_send.at[2], z_recv.at[2, c], z_up
+        )
+        block_bytes_wait(oz.at[3, :, cols], z_recv.at[1, c])
+        send(
+            oz.at[3, lower, cols], oz.at[2, lower, cols], z_send.at[3], z_recv.at[3, c], z_down
+        )
+        if c + 2 < CHUNKS:
+            start_z(c + 2)
 
     def piece(x, c):
         return pl.ds(pl.multiple_of((2 * x + c) * out_rows, 32), out_rows)
 
-    swaps = [
-        send(part.at[piece(x, 1 - core)], px.at[x], send_sem.at[6 + x], recv_sem.at[6 + x], sibling)
-        for x in range(4)
-    ]
+    def product(c):
+        cols = cols_of(c)
+        block_bytes_wait(oz.at[2, upper, cols], z_recv.at[2, c])
+        block_bytes_wait(oz.at[2, lower, cols], z_recv.at[3, c])
+
+        def rows_tile(j, carry):
+            rows = pl.ds(pl.multiple_of(j * tile, tile), tile)
+            total = jnp.dot(g_turned[0, rows, :], oz[0, :, cols], preferred_element_type=f32)
+            for k in (1, 2, 3):
+                total += jnp.dot(g_turned[k, rows, :], oz[k, :, cols], preferred_element_type=f32)
+            part[rows, cols] = total.astype(bf16)
+            return carry
+
+        lax.fori_loop(0, part.shape[0] // tile, rows_tile, 0)
+        for x in range(4):
+            send(
+                part.at[piece(x, 1 - core), cols],
+                px.at[x, :, cols],
+                p_send,
+                p_recv.at[c],
+                sibling,
+            )
+
+    def pair_sum(x, c):
+        cols = cols_of(c)
+        return part[piece(x, core), cols].astype(f32) + px[x, :, cols].astype(f32)
+
+    def send_half(c):
+        cols = cols_of(c)
+        block_bytes_wait(px.at[:, :, cols], p_recv.at[c])
+        half_send[:, cols] = pair_sum(lax.rem(plane_x + 2, 4), c).astype(bf16)
+        send(
+            half_send.at[top, cols], half_recv.at[top, cols], x_send.at[0], x_recv.at[0, c], x_up
+        )
+        send(
+            half_send.at[bottom, cols],
+            half_recv.at[bottom, cols],
+            x_send.at[1],
+            x_recv.at[1, c],
+            x_down,
+        )
+
+    def send_full(c):
+        cols = cols_of(c)
+        split = out_rows // 2
+        block_bytes_wait(half_recv.at[top, cols], x_recv.at[0, c])
+        ahead = pair_sum(lax.rem(plane_x + 1, 4), c)
+        full_send[0, top, cols] = (ahead[:split] + half_recv[top, cols].astype(f32)).astype(bf16)
+        full_send[0, bottom, cols] = ahead[split:].astype(bf16)
+        send(
+            full_send.at[0, :, cols], full_recv.at[0, :, cols], x_send.at[2], x_recv.at[2, c], x_up
+        )
+        block_bytes_wait(half_recv.at[bottom, cols], x_recv.at[1, c])
+        behind = pair_sum(lax.rem(plane_x + 3, 4), c)
+        full_send[1, top, cols] = behind[:split].astype(bf16)
+        full_send[1, bottom, cols] = (behind[split:] + half_recv[bottom, cols].astype(f32)).astype(
+            bf16
+        )
+        send(
+            full_send.at[1, :, cols],
+            full_recv.at[1, :, cols],
+            x_send.at[3],
+            x_recv.at[3, c],
+            x_down,
+        )
+
+    def finish(c):
+        cols = cols_of(c)
+        block_bytes_wait(full_recv.at[0, :, cols], x_recv.at[2, c])
+        block_bytes_wait(full_recv.at[1, :, cols], x_recv.at[3, c])
+        wg_out[:, cols] = (
+            pair_sum(plane_x, c)
+            + full_recv[0, :, cols].astype(f32)
+            + full_recv[1, :, cols].astype(f32)
+        )
+
+    def k_sum(z, x):
+        return (k_ref[z, x, core].astype(f32) + kx[z, x].astype(f32)).astype(bf16)
+
+    def k_along_x():
+        for k in (1, 2, 3):
+            x = lax.rem(plane_x + k, 4)
+            for z in range(4):
+                ks[z, x] = k_sum(z, x)
+            send(
+                ks.at[:, x],
+                k_row.at[plane_x],
+                k_send.at[k - 1],
+                k_recv.at[k - 1],
+                me + 2 * (x - plane_x),
+            )
+        for z in range(4):
+            k_row[plane_x, z] = k_sum(z, plane_x)
+
+    def k_along_z():
+        for k in range(3):
+            block_bytes_wait(k_row.at[0], k_recv.at[k])
+        for k in (1, 2, 3, 0):
+            z = lax.rem(my_z + k, 4)
+            for h in range(2):
+                pair = k_row[2 * h, z].astype(f32) + k_row[2 * h + 1, z].astype(f32)
+                k_pair[z, h] = pair.astype(bf16)
+            if k:
+                send(
+                    k_pair.at[z],
+                    k_col.at[my_z],
+                    k_send.at[2 + k],
+                    k_recv.at[2 + k],
+                    lax.rem(me + 8 * k, shards),
+                )
+            else:
+                k_col[my_z] = k_pair[z]
 
     def send_dq(k, carry):
         t = lax.rem(me + k, shards)
-        send(dq_ref.at[t], dq_home.at[my_rows, my_cols], send_sem.at[10], recv_sem.at[10], t)
-        return carry
-
-    for copy in swaps:
-        copy.wait()
-
-    def pair_sum(x):
-        return part[piece(x, core), :].astype(jnp.float32) + px[x].astype(jnp.float32)
-
-    along_x = []
-    for k in (1, 2, 3):
-        x = lax.rem(plane_x + k, 4)
-        rs[k - 1] = pair_sum(x).astype(jnp.bfloat16)
-        along_x.append(
-            send(
-                rs.at[k - 1],
-                rin.at[k - 1],
-                send_sem.at[10 + k],
-                recv_sem.at[10 + k],
-                me + 2 * (x - plane_x),
-            )
-        )
-    lax.fori_loop(1, shards, send_dq, 0)
-    wg_out[...] = pair_sum(plane_x)
-
-    block_bytes_wait(kin.at[pl.ds(0, chips - 1)], recv_sem.at[5])
-    for h in range(chips // 2):
-        pair = kin[2 * h].astype(jnp.float32) + kin[2 * h + 1].astype(jnp.float32)
-        pair = pair.astype(jnp.bfloat16)
-        gk_home[:, h * DH : (h + 1) * DH] = pair[:, :DH]
-        gv_home[:, h * DH : (h + 1) * DH] = pair[:, DH:]
-    for copy in along_x:
-        copy.wait()
-    wg_out[...] += (
-        rin[0].astype(jnp.float32) + rin[1].astype(jnp.float32) + rin[2].astype(jnp.float32)
-    )
-    block_bytes_wait(dq_ref.at[pl.ds(0, shards - 1)], recv_sem.at[10])
+        send(dq_ref.at[t], dq_home.at[my_rows, my_cols], send_sem.at[3], recv_sem.at[3], t)
+        return carry
+
+    start_z(0)
+    start_z(1)
+    swap.wait()
+    k_along_x()
+    stages = (forward_z, product, send_half, send_full, finish)
+    for step in range(CHUNKS + len(stages) - 1):
+        if step == K_STEP:
+            k_along_z()
+        if step == DQ_STEP:
+            lax.fori_loop(1, shards, send_dq, 0)
+        for i, stage in enumerate(stages):
+            if 0 <= step - i < CHUNKS:
+                stage(step - i)
+    for k in range(3):
+        block_bytes_wait(k_col.at[0], k_recv.at[3 + k])
+    for z in range(4):
+        for h in range(2):
+            cols = pl.ds((2 * z + h) * DH, DH)
+            gk_home[:, cols] = k_col[z, h, :, :DH]
+            gv_home[:, cols] = k_col[z, h, :, DH:]
+    block_bytes_wait(dq_ref.at[pl.ds(0, shards - 1)], recv_sem.at[3])
     block_bytes_wait(o_ref.at[pl.ds(0, shards - 1)], send_sem.at[0])
-    block_bytes_wait(ks.at[pl.ds(0, chips - 1)], send_sem.at[5])
-    block_bytes_wait(dq_ref.at[pl.ds(0, shards - 1)], send_sem.at[10])
+    for k in range(3):
+        block_bytes_wait(ks.at[:, 0], k_send.at[k])
+        block_bytes_wait(k_pair.at[0], k_send.at[3 + k])
+    block_bytes_wait(dq_ref.at[pl.ds(0, shards - 1)], send_sem.at[3])
+    block_bytes_wait(oz.at[0], z_send.at[0])
+    block_bytes_wait(oz.at[0], z_send.at[1])
+    block_bytes_wait(oz.at[1, upper], z_send.at[2])
+    block_bytes_wait(oz.at[3, lower], z_send.at[3])
+    block_bytes_wait(px, p_send)
+    block_bytes_wait(half_send.at[top], x_send.at[0])
+    block_bytes_wait(half_send.at[bottom], x_send.at[1])
+    block_bytes_wait(full_send.at[0], x_send.at[2])
+    block_bytes_wait(full_send.at[1], x_send.at[3])
 
 
 def bring_home(o_back, dq_back, key_back, grad_parts, out_rows):
     shards, part_rows, _ = o_back.shape
     slots = key_back.shape[1]
-    chips = shards // 2
     width = shards // 4 * DH
     rows = grad_parts[0].shape[1]
-    key_back = key_back.reshape(chips, 2, slots, 2 * DH)
+    key_back = key_back.reshape(4, 4, 2, slots, 2 * DH)
     vmem = pl.BlockSpec(memory_space=pltpu.VMEM)
     bf16 = jnp.bfloat16
     return pl.pallas_call(
@@ -650,16 +773,29 @@
         in_specs=[vmem] * 7,
         out_specs=(vmem,) * 4,
         scratch_shapes=[
+            pltpu.VMEM((4, rows, slots), bf16),
             pltpu.VMEM((4, slots, width), bf16),
-            pltpu.VMEM((chips, slots, 2 * DH), bf16),
-            pltpu.VMEM((chips, slots, 2 * DH), bf16),
-            pltpu.VMEM((chips, slots, 2 * DH), bf16),
+            pltpu.VMEM((4, 4, slots, 2 * DH), bf16),
+            pltpu.VMEM((4, 4, slots, 2 * DH), bf16),
+            pltpu.VMEM((4, 4, slots, 2 * DH), bf16),
+            pltpu.VMEM((4, 2, slots, 2 * DH), bf16),
+            pltpu.VMEM((4, 2, slots, 2 * DH), bf16),
             pltpu.VMEM((rows, width), bf16),
             pltpu.VMEM((4, out_rows, width), bf16),
-            pltpu.VMEM((3, out_rows, width), bf16),
-            pltpu.VMEM((3, out_rows, width), bf16),
-            pltpu.SemaphoreType.DMA((14,)),
-            pltpu.SemaphoreType.DMA((14,)),
+            pltpu.VMEM((out_rows, width), bf16),
+            pltpu.VMEM((out_rows, width), bf16),
+            pltpu.VMEM((2, out_rows, width), bf16),
+            pltpu.VMEM((2, out_rows, width), bf16),
+            pltpu.SemaphoreType.DMA((4,)),
+            pltpu.SemaphoreType.DMA((4,)),
+            pltpu.SemaphoreType.DMA((6,)),
+            pltpu.SemaphoreType.DMA((6,)),
+            pltpu.SemaphoreType.DMA((4,)),
+            pltpu.SemaphoreType.DMA((4, CHUNKS)),
+            pltpu.SemaphoreType.DMA,
+            pltpu.SemaphoreType.DMA((CHUNKS,)),
+            pltpu.SemaphoreType.DMA((4,)),
+            pltpu.SemaphoreType.DMA((4, CHUNKS)),
         ],
         compiler_params=pltpu.CompilerParams(
             collective_id=1, has_side_effects=True, vmem_limit_bytes=48 * 1024 * 1024

time: 165 us -> 142 us (0.86)
  Pallas kernels: 148 us -> 124 us
    pallas_call x1, Pallas kernels: 74.1 us -> 50.7 us  [bring_home(): pl.pallas_call(home_kernel, out_shape=(jax.ShapeDtypeStruct((slots, width...]
  transfers between devices with their start and end apart: 3 -> 3, of which waited for: 0 -> 0; matrix products, arithmetic and copies ran while one was open for 0% -> 0% of each run, Pallas kernels for 20% -> 23%
where the time goes in v5:
time: 142 us; the launch traced here: 141 us
  Pallas kernels  124 us (87%)
  matrix products  7.2 us (5%)
  starting transfers between devices  3.66 us (3%)
  local copies, waits for them, and re-layouts  2.7 us (2%)
  other arithmetic  2.69 us (2%)
    pallas_call x1, Pallas kernels, bring_home(): pl.pallas_call(home_kernel, out_shape=(jax.ShapeDtypeStruct((slots, width...  50.7 us
    pallas_call x1, Pallas kernels, spread(): pl.pallas_call(spread_kernel, out_shape=(jax.ShapeDtypeStruct((slots, col...  41.2 us
    pallas_call x1, Pallas kernels, attend(): pl.pallas_call(attend_kernel, out_shape=(jax.ShapeDtypeStruct((shards, pa...  32.3 us
    dot_general x4, matrix products, pick(): jnp.dot(which, values, preferred_element_type=jnp.float32)  5.52 us
    ppermute x3, starting transfers between devices, along_z(): lax.ppermute(blocks[k], 'seq', [(i, (i + 8 * k) % seq_count) for i in ran...  3.66 us
  transfers between devices with their start and end apart: 3, of which 0 were waited for; matrix products, arithmetic and copies ran while one was open for 0% of the time, Pallas kernels for 23%

profile of v5, /device:TPU:1, one launch (start us, length us, event | category | flops | bytes accessed | tf_op | source)
XLA Modules:
  0.0 141.3 jit_solution(9345053780951395861)
XLA Ops:
  0.6 0.0 copy-start
  0.6 0.0 copy-start.3
  0.7 1.8 %convolution_convert_fusion.4.v_ref = bf16[192,1024]{1,0:T(8,128)(2,1)S(1)} fusion(bf16[512,3,1024]{2,0,1:T(8,128)(2,1)} %param.5, s32[192]{0:T(256)} %bitcast.27), kind=kOutput, calls=%fused_computation.8 | convolution fusion | flops 201621504 | bytes 1442816 | tf_op jit(solution)/shard_map/dot_general | solution.py:834
  2.4 1.7 %convolution_convert_fusion.5.k_ref = bf16[192,1024]{1,0:T(8,128)(2,1)S(1)} fusion(bf16[512,3,1024]{2,0,1:T(8,128)(2,1)} %param.5, s32[192]{0:T(256)} %bitcast.28), kind=kOutput, calls=%fused_computation.9 | convolution fusion | flops 201621504 | bytes 1442816 | tf_op jit(solution)/shard_map/dot_general | solution.py:834
  4.1 0.5 broadcast.4
  4.6 0.0 copy-done.3
  4.6 0.7 reduce.3
  5.3 0.1 reshape_squeeze.3
  5.4 0.1 eq.33
  5.5 1.6 %convolution_convert_fusion.6.q_ref = bf16[192,1024]{1,0:T(8,128)(2,1)S(1)} fusion(bf16[512,3,1024]{2,0,1:T(8,128)(2,1)} %param.5, s32[192]{0:T(256)S(1)} %eq.33), kind=kOutput, calls=%fused_computation.10 | convolution fusion | flops 201621504 | bytes 1442560 | tf_op jit(solution)/shard_map/dot_general | solution.py:834
  7.1 0.0 copy-done
  7.2 0.5 convolution_convert_fusion.grad_ref
  7.6 0.0 copy-start.2
  7.6 41.2 %spread.1 = (bf16[192,1280]{1,0:T(8,128)(2,1)S(1)}, bf16[192,1280]{1,0:T(8,128)(2,1)S(1)}, bf16[192,1280]{1,0:T(8,128)(2,1)S(1)}, bf16[192,1280]{1,0:T(8,128)(2,...) custom-call(bf16[192,1280]{1,0:T(8,128)(2,1)S(1)} %convolution_conve, ...), custom_call_target="tpu_custom_call" | custom-call | tf_op jit(solution)/shard_map/spread/pallas_call | solution.py:463
  48.8 0.0 copy-start.1
  48.9 1.1 copy-done.1
  50.0 0.2 collective-permute-start
  50.2 2.8 %collective-permute-start.1 = (bf16[192,1280]{1,0:T(8,128)(2,1)S(1)}, bf16[192,1280]{1,0:T(8,128)(2,1)S(1)}, u32[]{:S(2)}, u32[]{:S(2)}) collective-permute-start(bf16[192,1280]{1,0:T(8,128)(2,1)S(1)} %get-tuple-element.26), channel_id=1, source_target_pairs={{0,64},{4,68},{8,72},{12,76},{16,80},{20,84},{24,88},{28,92},{32,9... | collective-permute-start | bytes 1474568 | tf_op jit(solution)/shard_map/ppermute | solution.py:848
  53.0 0.6 collective-permute-start.2
  53.7 0.0 copy-done.2
  53.7 32.3 %attend.1 = (bf16[32,48,128]{2,1,0:T(8,128)(2,1)S(1)}, bf16[32,48,128]{2,1,0:T(8,128)(2,1)S(1)}, bf16[32,192,256]{2,1,0:T(8,128)(2,1)}) custom-call(s32[32]{0:T(128)S(1)} %copy-done.2, s32[1]{0:T(128)} %bitcast.1.quarter_ref, bf16[32,48,128]{2,1,0:T(8,128)(2,1)S(1)} %get-tuple-element.17.q_hbm, bf16[32,48,128]{2,1,0:T(8,128)(2,1)S(1)} %get-tuple-element.18.g_hbm, ...), custom_call_target="tpu_custom_call" | custom-call | flops 7247757312 | bytes 16777216 | tf_op jit(solution)/shard_map/attend/pallas_call | solution.py:211
  86.0 0.0 collective-permute-done.g1_ref
  86.0 0.0 collective-permute-done.1.g2_ref
  86.0 0.0 collective-permute-done.2.g3_ref
  86.0 50.7 %home.1 = (bf16[192,1024]{1,0:T(8,128)(2,1)S(1)}, bf16[192,1024]{1,0:T(8,128)(2,1)S(1)}, bf16[192,1024]{1,0:T(8,128)(2,1)S(1)}, f32[160,1024]{1,0:T(8,128)S(1)}) custom-call(bf16[32,48,128]{2,1,0:T(8,128)(2,1)S(1)} %get-tuple-element.21.o_ref, bf16[32,48,128]{2,1,0:T(8,128)(2,1)S(1)} %get-tuple-element.22.dq_ref, bf16[4,4,2,192,256]{4,3,2,1,0:T(8,128)(2,1)} %bitcast.25, ...), custom_call_target="tpu_custom_call" | custom-call | tf_op jit(solution)/shard_map/home/pallas_call | solution.py:765
  136.7 0.6 fusion
  137.3 0.6 fusion.1
  137.9 0.6 fusion.2
  138.4 2.0 %pad_maximum_fusion = bf16[512,3,1024]{2,0,1:T(8,128)(2,1)} fusion(bf16[512,1,1024]{2,0,1:T(8,128)(2,1)S(1)} %fusion.2, bf16[512,1,1024]{2,0,1:T(8,128)(2,1)S(1)} %fusion.1, bf16[512,1,1024]{2,0,1:T(8,128)(2,1)S(1)} %fusion), kind=kLoop, calls=%fused_computation | loop fusion | flops 3145728 | bytes 6291456 | tf_op jit(solution)/shard_map/stack | solution.py:860
  140.4 0.8 copy.11
  (2 shorter events, 0.0 us)
Async XLA Ops:
  0.6 6.5 %copy-start = (bf16[512,1280]{1,0:T(8,128)(2,1)S(1)}, bf16[512,1280]{1,0:T(8,128)(2,1)}, u32[]{:S(2)}) copy-start(bf16[512,1280]{1,0:T(8,128)(2,1)} %param.6) | copy-start | bytes 3932164
  0.6 4.0 %copy-start.3 = (s32[1,192]{1,0:T(1,128)S(1)}, s32[1,192]{1,0:T(1,128)}, u32[]{:S(2)}) copy-start(s32[1,192]{1,0:T(1,128)} %param.8) | copy-start | bytes 2308
  7.6 46.0 %copy-start.2 = (s32[32]{0:T(128)S(1)}, s32[32]{0:T(128)}, u32[]{:S(2)}) copy-start(s32[32]{0:T(128)} %count_ref.1) | copy-start | bytes 388
  48.8 1.2 copy-start.1
  50.0 36.0 %collective-permute-start = (bf16[192,1280]{1,0:T(8,128)(2,1)S(1)}, bf16[192,1280]{1,0:T(8,128)(2,1)S(1)}, u32[]{:S(2)}, u32[]{:S(2)}) collective-permute-start(bf16[192,1280]{1,0:T(8,128)(2,1)S(1)} %get-tuple-element.25), channel_id=1, source_target_pairs={{0,32},{4,36},{8,40},{12,44},{16,48},{20,52},{24,56},{28,60},{32,6... | collective-permute-start | bytes 1474568 | tf_op jit(solution)/shard_map/ppermute | solution.py:848
  50.2 35.8 %collective-permute-start.1 = (bf16[192,1280]{1,0:T(8,128)(2,1)S(1)}, bf16[192,1280]{1,0:T(8,128)(2,1)S(1)}, u32[]{:S(2)}, u32[]{:S(2)}) collective-permute-start(bf16[192,1280]{1,0:T(8,128)(2,1)S(1)} %get-tuple-element.26), channel_id=1, source_target_pairs={{0,64},{4,68},{8,72},{12,76},{16,80},{20,84},{24,88},{28,92},{32,9... | collective-permute-start | bytes 1474568 | tf_op jit(solution)/shard_map/ppermute | solution.py:848
  53.0 33.0 %collective-permute-start.2 = (bf16[192,1280]{1,0:T(8,128)(2,1)S(1)}, bf16[192,1280]{1,0:T(8,128)(2,1)S(1)}, u32[]{:S(2)}, u32[]{:S(2)}) collective-permute-start(bf16[192,1280]{1,0:T(8,128)(2,1)S(1)} %get-tuple-element.27), channel_id=1, source_target_pairs={{0,96},{4,100},{8,104},{12,108},{16,112},{20,116},{24,120},{28,124... | collective-permute-start | bytes 1474568 | tf_op jit(solution)/shard_map/ppermute | solution.py:848

commit v6 on v5

--- a/solution.py
+++ b/solution.py
@@ -305,16 +305,22 @@
     acc,
     g_local,
     gblk,
+    k_col,
+    v_col,
     w_sem,
     copy_sem,
     y_send,
     y_recv,
-    kv_send,
-    kv_recv,
+    z_send,
+    z_recv,
+    x_send,
+    x_recv,
+    own_sem,
     pass_send,
     pass_recv,
     q_send,
     q_recv,
+    q_own,
 ):
     shards, part_rows, _ = q_in.shape
     slots, cols = grad_ref.shape
@@ -323,9 +329,8 @@
     row = lax.axis_index("head")
     core = me % 2
     sibling = me + 1 - 2 * core
-    chip = me // 2
-    chips = shards // 2
     my_z = me // 8
+    my_x = me // 2 % 4
     my_head = me // 4
     my_rows = pl.ds(pl.multiple_of((me % 4) * part_rows, GROUP), part_rows)
 
@@ -336,6 +341,9 @@
     def head_cols(head):
         return pl.ds(pl.multiple_of(head * DH, DH), DH)
 
+    def pair_cols(z):
+        return pl.ds(pl.multiple_of(z * 2 * DH, 2 * DH), 2 * DH)
+
     def slot_of(y):
         return lax.rem(y - my_z + 4, 4)
 
@@ -343,20 +351,46 @@
     to_right = send(grad_ref, gblk.at[slot_of(row)], y_send.at[0], y_recv.at[0], right, "head")
     to_left = send(grad_ref, gblk.at[slot_of(row)], y_send.at[1], y_recv.at[1], left, "head")
 
-    def send_kv(k, carry):
-        t = lax.rem(chip + k, chips)
-        source = head_cols(t // 2)
-        target = 2 * t + core
-        send(k_ref.at[:, source], k_in.at[me], kv_send.at[0], kv_recv.at[k], target)
-        send(v_ref.at[:, source], v_in.at[me], kv_send.at[1], kv_recv.at[chips + k], target)
-        return carry
-
-    lax.fori_loop(1, chips, send_kv, 0)
-    own = head_cols(my_head)
-    send(k_ref.at[:, own], k_in.at[me], pass_send.at[0], pass_recv.at[0], sibling)
-    send(v_ref.at[:, own], v_in.at[me], pass_send.at[1], pass_recv.at[1], sibling)
-    k_in[me] = k_ref[:, own]
-    v_in[me] = v_ref[:, own]
+    sides = ((k_ref, k_col, k_in), (v_ref, v_col, v_in))
+    for k in (1, 3, 2):
+        target = lax.rem(me + 8 * k, shards)
+        for i, (src, col, _) in enumerate(sides):
+            send(
+                src.at[:, pair_cols(lax.rem(my_z + k, 4))],
+                col.at[my_z],
+                z_send.at[i],
+                z_recv.at[i, k],
+                target,
+            )
+
+    def fan(k):
+        z = lax.rem(my_z - k + 4, 4)
+        for i, (src, col, out) in enumerate(sides):
+            if k:
+                block_bytes_wait(col.at[z], z_recv.at[i, k])
+            else:
+                col[z] = src[:, pair_cols(my_z)]
+            for d in (1, 3, 2):
+                x = lax.rem(my_x + d, 4)
+                send(
+                    col.at[z, :, head_cols(x // 2)],
+                    out.at[z, my_x, core],
+                    x_send.at[i],
+                    x_recv.at[i, k],
+                    me + 2 * (x - my_x),
+                )
+            pltpu.make_async_copy(
+                col.at[z, :, head_cols(my_x // 2)], out.at[z, my_x, core], own_sem.at[i, k]
+            ).start()
+
+    def pass_on(k):
+        z = lax.rem(my_z - k + 4, 4)
+        for i, (_, _, out) in enumerate(sides):
+            block_bytes_wait(out.at[z, pl.ds(0, 3), core], x_recv.at[i, k])
+            block_bytes_wait(out.at[z, my_x, core], own_sem.at[i, k])
+            send(out.at[z, :, core], out.at[z, :, core], pass_send.at[i], pass_recv.at[i], sibling)
+
+    fan(0)
 
     def send_q(k, carry):
         t = lax.rem(me + k, shards)
@@ -365,7 +399,8 @@
         return carry
 
     lax.fori_loop(1, shards, send_q, 0)
-    q_in[me] = q_ref[my_rows, own]
+    own_q = pltpu.make_async_copy(q_ref.at[my_rows, head_cols(my_head)], q_in.at[me], q_own.at[0])
+    own_q.start()
 
     width = 256
     tiles = acc.shape[1] // width
@@ -383,24 +418,19 @@
         lax.fori_loop(0, tiles, tile, 0)
 
     multiply(row, True)
+    for k in (1, 3, 2):
+        fan(k)
     to_right.wait_recv()
     from_left = gblk.at[slot_of(left), :, pl.ds(0, half)]
     on_right = send(from_left, from_left, y_send.at[2], y_recv.at[2], right, "head")
     to_left.wait_recv()
     from_right = gblk.at[slot_of(right), :, pl.ds(half, half)]
     on_left = send(from_right, from_right, y_send.at[3], y_recv.at[3], left, "head")
+    pass_on(0)
     multiply(left, False)
+    pass_on(1)
     multiply(right, False)
-
-    def pass_on(k, carry):
-        s = 2 * lax.rem(chip - k + chips, chips) + core
-        block_bytes_wait(k_in.at[s], kv_recv.at[k])
-        send(k_in.at[s], k_in.at[s], pass_send.at[0], pass_recv.at[0], sibling)
-        block_bytes_wait(v_in.at[s], kv_recv.at[chips + k])
-        send(v_in.at[s], v_in.at[s], pass_send.at[1], pass_recv.at[1], sibling)
-        return carry
-
-    lax.fori_loop(1, chips, pass_on, 0)
+    pass_on(3)
     on_right.wait_recv()
     on_left.wait_recv()
 
@@ -427,27 +457,30 @@
         return carry
 
     lax.fori_loop(0, tiles, finish, 0)
-    g_in[me] = g_local[my_rows, own]
+    own_g = pltpu.make_async_copy(
+        g_local.at[my_rows, head_cols(my_head)], g_in.at[me], q_own.at[1]
+    )
+    own_g.start()
     copies = [
         pltpu.make_async_copy(gblk.at[k], out, copy_sem.at[k])
         for k, out in enumerate((g0_out, g1_out, g2_out, g3_out))
     ]
     for copy in copies:
         copy.start()
+    pass_on(2)
     for copy in copies:
         copy.wait()
+    own_q.wait()
+    own_g.wait()
 
     others = pl.ds(0, shards - 1)
     block_bytes_wait(q_in.at[others], q_recv.at[0])
     block_bytes_wait(q_in.at[others], q_send.at[0])
-    passed = pl.ds(0, chips)
-    block_bytes_wait(k_in.at[passed], pass_recv.at[0])
-    block_bytes_wait(v_in.at[passed], pass_recv.at[1])
-    block_bytes_wait(k_in.at[passed], pass_send.at[0])
-    block_bytes_wait(v_in.at[passed], pass_send.at[1])
-    sent = pl.ds(0, chips - 1)
-    block_bytes_wait(k_in.at[sent], kv_send.at[0])
-    block_bytes_wait(v_in.at[sent], kv_send.at[1])
+    for i, (_, col, out) in enumerate(sides):
+        block_bytes_wait(out.at[:, :, core], pass_recv.at[i])
+        block_bytes_wait(out.at[:, :, core], pass_send.at[i])
+        block_bytes_wait(col.at[pl.ds(0, 3)], z_send.at[i])
+        block_bytes_wait(out.at[:, pl.ds(0, 3), core], x_send.at[i])
     for copy in (to_right, to_left, on_right, on_left):
         copy.wait_send()
     block_bytes_wait(g_in.at[others], q_recv.at[1])
@@ -460,31 +493,31 @@
     part_rows = slots // 4
     bf16 = jnp.bfloat16
     vmem = pl.BlockSpec(memory_space=pltpu.VMEM)
-    return pl.pallas_call(
+    block = jax.ShapeDtypeStruct((slots, cols), bf16)
+    small = jax.ShapeDtypeStruct((shards, part_rows, DH), bf16)
+    large = jax.ShapeDtypeStruct((4, 4, 2, slots, DH), bf16)
+    *blocks, query_in, grad_in, key_in, value_in = pl.pallas_call(
         spread_kernel,
-        out_shape=(
-            jax.ShapeDtypeStruct((slots, cols), bf16),
-            jax.ShapeDtypeStruct((slots, cols), bf16),
-            jax.ShapeDtypeStruct((slots, cols), bf16),
-            jax.ShapeDtypeStruct((slots, cols), bf16),
-            jax.ShapeDtypeStruct((shards, part_rows, DH), bf16),
-            jax.ShapeDtypeStruct((shards, part_rows, DH), bf16),
-            jax.ShapeDtypeStruct((shards, slots, DH), bf16),
-            jax.ShapeDtypeStruct((shards, slots, DH), bf16),
-        ),
+        out_shape=(block,) * 4 + (small,) * 2 + (large,) * 2,
         in_specs=[vmem] * 4 + [pl.BlockSpec(memory_space=pl.ANY)],
-        out_specs=(pl.BlockSpec(memory_space=pl.ANY),) * 4 + (vmem,) * 4,
+        out_specs=(pl.BlockSpec(memory_space=pl.ANY),) * 8,
         scratch_shapes=[
             pltpu.VMEM((depth, width), bf16),
             pltpu.VMEM((slots, width), jnp.float32),
             pltpu.VMEM((slots, width), bf16),
             pltpu.VMEM((4, slots, cols), bf16),
+            pltpu.VMEM((4, slots, 2 * DH), bf16),
+            pltpu.VMEM((4, slots, 2 * DH), bf16),
             pltpu.SemaphoreType.DMA,
             pltpu.SemaphoreType.DMA((4,)),
             pltpu.SemaphoreType.DMA((4,)),
             pltpu.SemaphoreType.DMA((4,)),
             pltpu.SemaphoreType.DMA((2,)),
-            pltpu.SemaphoreType.DMA((shards,)),
+            pltpu.SemaphoreType.DMA((2, 4)),
+            pltpu.SemaphoreType.DMA((2,)),
+            pltpu.SemaphoreType.DMA((2, 4)),
+            pltpu.SemaphoreType.DMA((2, 4)),
+            pltpu.SemaphoreType.DMA((2,)),
             pltpu.SemaphoreType.DMA((2,)),
             pltpu.SemaphoreType.DMA((2,)),
             pltpu.SemaphoreType.DMA((2,)),
@@ -495,6 +528,9 @@
         ),
         name="spread",
     )(grad_local, query, key, value, weight)
+    key_in = key_in.reshape(shards, slots, DH)
+    value_in = value_in.reshape(shards, slots, DH)
+    return (*blocks, query_in, grad_in, key_in, value_in)
 
 
 def home_kernel(

time: 142 us -> 138 us (0.972)
  Pallas kernels: 124 us -> 120 us
    pallas_call x1, Pallas kernels: 41.2 us -> 37.5 us  [spread(): pl.pallas_call(spread_kernel, out_shape=(block,) * 4 + (small,) * 2 + (la...]
    pallas_call x1, Pallas kernels: 32.3 us -> 30.4 us  [attend(): pl.pallas_call(attend_kernel, out_shape=(jax.ShapeDtypeStruct((shards, pa...]
    pallas_call x1, Pallas kernels: 50.7 us -> 52.1 us  [bring_home(): pl.pallas_call(home_kernel, out_shape=(jax.ShapeDtypeStruct((slots, width...]
  transfers between devices with their start and end apart: 3 -> 3, of which waited for: 0 -> 0; matrix products, arithmetic and copies ran while one was open for 0% -> 0% of each run, Pallas kernels for 23% -> 22%
where the time goes in v6:
time: 138 us; the launch traced here: 137 us
  Pallas kernels  120 us (87%)
  matrix products  7.2 us (5%)
  starting transfers between devices  3.87 us (3%)
  local copies, waits for them, and re-layouts  2.7 us (2%)
  other arithmetic  2.69 us (2%)
    pallas_call x1, Pallas kernels, bring_home(): pl.pallas_call(home_kernel, out_shape=(jax.ShapeDtypeStruct((slots, width...  52.1 us
    pallas_call x1, Pallas kernels, spread(): pl.pallas_call(spread_kernel, out_shape=(block,) * 4 + (small,) * 2 + (la...  37.5 us
    pallas_call x1, Pallas kernels, attend(): pl.pallas_call(attend_kernel, out_shape=(jax.ShapeDtypeStruct((shards, pa...  30.4 us
    dot_general x4, matrix products, pick(): jnp.dot(which, values, preferred_element_type=jnp.float32)  5.52 us
    ppermute x3, starting transfers between devices, along_z(): lax.ppermute(blocks[k], 'seq', [(i, (i + 8 * k) % seq_count) for i in ran...  3.87 us
  transfers between devices with their start and end apart: 3, of which 0 were waited for; matrix products, arithmetic and copies ran while one was open for 0% of the time, Pallas kernels for 22%

profile of v6, /device:TPU:1, one launch (start us, length us, event | category | flops | bytes accessed | tf_op | source)
XLA Modules:
  0.0 137.3 jit_solution(13489750161205222618)
XLA Ops:
  0.6 0.0 copy-start
  0.6 0.0 copy-start.3
  0.7 1.8 %convolution_convert_fusion.4.v_ref = bf16[192,1024]{1,0:T(8,128)(2,1)S(1)} fusion(bf16[512,3,1024]{2,0,1:T(8,128)(2,1)} %param.5, s32[192]{0:T(256)} %bitcast.30), kind=kOutput, calls=%fused_computation.8 | convolution fusion | flops 201621504 | bytes 1442816 | tf_op jit(solution)/shard_map/dot_general | solution.py:870
  2.4 1.7 %convolution_convert_fusion.5.k_ref = bf16[192,1024]{1,0:T(8,128)(2,1)S(1)} fusion(bf16[512,3,1024]{2,0,1:T(8,128)(2,1)} %param.5, s32[192]{0:T(256)} %bitcast.31), kind=kOutput, calls=%fused_computation.9 | convolution fusion | flops 201621504 | bytes 1442816 | tf_op jit(solution)/shard_map/dot_general | solution.py:870
  4.1 0.5 broadcast.4
  4.6 0.0 copy-done.3
  4.6 0.7 reduce.3
  5.3 0.1 reshape_squeeze.3
  5.4 0.1 eq.33
  5.5 1.6 %convolution_convert_fusion.6.q_ref = bf16[192,1024]{1,0:T(8,128)(2,1)S(1)} fusion(bf16[512,3,1024]{2,0,1:T(8,128)(2,1)} %param.5, s32[192]{0:T(256)S(1)} %eq.33), kind=kOutput, calls=%fused_computation.10 | convolution fusion | flops 201621504 | bytes 1442560 | tf_op jit(solution)/shard_map/dot_general | solution.py:870
  7.1 0.0 copy-done
  7.2 0.5 convolution_convert_fusion.grad_ref
  7.6 0.0 copy-start.2
  7.6 37.5 %spread.1 = (bf16[192,1280]{1,0:T(8,128)(2,1)S(1)}, bf16[192,1280]{1,0:T(8,128)(2,1)S(1)}, bf16[192,1280]{1,0:T(8,128)(2,1)S(1)}, bf16[192,1280]{1,0:T(8,128)(2,...) custom-call(bf16[192,1280]{1,0:T(8,128)(2,1)S(1)} %convolution_conve, ...), custom_call_target="tpu_custom_call" | custom-call | tf_op jit(solution)/shard_map/spread/pallas_call | solution.py:499
  45.1 0.0 copy-start.1
  45.1 1.1 copy-done.1
  46.3 0.5 collective-permute-start
  46.8 1.9 %collective-permute-start.1 = (bf16[192,1280]{1,0:T(8,128)(2,1)S(1)}, bf16[192,1280]{1,0:T(8,128)(2,1)S(1)}, u32[]{:S(2)}, u32[]{:S(2)}) collective-permute-start(bf16[192,1280]{1,0:T(8,128)(2,1)S(1)} %get-tuple-element.26), channel_id=1, source_target_pairs={{0,64},{4,68},{8,72},{12,76},{16,80},{20,84},{24,88},{28,92},{32,9... | collective-permute-start | bytes 1474568 | tf_op jit(solution)/shard_map/ppermute | solution.py:884
  48.7 1.4 %collective-permute-start.2 = (bf16[192,1280]{1,0:T(8,128)(2,1)S(1)}, bf16[192,1280]{1,0:T(8,128)(2,1)S(1)}, u32[]{:S(2)}, u32[]{:S(2)}) collective-permute-start(bf16[192,1280]{1,0:T(8,128)(2,1)S(1)} %get-tuple-element.27), channel_id=1, source_target_pairs={{0,96},{4,100},{8,104},{12,108},{16,112},{20,116},{24,120},{28,124... | collective-permute-start | bytes 1474568 | tf_op jit(solution)/shard_map/ppermute | solution.py:884
  50.1 0.0 copy-done.2
  50.1 30.4 %attend.1 = (bf16[32,48,128]{2,1,0:T(8,128)(2,1)S(1)}, bf16[32,48,128]{2,1,0:T(8,128)(2,1)S(1)}, bf16[32,192,256]{2,1,0:T(8,128)(2,1)}) custom-call(s32[32]{0:T(128)S(1)} %copy-done.2, s32[1]{0:T(128)} %bitcast.1.quarter_ref, bf16[32,48,128]{2,1,0:T(8,128)(2,1)S(1)} %get-tuple-element.17.q_hbm, bf16[32,48,128]{2,1,0:T(8,128)(2,1)S(1)} %get-tuple-element.18.g_hbm, ...), custom_call_target="tpu_custom_call" | custom-call | flops 7247757312 | bytes 16777216 | tf_op jit(solution)/shard_map/attend/pallas_call | solution.py:211
  80.5 0.0 collective-permute-done.g1_ref
  80.6 0.0 collective-permute-done.1.g2_ref
  80.6 0.0 collective-permute-done.2.g3_ref
  80.6 52.1 %home.1 = (bf16[192,1024]{1,0:T(8,128)(2,1)S(1)}, bf16[192,1024]{1,0:T(8,128)(2,1)S(1)}, bf16[192,1024]{1,0:T(8,128)(2,1)S(1)}, f32[160,1024]{1,0:T(8,128)S(1)}) custom-call(bf16[32,48,128]{2,1,0:T(8,128)(2,1)S(1)} %get-tuple-element.21.o_ref, bf16[32,48,128]{2,1,0:T(8,128)(2,1)S(1)} %get-tuple-element.22.dq_ref, bf16[4,4,2,192,256]{4,3,2,1,0:T(8,128)(2,1)} %bitcast.28, ...), custom_call_target="tpu_custom_call" | custom-call | tf_op jit(solution)/shard_map/home/pallas_call | solution.py:801
  132.7 0.6 fusion
  133.3 0.6 fusion.1
  133.9 0.6 fusion.2
  134.4 2.0 %pad_maximum_fusion = bf16[512,3,1024]{2,0,1:T(8,128)(2,1)} fusion(bf16[512,1,1024]{2,0,1:T(8,128)(2,1)S(1)} %fusion.2, bf16[512,1,1024]{2,0,1:T(8,128)(2,1)S(1)} %fusion.1, bf16[512,1,1024]{2,0,1:T(8,128)(2,1)S(1)} %fusion), kind=kLoop, calls=%fused_computation | loop fusion | flops 3145728 | bytes 6291456 | tf_op jit(solution)/shard_map/stack | solution.py:896
  136.4 0.8 copy.11
  (2 shorter events, 0.0 us)
Async XLA Ops:
  0.6 6.5 %copy-start = (bf16[512,1280]{1,0:T(8,128)(2,1)S(1)}, bf16[512,1280]{1,0:T(8,128)(2,1)}, u32[]{:S(2)}) copy-start(bf16[512,1280]{1,0:T(8,128)(2,1)} %param.6) | copy-start | bytes 3932164
  0.6 4.0 %copy-start.3 = (s32[1,192]{1,0:T(1,128)S(1)}, s32[1,192]{1,0:T(1,128)}, u32[]{:S(2)}) copy-start(s32[1,192]{1,0:T(1,128)} %param.8) | copy-start | bytes 2308
  7.6 42.5 %copy-start.2 = (s32[32]{0:T(128)S(1)}, s32[32]{0:T(128)}, u32[]{:S(2)}) copy-start(s32[32]{0:T(128)} %count_ref.1) | copy-start | bytes 388
  45.1 1.2 copy-start.1
  46.3 34.3 %collective-permute-start = (bf16[192,1280]{1,0:T(8,128)(2,1)S(1)}, bf16[192,1280]{1,0:T(8,128)(2,1)S(1)}, u32[]{:S(2)}, u32[]{:S(2)}) collective-permute-start(bf16[192,1280]{1,0:T(8,128)(2,1)S(1)} %get-tuple-element.25), channel_id=1, source_target_pairs={{0,32},{4,36},{8,40},{12,44},{16,48},{20,52},{24,56},{28,60},{32,6... | collective-permute-start | bytes 1474568 | tf_op jit(solution)/shard_map/ppermute | solution.py:884
  46.8 33.8 %collective-permute-start.1 = (bf16[192,1280]{1,0:T(8,128)(2,1)S(1)}, bf16[192,1280]{1,0:T(8,128)(2,1)S(1)}, u32[]{:S(2)}, u32[]{:S(2)}) collective-permute-start(bf16[192,1280]{1,0:T(8,128)(2,1)S(1)} %get-tuple-element.26), channel_id=1, source_target_pairs={{0,64},{4,68},{8,72},{12,76},{16,80},{20,84},{24,88},{28,92},{32,9... | collective-permute-start | bytes 1474568 | tf_op jit(solution)/shard_map/ppermute | solution.py:884
  48.7 31.8 %collective-permute-start.2 = (bf16[192,1280]{1,0:T(8,128)(2,1)S(1)}, bf16[192,1280]{1,0:T(8,128)(2,1)S(1)}, u32[]{:S(2)}, u32[]{:S(2)}) collective-permute-start(bf16[192,1280]{1,0:T(8,128)(2,1)S(1)} %get-tuple-element.27), channel_id=1, source_target_pairs={{0,96},{4,100},{8,104},{12,108},{16,112},{20,116},{24,120},{28,124... | collective-permute-start | bytes 1474568 | tf_op jit(solution)/shard_map/ppermute | solution.py:884

commit v7 on v6

--- a/solution.py
+++ b/solution.py
@@ -37,6 +37,7 @@
     g_ref,
     k_ref,
     v_ref,
+    k_stage,
     qc,
     gc,
     kc,
@@ -53,6 +54,7 @@
     acc,
     group_pos,
     load_sem,
+    store_sem,
 ):
     shards, part_rows, _ = q_ref.shape
     slots = k_ref.shape[1]
@@ -190,13 +192,23 @@
         first = lax.rem(quarter + s, 4)
         at_k = pl.multiple_of(at_k, GROUP)
         at_q = pl.multiple_of(at_q, GROUP)
-        dq_out[s] = oc[pl.ds(at_q, part_rows), :DH]
-        o_out[s] = oc[pl.ds(at_q, part_rows), DH:]
-        k_out[s, :, :DH] = (dkc[pl.ds(at_k, slots), :] * score_scale).astype(bf16)
-        k_out[s, :, DH:] = dvc[pl.ds(at_k, slots), :].astype(bf16)
+        q_ref[s] = oc[pl.ds(at_q, part_rows), :DH]
+        g_ref[s] = oc[pl.ds(at_q, part_rows), DH:]
+        k_stage[s, :, :DH] = (dkc[pl.ds(at_k, slots), :] * score_scale).astype(bf16)
+        k_stage[s, :, DH:] = dvc[pl.ds(at_k, slots), :].astype(bf16)
+        pltpu.make_async_copy(k_stage.at[s], k_out.at[s], store_sem.at[0]).start()
         return at_k + live * GROUP, at_q + (live - first + 3) // 4 * GROUP
 
     lax.fori_loop(0, shards, unpack, (jnp.int32(0), jnp.int32(0)))
+    stores = [
+        pltpu.make_async_copy(q_ref, dq_out, store_sem.at[1]),
+        pltpu.make_async_copy(g_ref, o_out, store_sem.at[2]),
+    ]
+    for store in stores:
+        store.start()
+    pltpu.make_async_copy(k_stage, k_out, store_sem.at[0]).wait()
+    for store in stores:
+        store.wait()
 
 
 def attend(counts, quarter, query_in, grad_in, key_in, value_in):
@@ -205,9 +217,8 @@
     keys = shards * slots
     queries = shards * part_rows
     bf16 = jnp.bfloat16
-    vmem = pl.BlockSpec(memory_space=pltpu.VMEM)
     smem = pl.BlockSpec(memory_space=pltpu.SMEM)
-    hbm = pl.BlockSpec(memory_space=pl.ANY)
+    hbm = pl.BlockSpec(memory_space=pltpu.HBM)
     return pl.pallas_call(
         attend_kernel,
         out_shape=(
@@ -216,12 +227,13 @@
             jax.ShapeDtypeStruct((shards, slots, 2 * DH), bf16),
         ),
         in_specs=[smem, smem, hbm, hbm, hbm, hbm],
-        out_specs=(vmem, vmem, vmem),
+        out_specs=(hbm, hbm, hbm),
         scratch_shapes=[
             pltpu.VMEM((shards, part_rows, DH), bf16),
             pltpu.VMEM((shards, part_rows, DH), bf16),
             pltpu.VMEM((shards, slots, DH), bf16),
             pltpu.VMEM((shards, slots, DH), bf16),
+            pltpu.VMEM((shards, slots, 2 * DH), bf16),
             pltpu.VMEM((queries + BQ, DH), bf16),
             pltpu.VMEM((queries + BQ, DH), bf16),
             pltpu.VMEM((keys + BK, 2 * DH), bf16),
@@ -238,6 +250,7 @@
             pltpu.VMEM((DH, BQ), jnp.float32),
             pltpu.SMEM((queries // GROUP + 8,), jnp.int32),
             pltpu.SemaphoreType.DMA((4,)),
+            pltpu.SemaphoreType.DMA((3,)),
         ],
         compiler_params=pltpu.CompilerParams(vmem_limit_bytes=52 * 1024 * 1024),
         cost_estimate=pl.CostEstimate(
@@ -500,7 +513,7 @@
         spread_kernel,
         out_shape=(block,) * 4 + (small,) * 2 + (large,) * 2,
         in_specs=[vmem] * 4 + [pl.BlockSpec(memory_space=pl.ANY)],
-        out_specs=(pl.BlockSpec(memory_space=pl.ANY),) * 8,
+        out_specs=(pl.BlockSpec(memory_space=pltpu.HBM),) * 8,
         scratch_shapes=[
             pltpu.VMEM((depth, width), bf16),
             pltpu.VMEM((slots, width), jnp.float32),
@@ -545,6 +558,8 @@
     gk_home,
     gv_home,
     wg_out,
+    g_vmem,
+    k_own,
     g_turned,
     oz,
     kx,
@@ -560,6 +575,7 @@
     full_recv,
     send_sem,
     recv_sem,
+    load_sem,
     k_send,
     k_recv,
     z_send,
@@ -581,6 +597,22 @@
     my_cols = pl.ds(pl.multiple_of((me // 4) * DH, DH), DH)
     f32, bf16 = jnp.float32, jnp.bfloat16
 
+    loads = [
+        pltpu.make_async_copy(src, dst, load_sem.at[i])
+        for i, (src, dst) in enumerate(
+            (
+                (o_ref.at[me], oz.at[0, my_rows, my_cols]),
+                (g0_ref, g_vmem.at[0]),
+                (g1_ref, g_vmem.at[1]),
+                (g2_ref, g_vmem.at[2]),
+                (g3_ref, g_vmem.at[3]),
+                (k_ref.at[:, :, core], k_own),
+                (dq_ref.at[me], dq_home.at[my_rows, my_cols]),
+            )
+        )
+    ]
+    for load in loads:
+        load.start()
     greet(shards - 1, lambda k: lax.rem(me + k, shards))
 
     def send_o(k, carry):
@@ -590,15 +622,15 @@
 
     lax.fori_loop(1, shards, send_o, 0)
     swap = send(k_ref.at[:, :, 1 - core], kx, send_sem.at[1], recv_sem.at[1], sibling)
-    oz[0, my_rows, my_cols] = o_ref[me]
-    dq_home[my_rows, my_cols] = dq_ref[me]
+    for load in loads:
+        load.wait()
 
     tile = 256
 
     def turn(j, carry):
         cols = pl.ds(pl.multiple_of(j * tile, tile), tile)
-        for k, g_ref in enumerate((g0_ref, g1_ref, g2_ref, g3_ref)):
-            g_turned[k, cols, :] = g_ref[:, cols].T
+        for k in range(4):
+            g_turned[k, cols, :] = g_vmem[k, :, cols].T
         return carry
 
     lax.fori_loop(0, part.shape[0] // tile, turn, 0)
@@ -712,7 +744,7 @@
         )
 
     def k_sum(z, x):
-        return (k_ref[z, x, core].astype(f32) + kx[z, x].astype(f32)).astype(bf16)
+        return (k_own[z, x].astype(f32) + kx[z, x].astype(f32)).astype(bf16)
 
     def k_along_x():
         for k in (1, 2, 3):
@@ -806,9 +838,11 @@
             jax.ShapeDtypeStruct((slots, width), bf16),
             jax.ShapeDtypeStruct((out_rows, width), jnp.float32),
         ),
-        in_specs=[vmem] * 7,
+        in_specs=[pl.BlockSpec(memory_space=pltpu.HBM)] * 7,
         out_specs=(vmem,) * 4,
         scratch_shapes=[
+            pltpu.VMEM((4, slots, rows), bf16),
+            pltpu.VMEM((4, 4, slots, 2 * DH), bf16),
             pltpu.VMEM((4, rows, slots), bf16),
             pltpu.VMEM((4, slots, width), bf16),
             pltpu.VMEM((4, 4, slots, 2 * DH), bf16),
@@ -824,6 +858,7 @@
             pltpu.VMEM((2, out_rows, width), bf16),
             pltpu.SemaphoreType.DMA((4,)),
             pltpu.SemaphoreType.DMA((4,)),
+            pltpu.SemaphoreType.DMA((7,)),
             pltpu.SemaphoreType.DMA((6,)),
             pltpu.SemaphoreType.DMA((6,)),
             pltpu.SemaphoreType.DMA((4,)),

time: 138 us -> 136 us (0.986)
  Pallas kernels: 120 us -> 118 us
where the time goes in v7:
time: 136 us
  Pallas kernels  118 us (87%)
  matrix products  7.2 us (5%)
  starting transfers between devices  3.87 us (3%)
  local copies, waits for them, and re-layouts  2.7 us (2%)
  other arithmetic  2.69 us (2%)
    pallas_call x1, Pallas kernels, bring_home(): pl.pallas_call(home_kernel, out_shape=(jax.ShapeDtypeStruct((slots, width...  51.5 us
    pallas_call x1, Pallas kernels, spread(): pl.pallas_call(spread_kernel, out_shape=(block,) * 4 + (small,) * 2 + (la...  37.5 us
    pallas_call x1, Pallas kernels, attend(): pl.pallas_call(attend_kernel, out_shape=(jax.ShapeDtypeStruct((shards, pa...  29.5 us
    dot_general x4, matrix products, pick(): jnp.dot(which, values, preferred_element_type=jnp.float32)  5.52 us
    ppermute x3, starting transfers between devices, along_z(): lax.ppermute(blocks[k], 'seq', [(i, (i + 8 * k) % seq_count) for i in ran...  3.87 us
  transfers between devices with their start and end apart: 3, of which 0 were waited for; matrix products, arithmetic and copies ran while one was open for 0% of the time, Pallas kernels for 22%

profile of v7, /device:TPU:1, one launch (start us, length us, event | category | flops | bytes accessed | tf_op | source)
XLA Modules:
  0.0 135.7 jit_solution(7325635764462623019)
XLA Ops:
  0.6 0.0 copy-start
  0.6 0.0 copy-start.3
  0.7 1.8 %convolution_convert_fusion.4.v_ref = bf16[192,1024]{1,0:T(8,128)(2,1)S(1)} fusion(bf16[512,3,1024]{2,0,1:T(8,128)(2,1)} %param.5, s32[192]{0:T(256)} %bitcast.30), kind=kOutput, calls=%fused_computation.8 | convolution fusion | flops 201621504 | bytes 1442816 | tf_op jit(solution)/shard_map/dot_general | solution.py:905
  2.4 1.7 %convolution_convert_fusion.5.k_ref = bf16[192,1024]{1,0:T(8,128)(2,1)S(1)} fusion(bf16[512,3,1024]{2,0,1:T(8,128)(2,1)} %param.5, s32[192]{0:T(256)} %bitcast.31), kind=kOutput, calls=%fused_computation.9 | convolution fusion | flops 201621504 | bytes 1442816 | tf_op jit(solution)/shard_map/dot_general | solution.py:905
  4.1 0.5 broadcast.4
  4.6 0.0 copy-done.3
  4.6 0.7 reduce.3
  5.3 0.1 reshape_squeeze.3
  5.4 0.1 eq.33
  5.5 1.6 %convolution_convert_fusion.6.q_ref = bf16[192,1024]{1,0:T(8,128)(2,1)S(1)} fusion(bf16[512,3,1024]{2,0,1:T(8,128)(2,1)} %param.5, s32[192]{0:T(256)S(1)} %eq.33), kind=kOutput, calls=%fused_computation.10 | convolution fusion | flops 201621504 | bytes 1442560 | tf_op jit(solution)/shard_map/dot_general | solution.py:905
  7.1 0.0 copy-done
  7.2 0.5 convolution_convert_fusion.grad_ref
  7.6 0.0 copy-start.2
  7.6 37.5 %spread.1 = (bf16[192,1280]{1,0:T(8,128)(2,1)S(1)}, bf16[192,1280]{1,0:T(8,128)(2,1)S(1)}, bf16[192,1280]{1,0:T(8,128)(2,1)S(1)}, bf16[192,1280]{1,0:T(8,128)(2,...) custom-call(bf16[192,1280]{1,0:T(8,128)(2,1)S(1)} %convolution_conve, ...), custom_call_target="tpu_custom_call" | custom-call | tf_op jit(solution)/shard_map/spread/pallas_call | solution.py:512
  45.1 0.0 copy-start.1
  45.1 1.1 copy-done.1
  46.3 0.5 collective-permute-start
  46.8 1.9 %collective-permute-start.1 = (bf16[192,1280]{1,0:T(8,128)(2,1)S(1)}, bf16[192,1280]{1,0:T(8,128)(2,1)S(1)}, u32[]{:S(2)}, u32[]{:S(2)}) collective-permute-start(bf16[192,1280]{1,0:T(8,128)(2,1)S(1)} %get-tuple-element.26), channel_id=1, source_target_pairs={{0,64},{4,68},{8,72},{12,76},{16,80},{20,84},{24,88},{28,92},{32,9... | collective-permute-start | bytes 1474568 | tf_op jit(solution)/shard_map/ppermute | solution.py:919
  48.7 1.4 %collective-permute-start.2 = (bf16[192,1280]{1,0:T(8,128)(2,1)S(1)}, bf16[192,1280]{1,0:T(8,128)(2,1)S(1)}, u32[]{:S(2)}, u32[]{:S(2)}) collective-permute-start(bf16[192,1280]{1,0:T(8,128)(2,1)S(1)} %get-tuple-element.27), channel_id=1, source_target_pairs={{0,96},{4,100},{8,104},{12,108},{16,112},{20,116},{24,120},{28,124... | collective-permute-start | bytes 1474568 | tf_op jit(solution)/shard_map/ppermute | solution.py:919
  50.1 0.0 copy-done.2
  50.1 29.5 %attend.1 = (bf16[32,48,128]{2,1,0:T(8,128)(2,1)S(1)}, bf16[32,48,128]{2,1,0:T(8,128)(2,1)S(1)}, bf16[32,192,256]{2,1,0:T(8,128)(2,1)}) custom-call(s32[32]{0:T(128)S(1)} %copy-done.2, s32[1]{0:T(128)} %bitcast.1.quarter_ref, bf16[32,48,128]{2,1,0:T(8,128)(2,1)S(1)} %get-tuple-element.17.q_hbm, bf16[32,48,128]{2,1,0:T(8,128)(2,1)S(1)} %get-tuple-element.18.g_hbm, ...), custom_call_target="tpu_custom_call" | custom-call | flops 7247757312 | bytes 16777216 | tf_op jit(solution)/shard_map/attend/pallas_call | solution.py:222
  79.7 0.0 collective-permute-done.g1_ref
  79.7 0.0 collective-permute-done.1.g2_ref
  79.7 0.0 collective-permute-done.2.g3_ref
  79.7 51.5 %home.1 = (bf16[192,1024]{1,0:T(8,128)(2,1)S(1)}, bf16[192,1024]{1,0:T(8,128)(2,1)S(1)}, bf16[192,1024]{1,0:T(8,128)(2,1)S(1)}, f32[160,1024]{1,0:T(8,128)S(1)}) custom-call(bf16[32,48,128]{2,1,0:T(8,128)(2,1)S(1)} %get-tuple-element.21.o_ref, bf16[32,48,128]{2,1,0:T(8,128)(2,1)S(1)} %get-tuple-element.22.dq_ref, bf16[4,4,2,192,256]{4,3,2,1,0:T(8,128)(2,1)} %bitcast.28, ...), custom_call_target="tpu_custom_call" | custom-call | tf_op jit(solution)/shard_map/home/pallas_call | solution.py:833
  131.2 0.6 fusion
  131.7 0.6 fusion.1
  132.3 0.6 fusion.2
  132.8 2.0 %pad_maximum_fusion = bf16[512,3,1024]{2,0,1:T(8,128)(2,1)} fusion(bf16[512,1,1024]{2,0,1:T(8,128)(2,1)S(1)} %fusion.2, bf16[512,1,1024]{2,0,1:T(8,128)(2,1)S(1)} %fusion.1, bf16[512,1,1024]{2,0,1:T(8,128)(2,1)S(1)} %fusion), kind=kLoop, calls=%fused_computation | loop fusion | flops 3145728 | bytes 6291456 | tf_op jit(solution)/shard_map/stack | solution.py:931
  134.9 0.8 copy.11
  (2 shorter events, 0.0 us)
Async XLA Ops:
  0.6 6.5 %copy-start = (bf16[512,1280]{1,0:T(8,128)(2,1)S(1)}, bf16[512,1280]{1,0:T(8,128)(2,1)}, u32[]{:S(2)}) copy-start(bf16[512,1280]{1,0:T(8,128)(2,1)} %param.6) | copy-start | bytes 3932164
  0.6 4.0 %copy-start.3 = (s32[1,192]{1,0:T(1,128)S(1)}, s32[1,192]{1,0:T(1,128)}, u32[]{:S(2)}) copy-start(s32[1,192]{1,0:T(1,128)} %param.8) | copy-start | bytes 2308
  7.6 42.5 %copy-start.2 = (s32[32]{0:T(128)S(1)}, s32[32]{0:T(128)}, u32[]{:S(2)}) copy-start(s32[32]{0:T(128)} %count_ref.1) | copy-start | bytes 388
  45.1 1.2 copy-start.1
  46.3 33.4 %collective-permute-start = (bf16[192,1280]{1,0:T(8,128)(2,1)S(1)}, bf16[192,1280]{1,0:T(8,128)(2,1)S(1)}, u32[]{:S(2)}, u32[]{:S(2)}) collective-permute-start(bf16[192,1280]{1,0:T(8,128)(2,1)S(1)} %get-tuple-element.25), channel_id=1, source_target_pairs={{0,32},{4,36},{8,40},{12,44},{16,48},{20,52},{24,56},{28,60},{32,6... | collective-permute-start | bytes 1474568 | tf_op jit(solution)/shard_map/ppermute | solution.py:919
  46.8 32.9 %collective-permute-start.1 = (bf16[192,1280]{1,0:T(8,128)(2,1)S(1)}, bf16[192,1280]{1,0:T(8,128)(2,1)S(1)}, u32[]{:S(2)}, u32[]{:S(2)}) collective-permute-start(bf16[192,1280]{1,0:T(8,128)(2,1)S(1)} %get-tuple-element.26), channel_id=1, source_target_pairs={{0,64},{4,68},{8,72},{12,76},{16,80},{20,84},{24,88},{28,92},{32,9... | collective-permute-start | bytes 1474568 | tf_op jit(solution)/shard_map/ppermute | solution.py:919
  48.7 31.0 %collective-permute-start.2 = (bf16[192,1280]{1,0:T(8,128)(2,1)S(1)}, bf16[192,1280]{1,0:T(8,128)(2,1)S(1)}, u32[]{:S(2)}, u32[]{:S(2)}) collective-permute-start(bf16[192,1280]{1,0:T(8,128)(2,1)S(1)} %get-tuple-element.27), channel_id=1, source_target_pairs={{0,96},{4,100},{8,104},{12,108},{16,112},{20,116},{24,120},{28,124... | collective-permute-start | bytes 1474568 | tf_op jit(solution)/shard_map/ppermute | solution.py:919

commit v8 on v7

--- a/solution.py
+++ b/solution.py
@@ -13,6 +13,7 @@
 GROUP = 16
 NEG = -1e30
 CHUNKS = 4
+VMEM_BYTES = 60 * 1024 * 1024
 K_STEP = 4
 DQ_STEP = 4
 
@@ -252,7 +253,7 @@
             pltpu.SemaphoreType.DMA((4,)),
             pltpu.SemaphoreType.DMA((3,)),
         ],
-        compiler_params=pltpu.CompilerParams(vmem_limit_bytes=52 * 1024 * 1024),
+        compiler_params=pltpu.CompilerParams(vmem_limit_bytes=VMEM_BYTES),
         cost_estimate=pl.CostEstimate(
             flops=6 * queries * keys * DH, bytes_accessed=16 * 1024 * 1024, transcendentals=0
         ),
@@ -264,7 +265,7 @@
     pltpu.make_async_copy(ref, ref, sem).wait()
 
 
-def greet(peers, peer_of, ring=0):
+def greet(peers, peer_of, ring=0, meanwhile=None):
     barrier = pltpu.get_barrier_semaphore()
 
     def signal(k, carry):
@@ -284,6 +285,8 @@
                 device_id_type=pl.DeviceIdType.MESH,
             )
         peers = peers + ring - 1
+    if meanwhile is not None:
+        meanwhile()
     pl.semaphore_wait(barrier, peers)
 
 
@@ -302,9 +305,9 @@
 
 def spread_kernel(
     grad_ref,
-    q_ref,
-    k_ref,
-    v_ref,
+    dealt_ref,
+    select_ref,
+    p_hbm,
     w_hbm,
     g0_out,
     g1_out,
@@ -315,12 +318,17 @@
     k_in,
     v_in,
     w_ref,
+    p_ref,
+    q_ref,
+    k_ref,
+    v_ref,
     acc,
     g_local,
     gblk,
     k_col,
     v_col,
     w_sem,
+    p_sem,
     copy_sem,
     y_send,
     y_recv,
@@ -348,8 +356,28 @@
     my_rows = pl.ds(pl.multiple_of((me % 4) * part_rows, GROUP), part_rows)
 
     load_w = pltpu.make_async_copy(w_hbm, w_ref, w_sem)
+    load_p = pltpu.make_async_copy(p_hbm, p_ref, p_sem)
+    load_p.start()
     load_w.start()
-    greet(shards - 1, lambda k: lax.rem(me + k, shards), 4)
+    width = 256
+    tiles = acc.shape[1] // width
+
+    def pick():
+        load_p.wait()
+
+        def tile(j, carry):
+            at = pl.ds(pl.multiple_of(j * width, width), width)
+            for i, (which, out) in enumerate(
+                ((dealt_ref, q_ref), (select_ref, k_ref), (select_ref, v_ref))
+            ):
+                out[:, at] = jnp.dot(
+                    which[...], p_ref[i, :, at], preferred_element_type=jnp.float32
+                ).astype(jnp.bfloat16)
+            return carry
+
+        lax.fori_loop(0, tiles, tile, 0)
+
+    greet(shards - 1, lambda k: lax.rem(me + k, shards), 4, pick)
 
     def head_cols(head):
         return pl.ds(pl.multiple_of(head * DH, DH), DH)
@@ -415,8 +443,6 @@
     own_q = pltpu.make_async_copy(q_ref.at[my_rows, head_cols(my_head)], q_in.at[me], q_own.at[0])
     own_q.start()
 
-    width = 256
-    tiles = acc.shape[1] // width
     gblk[slot_of(row)] = grad_ref[...]
     load_w.wait()
 
@@ -500,7 +526,7 @@
     block_bytes_wait(g_in.at[others], q_send.at[1])
 
 
-def spread(grad_local, query, key, value, weight, shards):
+def spread(grad_local, dealt_selector, selector, projections, weight, shards):
     slots, cols = grad_local.shape
     depth, width = weight.shape
     part_rows = slots // 4
@@ -512,15 +538,20 @@
     *blocks, query_in, grad_in, key_in, value_in = pl.pallas_call(
         spread_kernel,
         out_shape=(block,) * 4 + (small,) * 2 + (large,) * 2,
-        in_specs=[vmem] * 4 + [pl.BlockSpec(memory_space=pl.ANY)],
+        in_specs=[vmem] * 3 + [pl.BlockSpec(memory_space=pltpu.HBM)] * 2,
         out_specs=(pl.BlockSpec(memory_space=pltpu.HBM),) * 8,
         scratch_shapes=[
             pltpu.VMEM((depth, width), bf16),
+            pltpu.VMEM(projections.shape, bf16),
+            pltpu.VMEM((slots, width), bf16),
+            pltpu.VMEM((slots, width), bf16),
+            pltpu.VMEM((slots, width), bf16),
             pltpu.VMEM((slots, width), jnp.float32),
             pltpu.VMEM((slots, width), bf16),
             pltpu.VMEM((4, slots, cols), bf16),
             pltpu.VMEM((4, slots, 2 * DH), bf16),
             pltpu.VMEM((4, slots, 2 * DH), bf16),
+            pltpu.SemaphoreType.DMA,
             pltpu.SemaphoreType.DMA,
             pltpu.SemaphoreType.DMA((4,)),
             pltpu.SemaphoreType.DMA((4,)),
@@ -537,10 +568,10 @@
             pltpu.SemaphoreType.DMA((2,)),
         ],
         compiler_params=pltpu.CompilerParams(
-            collective_id=2, has_side_effects=True, vmem_limit_bytes=48 * 1024 * 1024
+            collective_id=2, has_side_effects=True, vmem_limit_bytes=VMEM_BYTES
         ),
         name="spread",
-    )(grad_local, query, key, value, weight)
+    )(grad_local, dealt_selector, selector, projections, weight)
     key_in = key_in.reshape(shards, slots, DH)
     value_in = value_in.reshape(shards, slots, DH)
     return (*blocks, query_in, grad_in, key_in, value_in)
@@ -554,9 +585,7 @@
     g1_ref,
     g2_ref,
     g3_ref,
-    dq_home,
-    gk_home,
-    gv_home,
+    home,
     wg_out,
     g_vmem,
     k_own,
@@ -607,7 +636,7 @@
                 (g2_ref, g_vmem.at[2]),
                 (g3_ref, g_vmem.at[3]),
                 (k_ref.at[:, :, core], k_own),
-                (dq_ref.at[me], dq_home.at[my_rows, my_cols]),
+                (dq_ref.at[me], home.at[0, my_rows, my_cols]),
             )
         )
     ]
@@ -782,7 +811,7 @@
 
     def send_dq(k, carry):
         t = lax.rem(me + k, shards)
-        send(dq_ref.at[t], dq_home.at[my_rows, my_cols], send_sem.at[3], recv_sem.at[3], t)
+        send(dq_ref.at[t], home.at[0, my_rows, my_cols], send_sem.at[3], recv_sem.at[3], t)
         return carry
 
     start_z(0)
@@ -803,8 +832,8 @@
     for z in range(4):
         for h in range(2):
             cols = pl.ds((2 * z + h) * DH, DH)
-            gk_home[:, cols] = k_col[z, h, :, :DH]
-            gv_home[:, cols] = k_col[z, h, :, DH:]
+            home[1, :, cols] = k_col[z, h, :, :DH]
+            home[2, :, cols] = k_col[z, h, :, DH:]
     block_bytes_wait(dq_ref.at[pl.ds(0, shards - 1)], recv_sem.at[3])
     block_bytes_wait(o_ref.at[pl.ds(0, shards - 1)], send_sem.at[0])
     for k in range(3):
@@ -833,13 +862,12 @@
     return pl.pallas_call(
         home_kernel,
         out_shape=(
-            jax.ShapeDtypeStruct((slots, width), bf16),
-            jax.ShapeDtypeStruct((slots, width), bf16),
-            jax.ShapeDtypeStruct((slots, width), bf16),
+            jax.ShapeDtypeStruct((3, slots, width), bf16),
             jax.ShapeDtypeStruct((out_rows, width), jnp.float32),
         ),
-        in_specs=[pl.BlockSpec(memory_space=pltpu.HBM)] * 7,
-        out_specs=(vmem,) * 4,
+        in_specs=[pl.BlockSpec(memory_space=pltpu.HBM)] * 3
+        + [pl.BlockSpec(memory_space=pl.ANY)] * 4,
+        out_specs=(vmem,) * 2,
         scratch_shapes=[
             pltpu.VMEM((4, slots, rows), bf16),
             pltpu.VMEM((4, 4, slots, 2 * DH), bf16),
@@ -869,7 +897,7 @@
             pltpu.SemaphoreType.DMA((4, CHUNKS)),
         ],
         compiler_params=pltpu.CompilerParams(
-            collective_id=1, has_side_effects=True, vmem_limit_bytes=48 * 1024 * 1024
+            collective_id=1, has_side_effects=True, vmem_limit_bytes=VMEM_BYTES
         ),
         name="home",
     )(o_back, dq_back, key_back, *grad_parts)
@@ -905,12 +933,14 @@
         return jnp.dot(which, values, preferred_element_type=jnp.float32).astype(jnp.bfloat16)
 
     grad_local = pick(dealt_selector, output_gradient)
-    query = pick(dealt_selector, projections[:, 0])
-    key = pick(selector, projections[:, 1])
-    value = pick(selector, projections[:, 2])
 
     *blocks, query_in, grad_in, key_in, value_in = spread(
-        grad_local, query, key, value, output_projection_weight, seq_count
+        grad_local,
+        dealt_selector,
+        selector,
+        projections.transpose(1, 0, 2),
+        output_projection_weight,
+        seq_count,
     )
 
     def along_z(k):
@@ -925,17 +955,14 @@
         surviving_token_count, my_quarter, query_in, grad_in, key_in, value_in
     )
     out_rows = output_projection_weight.shape[0] // seq_count
-    grad_query, grad_key, grad_value, weight_grad = bring_home(
-        o_back, dq_back, key_back, grad_parts, out_rows
+    grad_packed, weight_grad = bring_home(o_back, dq_back, key_back, grad_parts, out_rows)
+    projection_grad = lax.dot_general(
+        jnp.stack([dealt_selector, selector, selector]),
+        grad_packed,
+        (((1,), (1,)), ((0,), (0,))),
+        preferred_element_type=jnp.float32,
     )
-    projection_grad = jnp.stack(
-        [
-            contract_rows(dealt_selector, grad_query).astype(jnp.bfloat16),
-            contract_rows(selector, grad_key).astype(jnp.bfloat16),
-            contract_rows(selector, grad_value).astype(jnp.bfloat16),
-        ],
-        axis=1,
-    )
+    projection_grad = projection_grad.astype(jnp.bfloat16).transpose(1, 0, 2)
     return (projection_grad, weight_grad)
 
 

time: 136 us -> 129 us (0.949)
  Pallas kernels: 118 us -> 114 us
  matrix products: 7.2 us -> 5.28 us
    pallas_call x1, Pallas kernels: 29.5 us -> 23.6 us  [attend(): pl.pallas_call(attend_kernel, out_shape=(jax.ShapeDtypeStruct((shards, pa...]
    dot_general x4 -> x1, matrix products: 5.52 us -> 1.24 us  [pick(): jnp.dot(which, values, preferred_element_type=jnp.float32)]
    dot_general x3 -> x1, matrix products: 1.68 us -> 4.04 us  [on_device(): lax.dot_general(jnp.stack([dealt_selector, selector, selector]), grad_pac...]
    another operation x1 -> x0, other arithmetic: 2 us -> none  [on_device(): jnp.stack([contract_rows(dealt_selector, grad_query).astype(jnp.bfloat16)...]
  transfers between devices with their start and end apart: 3 -> 3, of which waited for: 0 -> 0; matrix products, arithmetic and copies ran while one was open for 0% -> 0% of each run, Pallas kernels for 22% -> 18%
where the time goes in v8:
time: 129 us; the launch traced here: 128 us
  Pallas kernels  114 us (88%)
  matrix products  5.28 us (4%)
  starting transfers between devices  3.64 us (3%)
  local copies, waits for them, and re-layouts  2.6 us (2%)
  other arithmetic  2.41 us (2%)
    pallas_call x1, Pallas kernels, bring_home(): pl.pallas_call(home_kernel, out_shape=(jax.ShapeDtypeStruct((3, slots, wi...  51.5 us
    pallas_call x1, Pallas kernels, spread(): pl.pallas_call(spread_kernel, out_shape=(block,) * 4 + (small,) * 2 + (la...  38.8 us
    pallas_call x1, Pallas kernels, attend(): pl.pallas_call(attend_kernel, out_shape=(jax.ShapeDtypeStruct((shards, pa...  23.6 us
    dot_general x1, matrix products, on_device(): lax.dot_general(jnp.stack([dealt_selector, selector, selector]), grad_pac...  4.04 us
    ppermute x3, starting transfers between devices, along_z(): lax.ppermute(blocks[k], 'seq', [(i, (i + 8 * k) % seq_count) for i in ran...  3.64 us
  transfers between devices with their start and end apart: 3, of which 0 were waited for; matrix products, arithmetic and copies ran while one was open for 0% of the time, Pallas kernels for 18%

profile of v8, /device:TPU:1, one launch (start us, length us, event | category | flops | bytes accessed | tf_op | source)
XLA Modules:
  0.0 128.5 jit_solution(7676134242398039801)
XLA Ops:
  0.6 0.0 copy-start
  0.6 0.0 copy-start.5
  0.7 0.5 broadcast.44
  1.2 1.3 %reduce.3 = s32[192]{0:T(256)S(1)} reduce(s32[1,192]{1,0:T(1,128)} %param.8, s32[]{:T(128)} %broadcast.44), dimensions={0}, to_apply=%param.8.reduce_sub_computation.3 | reduce | bytes 1540 | tf_op args[3]
  2.5 0.1 reshape_squeeze.3
  2.6 0.1 eq.57
  2.7 0.0 copy-done
  2.7 1.2 convolution_convert_fusion.grad_ref
  4.0 0.0 copy-done.5
  4.0 0.9 fusion.5
  4.9 38.8 %spread.1 = (bf16[192,1280]{1,0:T(8,128)(2,1)}, bf16[192,1280]{1,0:T(8,128)(2,1)}, bf16[192,1280]{1,0:T(8,128)(2,1)}, bf16[192,1280]{1,0:T(8,128)(2,1)}, bf16[32...) custom-call(bf16[192,1280]{1,0:T(8,128)(2,1)} %convolution_convert_f, ...), custom_call_target="tpu_custom_call" | custom-call | tf_op jit(solution)/shard_map/spread/pallas_call | solution.py:538
  43.6 0.4 collective-permute-start
  44.1 2.1 %collective-permute-start.1 = (bf16[192,1280]{1,0:T(8,128)(2,1)}, bf16[192,1280]{1,0:T(8,128)(2,1)S(1)}, u32[]{:S(2)}, u32[]{:S(2)}) collective-permute-start(bf16[192,1280]{1,0:T(8,128)(2,1)} %get-tuple-element.24), channel_id=1, source_target_pairs={{0,64},{4,68},{8,72},{12,76},{16,80},{20,84},{24,88},{28,92},{32,9... | collective-permute-start | bytes 1474568 | tf_op jit(solution)/shard_map/ppermute | solution.py:949
  46.2 1.1 collective-permute-start.2
  47.3 0.2 iota_compare_fusion.3
  47.5 23.6 %attend.1 = (bf16[32,48,128]{2,1,0:T(8,128)(2,1)}, bf16[32,48,128]{2,1,0:T(8,128)(2,1)}, bf16[32,192,256]{2,1,0:T(8,128)(2,1)}) custom-call(s32[32]{0:T(128)} %count_ref.1, s32[1]{0:T(128)} %bitcast.2.quarter_ref, bf16[32,48,128]{2,1,0:T(8,128)(2,1)} %get-tuple-element.15.q_hbm, bf16[32,48,128]{2,1,0:T(8,128)(2,1)} %get-tuple-element.16.g_hbm, ...), custom_call_target="tpu_custom_call" | custom-call | flops 7247757312 | bytes 16777216 | tf_op jit(solution)/shard_map/attend/pallas_call | solution.py:223
  71.0 0.0 collective-permute-done.g1_ref
  71.0 0.0 copy-start.2
  71.1 0.0 collective-permute-done.1.g2_ref
  71.1 0.0 copy-start.3
  71.1 0.0 collective-permute-done.2.g3_ref
  71.1 0.0 copy-start.4
  71.1 0.7 copy-done.2
  71.8 0.2 copy-done.3
  72.0 0.1 copy-done.4
  72.1 51.5 %home.1 = (bf16[3,192,1024]{2,1,0:T(8,128)(2,1)}, f32[160,1024]{1,0:T(8,128)}) custom-call(bf16[32,48,128]{2,1,0:T(8,128)(2,1)} %get-tuple-element.19.o_ref, bf16[32,48,128]{2,1,0:T(8,128)(2,1)} %get-tuple-element.20.dq_ref, bf16[4,4,2,192,256]{4,3,2,1,0:T(8,128)(2,1)} %bitcast.14, bf16[192,1280]{1,0:T(8,128)(2,1)} %get-tuple-element.22.g0_ref, ...), custom_call_target="tpu_custom_call" | custom-call | tf_op jit(solution)/shard_map/home/pallas_call | solution.py:862
  123.6 0.0 copy-start.1
  123.6 4.0 %convert_bitcast_fusion = bf16[512,3,1024]{2,0,1:T(8,128)(2,1)} fusion(bf16[3,192,1024]{2,1,0:T(8,128)(2,1)} %get-tuple-element.26, pred[1,192,512]{2,1,0:T(32,128)(4,1)S(1)} %get-tuple-element.30, pred[1,192,512]{2,1,0:T(32,128)(4,1)S(1)} %get-tuple-element.31), kind=kOutput, calls=%fused_computation | convolution fusion | flops 606142464 | bytes 4521984 | tf_op jit(solution)/shard_map/dot_general | solution.py:959
  127.7 0.0 copy-done.1
  127.7 0.8 copy.15
  (2 shorter events, 0.0 us)
Async XLA Ops:
  0.6 2.1 %copy-start = (bf16[512,1280]{1,0:T(8,128)(2,1)S(1)}, bf16[512,1280]{1,0:T(8,128)(2,1)}, u32[]{:S(2)}) copy-start(bf16[512,1280]{1,0:T(8,128)(2,1)} %param.6) | copy-start | bytes 3932164
  0.6 3.3 %copy-start.5 = (s32[1,192]{1,0:T(1,128)S(1)}, s32[1,192]{1,0:T(1,128)}, u32[]{:S(2)}) copy-start(s32[1,192]{1,0:T(1,128)} %param.8) | copy-start | bytes 2308
  43.6 27.4 %collective-permute-start = (bf16[192,1280]{1,0:T(8,128)(2,1)}, bf16[192,1280]{1,0:T(8,128)(2,1)S(1)}, u32[]{:S(2)}, u32[]{:S(2)}) collective-permute-start(bf16[192,1280]{1,0:T(8,128)(2,1)} %get-tuple-element.23), channel_id=1, source_target_pairs={{0,32},{4,36},{8,40},{12,44},{16,48},{20,52},{24,56},{28,60},{32,6... | collective-permute-start | bytes 1474568 | tf_op jit(solution)/shard_map/ppermute | solution.py:949
  44.1 27.0 %collective-permute-start.1 = (bf16[192,1280]{1,0:T(8,128)(2,1)}, bf16[192,1280]{1,0:T(8,128)(2,1)S(1)}, u32[]{:S(2)}, u32[]{:S(2)}) collective-permute-start(bf16[192,1280]{1,0:T(8,128)(2,1)} %get-tuple-element.24), channel_id=1, source_target_pairs={{0,64},{4,68},{8,72},{12,76},{16,80},{20,84},{24,88},{28,92},{32,9... | collective-permute-start | bytes 1474568 | tf_op jit(solution)/shard_map/ppermute | solution.py:949
  46.2 24.9 %collective-permute-start.2 = (bf16[192,1280]{1,0:T(8,128)(2,1)}, bf16[192,1280]{1,0:T(8,128)(2,1)S(1)}, u32[]{:S(2)}, u32[]{:S(2)}) collective-permute-start(bf16[192,1280]{1,0:T(8,128)(2,1)} %get-tuple-element.25), channel_id=1, source_target_pairs={{0,96},{4,100},{8,104},{12,108},{16,112},{20,116},{24,120},{28,124... | collective-permute-start | bytes 1474568 | tf_op jit(solution)/shard_map/ppermute | solution.py:949
  71.0 0.8 copy-start.2
  71.1 0.9 copy-start.3
  71.1 1.1 copy-start.4
  123.6 4.1 %copy-start.1 = (f32[160,1024]{1,0:T(8,128)S(1)}, f32[160,1024]{1,0:T(8,128)}, u32[]{:S(2)}) copy-start(f32[160,1024]{1,0:T(8,128)} %get-tuple-element.35) | copy-start | bytes 1966084

commit v9 on v8

--- a/solution.py
+++ b/solution.py
@@ -10,6 +10,7 @@
 DH = 128
 BQ = 256
 BK = 1536
+TAIL = 512
 GROUP = 16
 NEG = -1e30
 CHUNKS = 4
@@ -91,10 +92,23 @@
         lane = lax.broadcasted_iota(jnp.int32, (rows, DH), 1)
         return jnp.where((row >= live) & (lane == 0), NEG, 0.0).astype(bf16)
 
+    def live_groups(s):
+        live = (count_ref[s] + GROUP - 1) // GROUP
+        first = lax.rem(quarter + s, 4)
+        return live, first, (live - first + 3) // 4
+
+    rows_live = GROUP * lax.fori_loop(0, shards, lambda s, n: n + live_groups(s)[2], jnp.int32(0))
+    blocks = (rows_live + BQ - 1) // BQ
+    end_q = blocks * BQ
+    start_q = pl.multiple_of(end_q - rows_live, GROUP)
+    qc[pl.ds(0, BQ), :] = jnp.zeros((BQ, DH), bf16)
+    gc[pl.ds(0, BQ), :] = jnp.zeros((BQ, DH), bf16)
+    qpos[pl.ds(0, BQ), :] = jnp.zeros((BQ, DH), jnp.int32)
+    group_pos[0] = 0
+
     def pack(s, carry):
         at_k, at_q = carry
-        live = (count_ref[s] + GROUP - 1) // GROUP
-        first = lax.rem(quarter + s, 4)
+        live, first, mine = live_groups(s)
         at_k = pl.multiple_of(at_k, GROUP)
         at_q = pl.multiple_of(at_q, GROUP)
         kc[pl.ds(at_k, slots), :DH] = k_ref[s]
@@ -107,19 +121,14 @@
             base = at_k + (first + 4 * i) * GROUP
             qpos[pl.ds(at_q + i * GROUP, GROUP), :] = base + rows
             group_pos[at_q // GROUP + i] = base
-        return at_k + live * GROUP, at_q + (live - first + 3) // 4 * GROUP
-
-    end_k, end_q = lax.fori_loop(0, shards, pack, (jnp.int32(0), jnp.int32(0)))
+        return at_k + live * GROUP, at_q + mine * GROUP
+
+    end_k, _ = lax.fori_loop(0, shards, pack, (jnp.int32(0), start_q))
     end_k = pl.multiple_of(end_k, GROUP)
-    end_q = pl.multiple_of(end_q, GROUP)
     kc[pl.ds(end_k, BK), :DH] = jnp.zeros((BK, DH), bf16)
     kc[pl.ds(end_k, BK), DH:] = dead_marks(BK, 0)
     vc[pl.ds(end_k, BK), :] = jnp.zeros((BK, DH), bf16)
-    qc[pl.ds(end_q, BQ), :] = jnp.zeros((BQ, DH), bf16)
-    gc[pl.ds(end_q, BQ), :] = jnp.zeros((BQ, DH), bf16)
-    qpos[pl.ds(end_q, BQ), :] = jnp.zeros((BQ, DH), jnp.int32)
-    blocks = (end_q + BQ - 1) // BQ
-    oc[pl.ds(pl.multiple_of(blocks * BQ, BQ), part_rows), :] = jnp.zeros(
+    oc[pl.ds(pl.multiple_of(end_q, BQ), part_rows), :] = jnp.zeros(
         (part_rows, 2 * DH), bf16
     )
 
@@ -133,36 +142,48 @@
 
     def block(b, carry):
         rows = pl.ds(pl.multiple_of(b * BQ, BQ), BQ)
-        last_group = jnp.minimum((b + 1) * (BQ // GROUP), end_q // GROUP) - 1
-        chunks = (group_pos[last_group] + GROUP + BK - 1) // BK
-        clear_chunks = (group_pos[b * (BQ // GROUP)] + 1) // BK
+        key_end = group_pos[(b + 1) * (BQ // GROUP) - 1] + GROUP
+        chunks = (key_end + TAIL - 1) // BK
+        tails = (jnp.maximum(key_end - chunks * BK, 0) + TAIL - 1) // TAIL
+        first_end = jnp.where(b == 0, 0, group_pos[b * (BQ // GROUP)] + 1)
+        clear_chunks = jnp.minimum(first_end // BK, chunks)
+
+        def over(body, carry):
+            carry = lax.fori_loop(0, chunks, lambda c, x: body(c * BK, BK, x), carry)
+            return lax.fori_loop(
+                0, tails, lambda c, x: body(chunks * BK + c * TAIL, TAIL, x), carry
+            )
+
         q_turned[:DH, :] = qc[rows, :].T
         last_key = qpos[rows, :].T[0:1, :]
 
-        def score(c, top, masked):
-            at = pl.multiple_of(c * BK, BK)
-            keys = pl.ds(at, BK)
+        def score(at, size, top, masked):
+            at = pl.multiple_of(at, TAIL)
+            keys = pl.ds(at, size)
             s = jnp.dot(kc[keys, :], q_turned[...], preferred_element_type=jnp.float32)
             if masked:
-                key = at + lax.broadcasted_iota(jnp.int32, (BK, BQ), 0)
+                key = at + lax.broadcasted_iota(jnp.int32, (size, BQ), 0)
                 s = jnp.where(key <= last_key, s, NEG)
             s_scr[keys, :] = s
             return jnp.maximum(top, jnp.max(s, axis=0, keepdims=True))
 
         top = jnp.full((1, BQ), NEG, jnp.float32)
-        top = lax.fori_loop(0, clear_chunks, lambda c, t: score(c, t, False), top)
-        top = lax.fori_loop(clear_chunks, chunks, lambda c, t: score(c, t, True), top)
+        top = lax.fori_loop(0, clear_chunks, lambda c, t: score(c * BK, BK, t, False), top)
+        top = lax.fori_loop(clear_chunks, chunks, lambda c, t: score(c * BK, BK, t, True), top)
+        top = lax.fori_loop(
+            0, tails, lambda c, t: score(chunks * BK + c * TAIL, TAIL, t, True), top
+        )
         acc[...] = jnp.zeros((DH, BQ), jnp.float32)
 
-        def weigh(c, total):
-            keys = pl.ds(pl.multiple_of(c * BK, BK), BK)
+        def weigh(at, size, total):
+            keys = pl.ds(pl.multiple_of(at, TAIL), size)
             p = jnp.exp2((s_scr[keys, :] - top) * log2e)
             p_low = p.astype(bf16)
             p_scr[keys, :] = p_low
             acc[...] += jnp.dot(v_turned[:, keys], p_low, preferred_element_type=jnp.float32)
             return total + jnp.sum(p, axis=0, keepdims=True)
 
-        total = lax.fori_loop(0, chunks, weigh, jnp.zeros((1, BQ), jnp.float32))
+        total = over(weigh, jnp.zeros((1, BQ), jnp.float32))
         inverse = 1.0 / total
         attended = acc[...] * inverse
         oc[rows, DH:] = attended.T.astype(bf16)
@@ -171,8 +192,8 @@
         g_part = g_turned.T
         acc[...] = jnp.zeros((DH, BQ), jnp.float32)
 
-        def back(c, carry):
-            keys = pl.ds(pl.multiple_of(c * BK, BK), BK)
+        def back(at, size, carry):
+            keys = pl.ds(pl.multiple_of(at, TAIL), size)
             p_low = p_scr[keys, :]
             grad_probs = jnp.dot(vc[keys, :], g_turned, preferred_element_type=jnp.float32)
             ds = (p_low.astype(jnp.float32) * (grad_probs - row_dot)).astype(bf16)
@@ -181,7 +202,7 @@
             dvc[keys, :] += jnp.dot(p_low, g_part, preferred_element_type=jnp.float32)
             return carry
 
-        lax.fori_loop(0, chunks, back, 0)
+        over(back, 0)
         oc[rows, :DH] = (acc[...] * score_scale).T.astype(bf16)
         return carry
 
@@ -189,8 +210,7 @@
 
     def unpack(s, carry):
         at_k, at_q = carry
-        live = (count_ref[s] + GROUP - 1) // GROUP
-        first = lax.rem(quarter + s, 4)
+        live, first, mine = live_groups(s)
         at_k = pl.multiple_of(at_k, GROUP)
         at_q = pl.multiple_of(at_q, GROUP)
         q_ref[s] = oc[pl.ds(at_q, part_rows), :DH]
@@ -198,9 +218,9 @@
         k_stage[s, :, :DH] = (dkc[pl.ds(at_k, slots), :] * score_scale).astype(bf16)
         k_stage[s, :, DH:] = dvc[pl.ds(at_k, slots), :].astype(bf16)
         pltpu.make_async_copy(k_stage.at[s], k_out.at[s], store_sem.at[0]).start()
-        return at_k + live * GROUP, at_q + (live - first + 3) // 4 * GROUP
-
-    lax.fori_loop(0, shards, unpack, (jnp.int32(0), jnp.int32(0)))
+        return at_k + live * GROUP, at_q + mine * GROUP
+
+    lax.fori_loop(0, shards, unpack, (jnp.int32(0), start_q))
     stores = [
         pltpu.make_async_copy(q_ref, dq_out, store_sem.at[1]),
         pltpu.make_async_copy(g_ref, o_out, store_sem.at[2]),
@@ -303,10 +323,14 @@
     return copy
 
 
+def dealt_rows(group, first, part_rows):
+    at = lax.rem(group + 4 - first, 4) * part_rows + group // 4 * GROUP
+    return pl.ds(pl.multiple_of(at, GROUP), GROUP)
+
+
 def spread_kernel(
-    grad_ref,
-    dealt_ref,
-    select_ref,
+    all_grad_ref,
+    kept_ref,
     p_hbm,
     w_hbm,
     g0_out,
@@ -319,6 +343,8 @@
     v_in,
     w_ref,
     p_ref,
+    select,
+    grad_ref,
     q_ref,
     k_ref,
     v_ref,
@@ -363,16 +389,30 @@
     tiles = acc.shape[1] // width
 
     def pick():
+        token = lax.broadcasted_iota(jnp.int32, select.shape, 0)
+        select[...] = jnp.where(token == kept_ref[...], 1.0, 0.0).astype(jnp.bfloat16)
+
+        def deal(out, at, values):
+            for g in range(slots // GROUP):
+                out[dealt_rows(g, me % 4, part_rows), at] = values[g * GROUP : (g + 1) * GROUP]
+
+        def grad_tile(j, carry):
+            at = pl.ds(pl.multiple_of(j * width, width), width)
+            picked = contract_rows(select[...], all_grad_ref[:, at])
+            deal(grad_ref, at, picked.astype(jnp.bfloat16))
+            return carry
+
+        lax.fori_loop(0, cols // width, grad_tile, 0)
         load_p.wait()
 
         def tile(j, carry):
             at = pl.ds(pl.multiple_of(j * width, width), width)
-            for i, (which, out) in enumerate(
-                ((dealt_ref, q_ref), (select_ref, k_ref), (select_ref, v_ref))
-            ):
-                out[:, at] = jnp.dot(
-                    which[...], p_ref[i, :, at], preferred_element_type=jnp.float32
-                ).astype(jnp.bfloat16)
+            picked = [
+                contract_rows(select[...], p_ref[i, :, at]).astype(jnp.bfloat16) for i in range(3)
+            ]
+            deal(q_ref, at, picked[0])
+            k_ref[:, at] = picked[1]
+            v_ref[:, at] = picked[2]
             return carry
 
         lax.fori_loop(0, tiles, tile, 0)
@@ -526,8 +566,9 @@
     block_bytes_wait(g_in.at[others], q_send.at[1])
 
 
-def spread(grad_local, dealt_selector, selector, projections, weight, shards):
-    slots, cols = grad_local.shape
+def spread(output_gradient, kept, projections, weight, shards):
+    tokens, cols = output_gradient.shape
+    slots = kept.shape[1]
     depth, width = weight.shape
     part_rows = slots // 4
     bf16 = jnp.bfloat16
@@ -538,11 +579,13 @@
     *blocks, query_in, grad_in, key_in, value_in = pl.pallas_call(
         spread_kernel,
         out_shape=(block,) * 4 + (small,) * 2 + (large,) * 2,
-        in_specs=[vmem] * 3 + [pl.BlockSpec(memory_space=pltpu.HBM)] * 2,
+        in_specs=[vmem] * 2 + [pl.BlockSpec(memory_space=pltpu.HBM)] * 2,
         out_specs=(pl.BlockSpec(memory_space=pltpu.HBM),) * 8,
         scratch_shapes=[
             pltpu.VMEM((depth, width), bf16),
             pltpu.VMEM(projections.shape, bf16),
+            pltpu.VMEM((tokens, slots), bf16),
+            pltpu.VMEM((slots, cols), bf16),
             pltpu.VMEM((slots, width), bf16),
             pltpu.VMEM((slots, width), bf16),
             pltpu.VMEM((slots, width), bf16),
@@ -571,7 +614,7 @@
             collective_id=2, has_side_effects=True, vmem_limit_bytes=VMEM_BYTES
         ),
         name="spread",
-    )(grad_local, dealt_selector, selector, projections, weight)
+    )(output_gradient, kept, projections, weight)
     key_in = key_in.reshape(shards, slots, DH)
     value_in = value_in.reshape(shards, slots, DH)
     return (*blocks, query_in, grad_in, key_in, value_in)
@@ -897,10 +940,48 @@
             pltpu.SemaphoreType.DMA((4, CHUNKS)),
         ],
         compiler_params=pltpu.CompilerParams(
-            collective_id=1, has_side_effects=True, vmem_limit_bytes=VMEM_BYTES
+            collective_id=1, has_side_effects=True, vmem_limit_bytes=48 * 1024 * 1024
         ),
         name="home",
     )(o_back, dq_back, key_back, *grad_parts)
+
+
+def scatter_kernel(first_ref, kept_ref, packed_ref, out_ref, rows_ref):
+    slots = rows_ref.shape[0]
+
+    @pl.when(pl.program_id(0) == 0)
+    def _():
+        for g in range(slots // GROUP):
+            dealt = dealt_rows(g, first_ref[0], slots // 4)
+            rows_ref[g * GROUP : (g + 1) * GROUP, :] = packed_ref[0, dealt, :]
+
+    @pl.when(pl.program_id(0) > 0)
+    def _():
+        rows_ref[...] = packed_ref[0]
+
+    token = lax.broadcasted_iota(jnp.int32, (out_ref.shape[1], slots), 0)
+    select = jnp.where(token == kept_ref[...], 1.0, 0.0).astype(jnp.bfloat16)
+    out_ref[0] = jnp.dot(
+        select, rows_ref[...], preferred_element_type=jnp.float32
+    ).astype(jnp.bfloat16)
+
+
+def scatter(first, kept, packed, tokens):
+    parts, slots, width = packed.shape
+    return pl.pallas_call(
+        scatter_kernel,
+        grid=(parts,),
+        out_shape=jax.ShapeDtypeStruct((parts, tokens, width), jnp.bfloat16),
+        in_specs=[
+            pl.BlockSpec(memory_space=pltpu.SMEM),
+            pl.BlockSpec((1, slots), lambda i: (0, 0)),
+            pl.BlockSpec((1, slots, width), lambda i: (i, 0, 0)),
+        ],
+        out_specs=pl.BlockSpec((1, tokens, width), lambda i: (i, 0, 0)),
+        scratch_shapes=[pltpu.VMEM((slots, width), jnp.bfloat16)],
+        compiler_params=pltpu.CompilerParams(vmem_limit_bytes=32 * 1024 * 1024),
+        name="scatter",
+    )(first, kept, packed)
 
 
 def on_device(
@@ -920,24 +1001,9 @@
     me = lax.axis_index("seq")
     my_quarter = (me % quarters).astype(jnp.int32)[None]
 
-    kept = kept_token_indices[0]
-    dealt = kept.reshape(part_rows // GROUP, quarters, GROUP).transpose(1, 0, 2)
-    dealt = lax.dynamic_slice_in_dim(
-        jnp.concatenate([dealt, dealt], axis=0), me % quarters, quarters, axis=0
-    ).reshape(slots)
-    token = jnp.arange(tok_dev, dtype=jnp.int32)[None, :]
-    selector = (kept[:, None] == token).astype(jnp.bfloat16)
-    dealt_selector = (dealt[:, None] == token).astype(jnp.bfloat16)
-
-    def pick(which, values):
-        return jnp.dot(which, values, preferred_element_type=jnp.float32).astype(jnp.bfloat16)
-
-    grad_local = pick(dealt_selector, output_gradient)
-
     *blocks, query_in, grad_in, key_in, value_in = spread(
-        grad_local,
-        dealt_selector,
-        selector,
+        output_gradient,
+        kept_token_indices,
         projections.transpose(1, 0, 2),
         output_projection_weight,
         seq_count,
@@ -956,13 +1022,8 @@
     )
     out_rows = output_projection_weight.shape[0] // seq_count
     grad_packed, weight_grad = bring_home(o_back, dq_back, key_back, grad_parts, out_rows)
-    projection_grad = lax.dot_general(
-        jnp.stack([dealt_selector, selector, selector]),
-        grad_packed,
-        (((1,), (1,)), ((0,), (0,))),
-        preferred_element_type=jnp.float32,
-    )
-    projection_grad = projection_grad.astype(jnp.bfloat16).transpose(1, 0, 2)
+    projection_grad = scatter(my_quarter, kept_token_indices, grad_packed, tok_dev)
+    projection_grad = projection_grad.transpose(1, 0, 2)
     return (projection_grad, weight_grad)
 
 

time: 129 us -> 122 us (0.946)
  matrix products: 5.28 us -> 0 us
  other arithmetic: 2.41 us -> 0 us
    dot_general x2 -> x0, matrix products: 5.28 us -> none  [the longest x1 4.04 us: on_device(): lax.dot_general(jnp.stack([dealt_selector, selector, selector]), grad_pac...]
    pallas_call x0 -> x1, Pallas kernels: none -> 2.9 us  [scatter(): pl.pallas_call(scatter_kernel, grid=(parts,), out_shape=jax.ShapeDtypeStr...]
    pallas_call x1, Pallas kernels: 51.5 us -> 49.5 us  [bring_home(): pl.pallas_call(home_kernel, out_shape=(jax.ShapeDtypeStruct((3, slots, wi...]
    unnamed x1 -> x0, other arithmetic: 1.34 us -> none
    unnamed x14 -> x9, local copies, waits for them, and re-layouts: 2.42 us -> 2.83 us
  transfers between devices with their start and end apart: 3 -> 3, of which waited for: 0 -> 0; matrix products, arithmetic and copies ran while one was open for 0% -> 0% of each run, Pallas kernels for 18% -> 19%
where the time goes in v9:
time: 122 us
  Pallas kernels  115 us (94%)
  starting transfers between devices  3.64 us (3%)
  local copies, waits for them, and re-layouts  2.83 us (2%)
    pallas_call x1, Pallas kernels, bring_home(): pl.pallas_call(home_kernel, out_shape=(jax.ShapeDtypeStruct((3, slots, wi...  49.5 us
    pallas_call x1, Pallas kernels, spread(): pl.pallas_call(spread_kernel, out_shape=(block,) * 4 + (small,) * 2 + (la...  39 us
    pallas_call x1, Pallas kernels, attend(): pl.pallas_call(attend_kernel, out_shape=(jax.ShapeDtypeStruct((shards, pa...  23.2 us
    ppermute x3, starting transfers between devices, along_z(): lax.ppermute(blocks[k], 'seq', [(i, (i + 8 * k) % seq_count) for i in ran...  3.64 us
    pallas_call x1, Pallas kernels, scatter(): pl.pallas_call(scatter_kernel, grid=(parts,), out_shape=jax.ShapeDtypeStr...  2.9 us
    unnamed x9, local copies, waits for them, and re-layouts  2.83 us
  transfers between devices with their start and end apart: 3, of which 0 were waited for; matrix products, arithmetic and copies ran while one was open for 0% of the time, Pallas kernels for 19%

profile of v9, /device:TPU:1, one launch (start us, length us, event | category | flops | bytes accessed | tf_op | source)
XLA Modules:
  0.0 121.8 jit_solution(4504666593471659668)
XLA Ops:
  0.6 39.0 %spread.1 = (bf16[192,1280]{1,0:T(8,128)(2,1)}, bf16[192,1280]{1,0:T(8,128)(2,1)}, bf16[192,1280]{1,0:T(8,128)(2,1)}, bf16[192,1280]{1,0:T(8,128)(2,1)}, bf16[32...) custom-call(bf16[512,1280]{1,0:T(8,128)(2,1)} %all_grad_ref.1, ...), custom_call_target="tpu_custom_call" | custom-call | tf_op jit(solution)/shard_map/spread/pallas_call | solution.py:579
  39.6 0.4 collective-permute-start
  40.1 2.2 %collective-permute-start.1 = (bf16[192,1280]{1,0:T(8,128)(2,1)}, bf16[192,1280]{1,0:T(8,128)(2,1)S(1)}, u32[]{:S(2)}, u32[]{:S(2)}) collective-permute-start(bf16[192,1280]{1,0:T(8,128)(2,1)} %get-tuple-element.24), channel_id=1, source_target_pairs={{0,64},{4,68},{8,72},{12,76},{16,80},{20,84},{24,88},{28,92},{32,9... | collective-permute-start | bytes 1474568 | tf_op jit(solution)/shard_map/ppermute | solution.py:1015
  42.3 0.9 collective-permute-start.2
  43.3 0.0 copy-start
  43.3 23.2 %attend.1 = (bf16[32,48,128]{2,1,0:T(8,128)(2,1)}, bf16[32,48,128]{2,1,0:T(8,128)(2,1)}, bf16[32,192,256]{2,1,0:T(8,128)(2,1)}) custom-call(s32[32]{0:T(128)} %count_ref.1, s32[1]{0:T(128)} %bitcast.quarter_ref.first_ref, bf16[32,48,128]{2,1,0:T(8,128)(2,1)} %get-tuple-element.15.q_hbm, bf16[32,48,128]{2,1,0:T(8,128)(2,1)} %get-tuple-element.16.g_hbm, ...), custom_call_target="tpu_custom_call" | custom-call | flops 7247757312 | bytes 16777216 | tf_op jit(solution)/shard_map/attend/pallas_call | solution.py:243
  66.5 0.0 copy-start.3
  66.5 0.0 collective-permute-done.g1_ref
  66.5 0.0 collective-permute-done.1.g2_ref
  66.6 0.0 collective-permute-done.2.g3_ref
  66.6 0.0 copy-done
  66.6 0.0 copy-start.1
  66.6 1.0 copy-done.1
  67.6 0.0 copy-start.2
  67.6 1.0 copy-done.2
  68.6 49.5 %home.1 = (bf16[3,192,1024]{2,1,0:T(8,128)(2,1)S(1)}, f32[160,1024]{1,0:T(8,128)S(1)}) custom-call(bf16[32,48,128]{2,1,0:T(8,128)(2,1)S(1)} %copy-done.2, bf16[32,48,128]{2,1,0:T(8,128)(2,1)S(1)} %copy-done.1, bf16[4,4,2,192,256]{4,3,2,1,0:T(8,128)(2,1)} %bitcast.6, bf16[192,1280]{1,0:T(8,128)(2,1)S(1)} %copy-done, ...), custom_call_target="tpu_custom_call" | custom-call | tf_op jit(solution)/shard_map/home/pallas_call | solution.py:905
  118.0 0.0 copy-done.3
  118.0 2.9 %scatter.1 = bf16[3,512,1024]{2,1,0:T(8,128)(2,1)} custom-call(s32[1]{0:T(128)} %bitcast.quarter_ref.first_ref, s32[1,192]{1,0:T(1,128)S(1)} %copy-done.3, bf16[3,192,1024]{2,1,0:T(8,128)(2,1)S(1)} %get-tuple-element.26.packed_ref), custom_call_target="tpu_custom_call" | custom-call | tf_op jit(solution)/shard_map/scatter/pallas_call | solution.py:971
  120.9 0.8 copy.8
Async XLA Ops:
  39.6 26.9 %collective-permute-start = (bf16[192,1280]{1,0:T(8,128)(2,1)}, bf16[192,1280]{1,0:T(8,128)(2,1)S(1)}, u32[]{:S(2)}, u32[]{:S(2)}) collective-permute-start(bf16[192,1280]{1,0:T(8,128)(2,1)} %get-tuple-element.23), channel_id=1, source_target_pairs={{0,32},{4,36},{8,40},{12,44},{16,48},{20,52},{24,56},{28,60},{32,6... | collective-permute-start | bytes 1474568 | tf_op jit(solution)/shard_map/ppermute | solution.py:1015
  40.1 26.5 %collective-permute-start.1 = (bf16[192,1280]{1,0:T(8,128)(2,1)}, bf16[192,1280]{1,0:T(8,128)(2,1)S(1)}, u32[]{:S(2)}, u32[]{:S(2)}) collective-permute-start(bf16[192,1280]{1,0:T(8,128)(2,1)} %get-tuple-element.24), channel_id=1, source_target_pairs={{0,64},{4,68},{8,72},{12,76},{16,80},{20,84},{24,88},{28,92},{32,9... | collective-permute-start | bytes 1474568 | tf_op jit(solution)/shard_map/ppermute | solution.py:1015
  42.3 24.2 %collective-permute-start.2 = (bf16[192,1280]{1,0:T(8,128)(2,1)}, bf16[192,1280]{1,0:T(8,128)(2,1)S(1)}, u32[]{:S(2)}, u32[]{:S(2)}) collective-permute-start(bf16[192,1280]{1,0:T(8,128)(2,1)} %get-tuple-element.25), channel_id=1, source_target_pairs={{0,96},{4,100},{8,104},{12,108},{16,112},{20,116},{24,120},{28,124... | collective-permute-start | bytes 1474568 | tf_op jit(solution)/shard_map/ppermute | solution.py:1015
  43.3 23.3 %copy-start = (bf16[192,1280]{1,0:T(8,128)(2,1)S(1)}, bf16[192,1280]{1,0:T(8,128)(2,1)}, u32[]{:S(2)}) copy-start(bf16[192,1280]{1,0:T(8,128)(2,1)} %get-tuple-element.22.g0_ref) | copy-start | bytes 1474564
  66.5 51.5 %copy-start.3 = (s32[1,192]{1,0:T(1,128)S(1)}, s32[1,192]{1,0:T(1,128)}, u32[]{:S(2)}) copy-start(s32[1,192]{1,0:T(1,128)} %kept_ref.3) | copy-start | bytes 2308
  66.6 1.0 copy-start.1
  67.6 1.0 copy-start.2

commit v10 on v9

--- a/solution.py
+++ b/solution.py
@@ -14,7 +14,7 @@
 GROUP = 16
 NEG = -1e30
 CHUNKS = 4
-VMEM_BYTES = 60 * 1024 * 1024
+VMEM_BYTES = 63 * 1024 * 1024 + 640 * 1024
 K_STEP = 4
 DQ_STEP = 4
 
@@ -940,17 +940,21 @@
             pltpu.SemaphoreType.DMA((4, CHUNKS)),
         ],
         compiler_params=pltpu.CompilerParams(
-            collective_id=1, has_side_effects=True, vmem_limit_bytes=48 * 1024 * 1024
+            collective_id=1, has_side_effects=True, vmem_limit_bytes=VMEM_BYTES
         ),
         name="home",
     )(o_back, dq_back, key_back, *grad_parts)
 
 
-def scatter_kernel(first_ref, kept_ref, packed_ref, out_ref, rows_ref):
+def scatter_kernel(
+    first_ref, kept_ref, packed_ref, weight_ref, out_ref, weight_out, rows_ref, move_sem
+):
     slots = rows_ref.shape[0]
+    move = pltpu.make_async_copy(weight_ref, weight_out, move_sem)
 
     @pl.when(pl.program_id(0) == 0)
     def _():
+        move.start()
         for g in range(slots // GROUP):
             dealt = dealt_rows(g, first_ref[0], slots // 4)
             rows_ref[g * GROUP : (g + 1) * GROUP, :] = packed_ref[0, dealt, :]
@@ -965,23 +969,34 @@
         select, rows_ref[...], preferred_element_type=jnp.float32
     ).astype(jnp.bfloat16)
 
-
-def scatter(first, kept, packed, tokens):
+    @pl.when(pl.program_id(0) == pl.num_programs(0) - 1)
+    def _():
+        move.wait()
+
+
+def scatter(first, kept, packed, weight_grad, tokens):
     parts, slots, width = packed.shape
     return pl.pallas_call(
         scatter_kernel,
         grid=(parts,),
-        out_shape=jax.ShapeDtypeStruct((parts, tokens, width), jnp.bfloat16),
+        out_shape=(
+            jax.ShapeDtypeStruct((parts, tokens, width), jnp.bfloat16),
+            jax.ShapeDtypeStruct(weight_grad.shape, jnp.float32),
+        ),
         in_specs=[
             pl.BlockSpec(memory_space=pltpu.SMEM),
             pl.BlockSpec((1, slots), lambda i: (0, 0)),
             pl.BlockSpec((1, slots, width), lambda i: (i, 0, 0)),
+            pl.BlockSpec(memory_space=pl.ANY),
         ],
-        out_specs=pl.BlockSpec((1, tokens, width), lambda i: (i, 0, 0)),
-        scratch_shapes=[pltpu.VMEM((slots, width), jnp.bfloat16)],
-        compiler_params=pltpu.CompilerParams(vmem_limit_bytes=32 * 1024 * 1024),
+        out_specs=(
+            pl.BlockSpec((1, tokens, width), lambda i: (i, 0, 0)),
+            pl.BlockSpec(memory_space=pl.ANY),
+        ),
+        scratch_shapes=[pltpu.VMEM((slots, width), jnp.bfloat16), pltpu.SemaphoreType.DMA],
+        compiler_params=pltpu.CompilerParams(vmem_limit_bytes=VMEM_BYTES),
         name="scatter",
-    )(first, kept, packed)
+    )(first, kept, packed, weight_grad)
 
 
 def on_device(
@@ -1022,7 +1037,9 @@
     )
     out_rows = output_projection_weight.shape[0] // seq_count
     grad_packed, weight_grad = bring_home(o_back, dq_back, key_back, grad_parts, out_rows)
-    projection_grad = scatter(my_quarter, kept_token_indices, grad_packed, tok_dev)
+    projection_grad, weight_grad = scatter(
+        my_quarter, kept_token_indices, grad_packed, weight_grad, tok_dev
+    )
     projection_grad = projection_grad.transpose(1, 0, 2)
     return (projection_grad, weight_grad)
 

time: 122 us -> 143 us (1.17)
  Pallas kernels: 115 us -> 138 us
  local copies, waits for them, and re-layouts: 2.83 us -> 0 us
    pallas_call x1, Pallas kernels: 2.9 us -> 22.9 us  [scatter(): pl.pallas_call(scatter_kernel, grid=(parts,), out_shape=(jax.ShapeDtypeSt...]
    pallas_call x1, Pallas kernels: 23.2 us -> 26.2 us  [attend(): pl.pallas_call(attend_kernel, out_shape=(jax.ShapeDtypeStruct((shards, pa...]
    unnamed x9 -> x0, local copies, waits for them, and re-layouts: 2.83 us -> none
  transfers between devices with their start and end apart: 3 -> 3, of which waited for: 0 -> 0; matrix products, arithmetic and copies ran while one was open for 0% -> 0% of each run, Pallas kernels for 19% -> 18%
where the time goes in v10:
time: 143 us
  Pallas kernels  138 us (97%)
  starting transfers between devices  3.64 us (3%)
    pallas_call x1, Pallas kernels, bring_home(): pl.pallas_call(home_kernel, out_shape=(jax.ShapeDtypeStruct((3, slots, wi...  50.1 us
    pallas_call x1, Pallas kernels, spread(): pl.pallas_call(spread_kernel, out_shape=(block,) * 4 + (small,) * 2 + (la...  39 us
    pallas_call x1, Pallas kernels, attend(): pl.pallas_call(attend_kernel, out_shape=(jax.ShapeDtypeStruct((shards, pa...  26.2 us
    pallas_call x1, Pallas kernels, scatter(): pl.pallas_call(scatter_kernel, grid=(parts,), out_shape=(jax.ShapeDtypeSt...  22.9 us
    ppermute x3, starting transfers between devices, along_z(): lax.ppermute(blocks[k], 'seq', [(i, (i + 8 * k) % seq_count) for i in ran...  3.64 us
  transfers between devices with their start and end apart: 3, of which 0 were waited for; matrix products, arithmetic and copies ran while one was open for 0% of the time, Pallas kernels for 18%

profile of v10, /device:TPU:1, one launch (start us, length us, event | category | flops | bytes accessed | tf_op | source)
XLA Modules:
  0.0 142.6 jit_solution(16160516990399623319)
XLA Ops:
  0.6 39.0 %spread.1 = (bf16[192,1280]{1,0:T(8,128)(2,1)}, bf16[192,1280]{1,0:T(8,128)(2,1)}, bf16[192,1280]{1,0:T(8,128)(2,1)}, bf16[192,1280]{1,0:T(8,128)(2,1)}, bf16[32...) custom-call(bf16[512,1280]{1,0:T(8,128)(2,1)} %all_grad_ref.1, ...), custom_call_target="tpu_custom_call" | custom-call | tf_op jit(solution)/shard_map/spread/pallas_call | solution.py:579
  39.6 0.4 collective-permute-start
  40.1 2.2 %collective-permute-start.1 = (bf16[192,1280]{1,0:T(8,128)(2,1)}, bf16[192,1280]{1,0:T(8,128)(2,1)}, u32[]{:S(2)}, u32[]{:S(2)}) collective-permute-start(bf16[192,1280]{1,0:T(8,128)(2,1)} %get-tuple-element.26), channel_id=1, source_target_pairs={{0,64},{4,68},{8,72},{12,76},{16,80},{20,84},{24,88},{28,92},{32,9... | collective-permute-start | bytes 1474568 | tf_op jit(solution)/shard_map/ppermute | solution.py:1030
  42.3 0.9 collective-permute-start.2
  43.3 26.2 %attend.1 = (bf16[32,48,128]{2,1,0:T(8,128)(2,1)}, bf16[32,48,128]{2,1,0:T(8,128)(2,1)}, bf16[32,192,256]{2,1,0:T(8,128)(2,1)}) custom-call(s32[32]{0:T(128)} %count_ref.1, s32[1]{0:T(128)} %bitcast.quarter_ref.first_ref, bf16[32,48,128]{2,1,0:T(8,128)(2,1)} %get-tuple-element.17.q_hbm, bf16[32,48,128]{2,1,0:T(8,128)(2,1)} %get-tuple-element.18.g_hbm, ...), custom_call_target="tpu_custom_call" | custom-call | flops 7247757312 | bytes 16777216 | tf_op jit(solution)/shard_map/attend/pallas_call | solution.py:243
  69.5 0.0 collective-permute-done.g1_ref
  69.5 0.0 collective-permute-done.1.g2_ref
  69.5 0.0 collective-permute-done.2.g3_ref
  69.5 50.1 %home.1 = (bf16[3,192,1024]{2,1,0:T(8,128)(2,1)}, f32[160,1024]{1,0:T(8,128)}) custom-call(bf16[32,48,128]{2,1,0:T(8,128)(2,1)} %get-tuple-element.21.o_ref, bf16[32,48,128]{2,1,0:T(8,128)(2,1)} %get-tuple-element.22.dq_ref, bf16[4,4,2,192,256]{4,3,2,1,0:T(8,128)(2,1)} %bitcast.6, bf16[192,1280]{1,0:T(8,128)(2,1)} %get-tuple-element.24.g0_ref, ...), custom_call_target="tpu_custom_call" | custom-call | tf_op jit(solution)/shard_map/home/pallas_call | solution.py:905
  119.7 22.9 %scatter.1 = (bf16[3,512,1024]{2,1,0:T(8,128)(2,1)}, f32[160,1024]{1,0:T(8,128)}) custom-call(s32[1]{0:T(128)} %bitcast.quarter_ref.first_ref, s32[1,192]{1,0:T(1,128)} %kept_ref.3, bf16[3,192,1024]{2,1,0:T(8,128)(2,1)} %get-tuple-element.28.packed_ref, f32[160,1024]{1,0:T(8,128)} %get-tuple-element.29.weight_ref), custom_call_target="tpu_custom_call" | custom-call | tf_op jit(solution)/shard_map/scatter/pallas_call | solution.py:979
Async XLA Ops:
  39.6 29.9 %collective-permute-start = (bf16[192,1280]{1,0:T(8,128)(2,1)}, bf16[192,1280]{1,0:T(8,128)(2,1)}, u32[]{:S(2)}, u32[]{:S(2)}) collective-permute-start(bf16[192,1280]{1,0:T(8,128)(2,1)} %get-tuple-element.25), channel_id=1, source_target_pairs={{0,32},{4,36},{8,40},{12,44},{16,48},{20,52},{24,56},{28,60},{32,6... | collective-permute-start | bytes 1474568 | tf_op jit(solution)/shard_map/ppermute | solution.py:1030
  40.1 29.4 %collective-permute-start.1 = (bf16[192,1280]{1,0:T(8,128)(2,1)}, bf16[192,1280]{1,0:T(8,128)(2,1)}, u32[]{:S(2)}, u32[]{:S(2)}) collective-permute-start(bf16[192,1280]{1,0:T(8,128)(2,1)} %get-tuple-element.26), channel_id=1, source_target_pairs={{0,64},{4,68},{8,72},{12,76},{16,80},{20,84},{24,88},{28,92},{32,9... | collective-permute-start | bytes 1474568 | tf_op jit(solution)/shard_map/ppermute | solution.py:1030
  42.3 27.2 %collective-permute-start.2 = (bf16[192,1280]{1,0:T(8,128)(2,1)}, bf16[192,1280]{1,0:T(8,128)(2,1)}, u32[]{:S(2)}, u32[]{:S(2)}) collective-permute-start(bf16[192,1280]{1,0:T(8,128)(2,1)} %get-tuple-element.27), channel_id=1, source_target_pairs={{0,96},{4,100},{8,104},{12,108},{16,112},{20,116},{24,120},{28,124... | collective-permute-start | bytes 1474568 | tf_op jit(solution)/shard_map/ppermute | solution.py:1030

commit v11 on v10

--- a/solution.py
+++ b/solution.py
@@ -987,7 +987,7 @@
             pl.BlockSpec(memory_space=pltpu.SMEM),
             pl.BlockSpec((1, slots), lambda i: (0, 0)),
             pl.BlockSpec((1, slots, width), lambda i: (i, 0, 0)),
-            pl.BlockSpec(memory_space=pl.ANY),
+            pl.BlockSpec(weight_grad.shape, lambda i: (0, 0)),
         ],
         out_specs=(
             pl.BlockSpec((1, tokens, width), lambda i: (i, 0, 0)),

time: 143 us -> 124 us (0.87)
  Pallas kernels: 138 us -> 120 us
    pallas_call x1, Pallas kernels: 22.9 us -> 4.44 us  [scatter(): pl.pallas_call(scatter_kernel, grid=(parts,), out_shape=(jax.ShapeDtypeSt...]
  transfers between devices with their start and end apart: 3 -> 3, of which waited for: 0 -> 0; matrix products, arithmetic and copies ran while one was open for 0% -> 0% of each run, Pallas kernels for 18% -> 21%
where the time goes in v11:
time: 124 us
  Pallas kernels  120 us (97%)
  starting transfers between devices  3.64 us (3%)
    pallas_call x1, Pallas kernels, bring_home(): pl.pallas_call(home_kernel, out_shape=(jax.ShapeDtypeStruct((3, slots, wi...  50.1 us
    pallas_call x1, Pallas kernels, spread(): pl.pallas_call(spread_kernel, out_shape=(block,) * 4 + (small,) * 2 + (la...  39 us
    pallas_call x1, Pallas kernels, attend(): pl.pallas_call(attend_kernel, out_shape=(jax.ShapeDtypeStruct((shards, pa...  26.2 us
    pallas_call x1, Pallas kernels, scatter(): pl.pallas_call(scatter_kernel, grid=(parts,), out_shape=(jax.ShapeDtypeSt...  4.44 us
    ppermute x3, starting transfers between devices, along_z(): lax.ppermute(blocks[k], 'seq', [(i, (i + 8 * k) % seq_count) for i in ran...  3.64 us
  transfers between devices with their start and end apart: 3, of which 0 were waited for; matrix products, arithmetic and copies ran while one was open for 0% of the time, Pallas kernels for 21%

profile of v11, /device:TPU:1, one launch (start us, length us, event | category | flops | bytes accessed | tf_op | source)
XLA Modules:
  0.0 124.1 jit_solution(1602426464636409850)
XLA Ops:
  0.6 39.0 %spread.1 = (bf16[192,1280]{1,0:T(8,128)(2,1)}, bf16[192,1280]{1,0:T(8,128)(2,1)}, bf16[192,1280]{1,0:T(8,128)(2,1)}, bf16[192,1280]{1,0:T(8,128)(2,1)}, bf16[32...) custom-call(bf16[512,1280]{1,0:T(8,128)(2,1)} %all_grad_ref.1, ...), custom_call_target="tpu_custom_call" | custom-call | tf_op jit(solution)/shard_map/spread/pallas_call | solution.py:579
  39.6 0.4 collective-permute-start
  40.1 2.2 %collective-permute-start.1 = (bf16[192,1280]{1,0:T(8,128)(2,1)}, bf16[192,1280]{1,0:T(8,128)(2,1)}, u32[]{:S(2)}, u32[]{:S(2)}) collective-permute-start(bf16[192,1280]{1,0:T(8,128)(2,1)} %get-tuple-element.26), channel_id=1, source_target_pairs={{0,64},{4,68},{8,72},{12,76},{16,80},{20,84},{24,88},{28,92},{32,9... | collective-permute-start | bytes 1474568 | tf_op jit(solution)/shard_map/ppermute | solution.py:1030
  42.3 0.9 collective-permute-start.2
  43.3 26.2 %attend.1 = (bf16[32,48,128]{2,1,0:T(8,128)(2,1)}, bf16[32,48,128]{2,1,0:T(8,128)(2,1)}, bf16[32,192,256]{2,1,0:T(8,128)(2,1)}) custom-call(s32[32]{0:T(128)} %count_ref.1, s32[1]{0:T(128)} %bitcast.quarter_ref.first_ref, bf16[32,48,128]{2,1,0:T(8,128)(2,1)} %get-tuple-element.17.q_hbm, bf16[32,48,128]{2,1,0:T(8,128)(2,1)} %get-tuple-element.18.g_hbm, ...), custom_call_target="tpu_custom_call" | custom-call | flops 7247757312 | bytes 16777216 | tf_op jit(solution)/shard_map/attend/pallas_call | solution.py:243
  69.5 0.0 collective-permute-done.g1_ref
  69.5 0.0 collective-permute-done.1.g2_ref
  69.5 0.0 collective-permute-done.2.g3_ref
  69.5 50.1 %home.1 = (bf16[3,192,1024]{2,1,0:T(8,128)(2,1)}, f32[160,1024]{1,0:T(8,128)}) custom-call(bf16[32,48,128]{2,1,0:T(8,128)(2,1)} %get-tuple-element.21.o_ref, bf16[32,48,128]{2,1,0:T(8,128)(2,1)} %get-tuple-element.22.dq_ref, bf16[4,4,2,192,256]{4,3,2,1,0:T(8,128)(2,1)} %bitcast.6, bf16[192,1280]{1,0:T(8,128)(2,1)} %get-tuple-element.24.g0_ref, ...), custom_call_target="tpu_custom_call" | custom-call | tf_op jit(solution)/shard_map/home/pallas_call | solution.py:905
  119.7 4.4 %scatter.1 = (bf16[3,512,1024]{2,1,0:T(8,128)(2,1)}, f32[160,1024]{1,0:T(8,128)}) custom-call(s32[1]{0:T(128)} %bitcast.quarter_ref.first_ref, s32[1,192]{1,0:T(1,128)} %kept_ref.3, bf16[3,192,1024]{2,1,0:T(8,128)(2,1)} %get-tuple-element.28.packed_ref, f32[160,1024]{1,0:T(8,128)} %get-tuple-element.29.weight_ref), custom_call_target="tpu_custom_call" | custom-call | tf_op jit(solution)/shard_map/scatter/pallas_call | solution.py:979
Async XLA Ops:
  39.6 29.9 %collective-permute-start = (bf16[192,1280]{1,0:T(8,128)(2,1)}, bf16[192,1280]{1,0:T(8,128)(2,1)}, u32[]{:S(2)}, u32[]{:S(2)}) collective-permute-start(bf16[192,1280]{1,0:T(8,128)(2,1)} %get-tuple-element.25), channel_id=1, source_target_pairs={{0,32},{4,36},{8,40},{12,44},{16,48},{20,52},{24,56},{28,60},{32,6... | collective-permute-start | bytes 1474568 | tf_op jit(solution)/shard_map/ppermute | solution.py:1030
  40.1 29.4 %collective-permute-start.1 = (bf16[192,1280]{1,0:T(8,128)(2,1)}, bf16[192,1280]{1,0:T(8,128)(2,1)}, u32[]{:S(2)}, u32[]{:S(2)}) collective-permute-start(bf16[192,1280]{1,0:T(8,128)(2,1)} %get-tuple-element.26), channel_id=1, source_target_pairs={{0,64},{4,68},{8,72},{12,76},{16,80},{20,84},{24,88},{28,92},{32,9... | collective-permute-start | bytes 1474568 | tf_op jit(solution)/shard_map/ppermute | solution.py:1030
  42.3 27.2 %collective-permute-start.2 = (bf16[192,1280]{1,0:T(8,128)(2,1)}, bf16[192,1280]{1,0:T(8,128)(2,1)}, u32[]{:S(2)}, u32[]{:S(2)}) collective-permute-start(bf16[192,1280]{1,0:T(8,128)(2,1)} %get-tuple-element.27), channel_id=1, source_target_pairs={{0,96},{4,100},{8,104},{12,108},{16,112},{20,116},{24,120},{28,124... | collective-permute-start | bytes 1474568 | tf_op jit(solution)/shard_map/ppermute | solution.py:1030
